TPU v7x, 128 devices: a whole 4x4x4 slice. The times are simulated.
128 devices in a mesh: dp: 8 (over x, y_hi), seq: 16 (over y_lo, z, core).
Axes of the slice: x: 4, y: 4 (y_hi: 2, y_lo: 2; y = y_hi * 2 + y_lo), z: 4, core: 2. Of those that a mesh axis runs over, the one named last changes fastest.
Arguments:
- tokens: int32 [8, 262144], P('dp', 'seq'), may hold values from 0 to 3
- dilation: int32 [8], P('dp'), may hold values from 1 to 16, as said below
- w_stem: bfloat16 [512, 768], replicated, may hold values from -0.5 to 0.5
- conv_w: bfloat16 [5, 4, 192, 192], replicated, may hold values from -0.1875 to 0.1875
- w_query: bfloat16 [768, 768], replicated, may hold values from -3.6084392 to 3.6084392
- w_key: bfloat16 [768, 768], replicated, may hold values from -0.14433757 to 0.14433757
- w_value: bfloat16 [768, 768], replicated, may hold values from -0.21875 to 0.21875
- w_out: bfloat16 [768, 768], replicated, may hold values from -0.21875 to 0.21875
- cotangent: bfloat16 [8, 2048, 768], P('dp', 'seq'), may hold values from -0.046875 to 0.046875
Outputs:
- mixed: bfloat16 [8, 2048, 768], P('dp', 'seq')
- grad_conv: float32 [5, 4, 192, 192], replicated
- grad_query: float32 [768, 768], replicated
- grad_key: float32 [768, 768], replicated
- grad_value: float32 [768, 768], replicated
- grad_out: float32 [768, 768], replicated
Inputs may be any that keep to these rules, and one draw needn't show every extreme that they name: Some sequence has dilation 16.
All inputs are finite; a program needn't handle non-finite values.
Results may differ from a plain program's by a relative error of at most 0.04.
The roundings to bfloat16 on the way count: a program that leaves them out, or rounds other values in their place, can miss the bound.
Values may be sent and summed in bfloat16 or wider, within the bound.
No kernel may reach another device: no remote copies, remote signals or barrier semaphores. Data moves between devices by JAX's collectives and lax.ppermute only.
A program may use at most 192 MiB of HBM per device.

v0:
```python
import jax
import jax.numpy as jnp
from jax import lax
from jax.sharding import PartitionSpec as P

H = 16
G = 4
KW = 5
DMAX = 16


def swapped(block, axis, apart):
    count = lax.axis_size(axis)
    route = []
    for low in range(count):
        high = low | 1 << apart
        if high != low and high < count:
            route += [(low, high), (high, low)]
    return lax.ppermute(block, axis, route)


def with_halo(cells, sides, width):
    for axis, dim in sides:
        count = lax.axis_size(axis)
        ends = count - 1
        head = lax.slice_in_dim(cells, 0, width, axis=dim)
        tail = lax.slice_in_dim(cells, cells.shape[dim] - width, cells.shape[dim], axis=dim)
        cells = jnp.concatenate(
            [
                lax.ppermute(tail, axis, [(i, (i + 1) % count) for i in range(ends)]),
                cells,
                lax.ppermute(head, axis, [((i + 1) % count, i) for i in range(ends)]),
            ],
            axis=dim,
        )
    return cells


def one_hot_rows(letters_in, local_rows):
    alphabet = jnp.arange(4, dtype=jnp.int32)
    hot_table = (letters_in[..., None] == alphabet).astype(jnp.bfloat16)
    return hot_table.reshape(letters_in.shape[0], local_rows, -1)


def take_rows(padded, spacings, tap_index, local_rows, margin):

    def pick(sequence_row, spacing):
        return lax.dynamic_slice_in_dim(
            sequence_row, margin + (tap_index - KW // 2) * spacing, local_rows, 0
        )

    return jax.vmap(pick)(padded, spacings)


def probabilities(query, keys):
    score_scale = query.shape[-1] ** (-0.5)
    scores = (
        jnp.einsum("nqhd,nkhd->nhqk", query, keys, preferred_element_type=jnp.float32) * score_scale
    )
    highest = jnp.max(scores, axis=-1, keepdims=True)
    powers = jnp.exp(scores - highest)
    return powers / jnp.sum(powers, axis=-1, keepdims=True)


def attend(query, keys, values):
    rounded = probabilities(query, keys).astype(jnp.bfloat16)
    return jnp.einsum(
        "nhqk,nkhd->nqhd", rounded, values, preferred_element_type=jnp.float32
    ).astype(jnp.bfloat16)


def attend_back(query, keys, values, output, grad_attn, part_rows):
    score_scale = query.shape[-1] ** (-0.5)
    probs_full = probabilities(query, keys)
    rounded = probs_full.astype(jnp.bfloat16)
    grad_p = jnp.einsum("nqhd,nkhd->nhqk", grad_attn, values, preferred_element_type=jnp.float32)
    row_dot = jnp.sum(grad_attn.astype(jnp.float32) * output.astype(jnp.float32), axis=-1)
    row_dot = jnp.transpose(row_dot, (0, 2, 1))[..., None]
    grad_s = (probs_full * (grad_p - row_dot)).astype(jnp.bfloat16)
    grad_query = (
        jnp.einsum("nhqk,nkhd->nqhd", grad_s, keys, preferred_element_type=jnp.float32)
        * score_scale
    ).astype(jnp.bfloat16)
    members, head_count, query_len, key_len = grad_s.shape
    blocks = query_len // part_rows
    head_dim = query.shape[-1]
    grad_s_parts = grad_s.reshape(members, head_count, blocks, part_rows, key_len)
    rounded_parts = rounded.reshape(members, head_count, blocks, part_rows, key_len)
    query_segments = query.reshape(members, blocks, part_rows, head_count, head_dim)
    gradient_pieces_split = grad_attn.reshape(members, blocks, part_rows, head_count, head_dim)
    key_segments = (
        jnp.einsum(
            "nhbqk,nbqhd->nbkhd", grad_s_parts, query_segments, preferred_element_type=jnp.float32
        )
        * score_scale
    )
    value_segments = jnp.einsum(
        "nhbqk,nbqhd->nbkhd",
        rounded_parts,
        gradient_pieces_split,
        preferred_element_type=jnp.float32,
    )
    key_segments = lax.optimization_barrier(key_segments.astype(jnp.bfloat16)).astype(jnp.float32)
    value_segments = lax.optimization_barrier(value_segments.astype(jnp.bfloat16)).astype(
        jnp.float32
    )
    return (grad_query, jnp.sum(key_segments, axis=1), jnp.sum(value_segments, axis=1))


def times_transpose(left, weight):
    return lax.dot_general(
        left, weight, (((2,), (1,)), ((), ())), preferred_element_type=jnp.float32
    )


def contract_rows(left, right):
    return lax.dot_general(
        left, right, (((0, 1), (0, 1)), ((), ())), preferred_element_type=jnp.float32
    )


def body(tokens, dilation, w_stem, conv_w, w_query, w_key, w_value, w_out, cotangent):
    seq_local, local_rows, channels = cotangent.shape
    members = 2 * seq_local
    ranks = lax.axis_size("seq")
    length = local_rows * ranks
    head_dim = channels // H
    group_dim = channels // G
    margin = 2 * DMAX
    mirrored = tokens
    for bit_index in range(ranks.bit_length() - 1):
        mirrored = swapped(mirrored, "seq", bit_index)
    letters_in = jnp.concatenate([tokens, 3 - mirrored[:, ::-1]], 0)
    hot_table = one_hot_rows(letters_in, local_rows)
    embedded = jnp.dot(hot_table, w_stem, preferred_element_type=jnp.float32).astype(jnp.bfloat16)
    kernels = jnp.stack([conv_w, conv_w])
    padded = with_halo(embedded, (("seq", 1),), margin)
    spacings = jnp.concatenate([dilation, dilation], 0)
    shifted = jnp.stack(
        [take_rows(padded, spacings, tap_index, local_rows, margin) for tap_index in range(KW)]
    )
    shifted_grouped = shifted.reshape(KW, 2, seq_local, local_rows, G, group_dim)
    preact = jnp.einsum(
        "kbsrgi,bkgio->bsrgo", shifted_grouped, kernels, preferred_element_type=jnp.float32
    ).reshape(members, local_rows, channels)
    hidden = (embedded.astype(jnp.float32) + jax.nn.gelu(preact)).astype(jnp.bfloat16)
    query = jnp.dot(hidden, w_query, preferred_element_type=jnp.float32).astype(jnp.bfloat16)
    key_rows = jnp.dot(hidden, w_key, preferred_element_type=jnp.float32).astype(jnp.bfloat16)
    value_rows = jnp.dot(hidden, w_value, preferred_element_type=jnp.float32).astype(jnp.bfloat16)
    keys_all, values_all = (
        lax.all_gather(key_rows, "seq", axis=1, tiled=True),
        lax.all_gather(value_rows, "seq", axis=1, tiled=True),
    )
    query_heads = query.reshape(members, local_rows, H, head_dim)
    keys_heads = keys_all.reshape(members, length, H, head_dim)
    values_heads = values_all.reshape(members, length, H, head_dim)
    attn_heads = attend(query_heads, keys_heads, values_heads)
    attn = attn_heads.reshape(members, local_rows, channels)
    branch_out = (
        hidden.astype(jnp.float32) + jnp.dot(attn, w_out, preferred_element_type=jnp.float32)
    ).astype(jnp.bfloat16)
    first_out = branch_out[:seq_local]
    second_out = branch_out[seq_local:]
    reversed_out = second_out[:, ::-1]
    for bit_index in range(ranks.bit_length() - 1):
        reversed_out = swapped(reversed_out, "seq", bit_index)
    mixed = (first_out.astype(jnp.float32) + reversed_out.astype(jnp.float32)).astype(jnp.bfloat16)
    mirrored_grad = cotangent
    for bit_index in range(ranks.bit_length() - 1):
        mirrored_grad = swapped(mirrored_grad, "seq", bit_index)
    grad_branch = jnp.concatenate([cotangent, mirrored_grad[:, ::-1]], 0)
    grad_out_w = contract_rows(attn, grad_branch)
    grad_attn = times_transpose(grad_branch, w_out).astype(jnp.bfloat16)
    grad_attn_heads = grad_attn.reshape(members, local_rows, H, head_dim)
    grad_q_heads, key_terms, value_terms = attend_back(
        query_heads, keys_heads, values_heads, attn_heads, grad_attn_heads, local_rows
    )
    grad_k_sum, grad_v_sum = (
        lax.psum_scatter(
            key_terms.reshape(members, length, channels).astype(jnp.bfloat16),
            "seq",
            scatter_dimension=1,
            tiled=True,
        ).astype(jnp.float32),
        lax.psum_scatter(
            value_terms.reshape(members, length, channels).astype(jnp.bfloat16),
            "seq",
            scatter_dimension=1,
            tiled=True,
        ).astype(jnp.float32),
    )
    grad_q_rows = grad_q_heads.reshape(members, local_rows, channels)
    grad_k_rows = grad_k_sum.astype(jnp.bfloat16)
    grad_v_rows = grad_v_sum.astype(jnp.bfloat16)
    grad_hidden = grad_branch.astype(jnp.float32)
    grad_hidden = grad_hidden + times_transpose(grad_q_rows, w_query)
    grad_hidden = grad_hidden + times_transpose(grad_k_rows, w_key)
    grad_hidden = grad_hidden + times_transpose(grad_v_rows, w_value)
    unused, pull_back = jax.vjp(jax.nn.gelu, preact)
    grad_pre = pull_back(grad_hidden)[0].astype(jnp.bfloat16)
    conv_terms = jnp.einsum(
        "kbsrgi,bsrgo->bkgio",
        shifted_grouped,
        grad_pre.reshape(2, seq_local, local_rows, G, group_dim),
        preferred_element_type=jnp.float32,
    )
    grad_conv_local = conv_terms[0] + conv_terms[1]
    grad_q_w = contract_rows(hidden, grad_q_rows)
    grad_k_w = contract_rows(hidden, grad_k_rows)
    grad_v_w = contract_rows(hidden, grad_v_rows)
    grad_conv, grad_query, grad_key, grad_value, grad_out = lax.psum(
        (grad_conv_local, grad_q_w, grad_k_w, grad_v_w, grad_out_w), ("dp", "seq")
    )
    return (mixed, grad_conv, grad_query, grad_key, grad_value, grad_out)


def solution(mesh):
    in_specs = (P("dp", "seq"), P("dp"), P(), P(), P(), P(), P(), P(), P("dp", "seq", None))
    out_specs = (P("dp", "seq", None), P(), P(), P(), P(), P())
    return jax.shard_map(body, mesh=mesh, in_specs=in_specs, out_specs=out_specs, check_vma=False)
```

profile of v0, /device:TPU:1, one launch (start us, length us, event | category | flops | bytes accessed | tf_op | source)
XLA Modules:
  0.0 598.4 jit_solution(9449762202873269680)
XLA Ops:
  7.2 1.5 collective-permute-start
  9.9 1.7 collective-permute-start.1
  11.6 2.2 collective-permute-done.1
  13.7 2.9 collective-permute-start.2
  17.4 3.9 copy.44
  21.3 1.3 collective-permute-start.3
  22.7 1.7 collective-permute-done.3
  24.4 11.1 %rev.9 = s32[1,16384]{1,0:T(1,128)S(1)} reverse(s32[1,16384]{1,0:T(1,128)S(1)} %collective-permute-done.3), dimensions={1} | reverse | bytes 131072 | tf_op jit(solution)/shard_map/rev | solution.py:133
  35.7 6.6 %eq.20 = s32[2,16384,4]{2,1,0:T(8,128)} broadcast(s32[2,16384]{1,0:T(2,128)S(1)} %pad_add_fusion), dimensions={0,1} | broadcast | bytes 655360 | tf_op jit(solution)/shard_map/eq | solution.py:41
  42.3 15.2 %eq.21 = s32[2,128,512]{2,1,0:T(8,128)S(1)} reshape(s32[2,16384,4]{2,1,0:T(8,128)} %eq.20) | data formatting | bytes 1048576 | tf_op jit(solution)/shard_map/eq | solution.py:41
  57.9 5.5 collective-permute-start.4
  63.4 2.4 collective-permute-start.5
  65.9 3.4 collective-permute-done.5
  70.0 1.6 gather_fusion.4
  72.1 1.6 gather_fusion.3
  74.2 2.3 gather_fusion.1
  76.5 1.3 copy.48
  77.8 2.3 gather_fusion
  80.1 2.3 gather_fusion.2
  82.4 1.3 copy.50
  83.7 1.9 copy.46
  87.3 2.3 fusion.10
  89.6 2.3 copy.59
  92.0 1.4 add_convert_fusion
  94.7 2.5 convolution_convert_fusion.3
  97.4 1.4 collective-permute-done.10
  98.8 6.4 %collective-permute-done.11 = bf16[1,128,768]{2,1,0:T(8,128)(2,1)S(1)} collective-permute-done((bf16[1,128,768]{2,1,0:T(8,128)(2,1)S(1)}, bf16[1,128,768]{2,1,0:T(8,128)(2,1)S(1)}, u32[]{:S(2)}, u32[]{:S(2)}) %collective-permute-start.11) | collective-permute-done | bytes 196640 | tf_op jit(solution)/shard_map/ppermute | solution.py:19
  105.2 5.0 collective-permute-start.12
  110.2 8.9 %collective-permute-done.12 = bf16[1,128,768]{2,1,0:T(8,128)(2,1)S(1)} collective-permute-done((bf16[1,128,768]{2,1,0:T(8,128)(2,1)S(1)}, bf16[1,128,768]{2,1,0:T(8,128)(2,1)S(1)}, u32[]{:S(2)}, u32[]{:S(2)}) %collective-permute-start.12) | collective-permute-done | bytes 196640 | tf_op jit(solution)/shard_map/ppermute | solution.py:19
  120.0 9.3 %collective-permute-done.13 = bf16[1,128,768]{2,1,0:T(8,128)(2,1)S(1)} collective-permute-done((bf16[1,128,768]{2,1,0:T(8,128)(2,1)S(1)}, bf16[1,128,768]{2,1,0:T(8,128)(2,1)S(1)}, u32[]{:S(2)}, u32[]{:S(2)}) %collective-permute-start.13) | collective-permute-done | bytes 196640 | tf_op jit(solution)/shard_map/ppermute | solution.py:19
  129.6 1.9 convolution_convert_fusion
  131.7 15.5 %all-gather.5.cloned.1.call-done = bf16[2,2048,768]{2,1,0:T(8,128)(2,1)} async-done(((bf16[2,128,768]{2,1,0:T(8,128)(2,1)}), bf16[2,2048,768]{2,1,0:T(8,128)(2,1)}) %all-gather.5.cloned.1.call-update) | async-done | bytes 6291472 | tf_op jit(solution)/shard_map/all_gather | solution.py:151
  147.2 8.7 %copy.62 = bf16[2,2048,768]{1,2,0:T(8,128)(2,1)} copy(bf16[2,2048,768]{2,1,0:T(8,128)(2,1)} %all-gather.5.cloned.1.call-done) | data formatting | bytes 12582912 | tf_op jit(solution)/shard_map/all_gather | solution.py:151
  155.9 18.2 %fusion.49 = (f32[2,16,128]{2,1,0:T(8,128)S(1)}, f32[2,16,128,2048]{3,2,1,0:T(8,128)}) fusion(bf16[2,128,16,48]{1,3,2,0:T(8,128)(2,1)S(1)} %bitcast.135, bf16[2,2048,16,48]{1,3,2,0:T(8,128)(2,1)} %bitcast.122), kind=kOutput, calls=%fused_computation.94 | convolution fusion | flops 830474240 | bytes 40255488 | tf_op jit(solution)/shard_map/sub | solution.py:61
  174.1 18.9 %fusion.5 = bf16[2,16,128,2048]{3,2,1,0:T(8,128)(2,1)} fusion(f32[2,16,128,2048]{3,2,1,0:T(8,128)} %get-tuple-element.26, f32[2,16,128]{2,1,0:T(8,128)S(1)} %get-tuple-element.25), kind=kLoop, calls=%fused_computation.12 | loop fusion | flops 16777216 | bytes 50348032 | tf_op jit(solution)/shard_map/convert_element_type | solution.py:66
  193.0 8.7 %copy.60 = bf16[2,2048,768]{1,2,0:T(8,128)(2,1)} copy(bf16[2,2048,768]{2,1,0:T(8,128)(2,1)} %all-gather.3.cloned.1.call-done) | data formatting | bytes 12582912 | tf_op jit(solution)/shard_map/all_gather | solution.py:152
  201.7 10.9 %multiply_reduce_fusion.1 = (f32[2,128,16]{1,2,0:T(8,128)S(1)}, bf16[2,16,48,128]{3,2,1,0:T(8,128)(2,1)S(1)}) fusion(bf16[2,128,16,48]{1,3,2,0:T(8,128)(2,1)S(1)} %bitcast.128, bf16[2,2048,16,48]{1,3,2,0:T(8,128)(2,1)} %bitcast.124, bf16[2,16,128,2048]{3,2,1,0:T(8,128)(2,1)} %fusion.5), kind=kOutput, calls=%fused_computation.61 | convolution fusion | flops 806285312 | bytes 23871488 | tf_op jit(solution)/shard_map/nhqk,nkhd->nqhd/dot_general | solution.py:67
  212.6 17.2 %multiply_convert_fusion = bf16[2,16,128,2048]{3,2,1,0:T(8,128)(2,1)} fusion(f32[2,16,128]{2,1,0:T(8,128)S(1)} %bitcast.145, f32[2,16,128,2048]{3,2,1,0:T(8,128)} %get-tuple-element.26, f32[2,16,128]{2,1,0:T(8,128)S(1)} %get-tuple-element.25, bf16[2,128,16,48]{1,3,2,0:T(8,128)(2,1)S(1)} %bitcast.129, bf16[2,2048,16,48]{1,3,2,0:T(8,128)(2,1)S(1)} %bitcast.125), kind=kOutput, calls=%fused_computation.6 | convolution fusion | flops 838860800 | bytes 57049088 | tf_op jit(solution)/shard_map/nqhd,nkhd->nhqk/dot_general | solution.py:76
  229.9 10.9 %fusion.6 = bf16[2,1,2048,16,48]{2,4,3,0,1:T(8,128)(2,1)} fusion(bf16[2,128,16,48]{1,3,2,0:T(8,128)(2,1)S(1)} %bitcast.136, bf16[2,16,128,2048]{3,2,1,0:T(8,128)(2,1)} %multiply_convert_fusion), kind=kOutput, calls=%fused_computation.14 | convolution fusion | flops 811597824 | bytes 23461888 | tf_op jit(solution)/shard_map/nhbqk,nbqhd->nbkhd/dot_general | solution.py:92
  240.7 8.6 %copy.66 = bf16[2,2048,768]{2,1,0:T(8,128)(2,1)} copy(bf16[2,2048,768]{1,2,0:T(8,128)(2,1)} %bitcast.127) | data formatting | bytes 12582912 | tf_op jit(solution)/shard_map/convert_element_type | solution.py:180
  249.5 10.7 %convert_bitcast_fusion = bf16[2,1,2048,16,48]{2,4,3,0,1:T(8,128)(2,1)} fusion(bf16[2,128,16,48]{1,3,2,0:T(8,128)(2,1)S(1)} %bitcast.130, bf16[2,16,128,2048]{3,2,1,0:T(8,128)(2,1)} %fusion.5), kind=kOutput, calls=%fused_computation.15 | convolution fusion | flops 808452096 | bytes 23461888 | tf_op jit(solution)/shard_map/nhbqk,nbqhd->nbkhd/dot_general | solution.py:97
  260.2 8.7 %copy.67 = bf16[2,2048,768]{2,1,0:T(8,128)(2,1)} copy(bf16[2,2048,768]{1,2,0:T(8,128)(2,1)} %bitcast.126) | data formatting | bytes 12582912 | tf_op jit(solution)/shard_map/convert_element_type | solution.py:186
  269.0 1.9 convolution_bitcast_fusion.1
  270.9 11.2 %fusion.17 = bf16[2,16,48,128]{3,2,1,0:T(8,128)(2,1)S(1)} fusion(bf16[2,2048,16,48]{1,3,2,0:T(8,128)(2,1)} %bitcast.123, bf16[2,16,128,2048]{3,2,1,0:T(8,128)(2,1)} %multiply_convert_fusion), kind=kOutput, calls=%fused_computation.39 | convolution fusion | flops 805699584 | bytes 23461888 | tf_op jit(solution)/shard_map/nhqk,nkhd->nqhd/dot_general | solution.py:81
  282.1 1.9 convolution_bitcast_fusion.4
  284.0 1.4 fusion.23
  285.4 31.8 %reduce-scatter.3.cloned.1.call-done = bf16[2,128,768]{2,1,0:T(8,128)(2,1)} async-done(((bf16[2,2048,768]{2,1,0:T(8,128)(2,1)}), bf16[2,128,768]{2,1,0:T(8,128)(2,1)}) %reduce-scatter.3.cloned.1.call-update) | async-done | bytes 393232 | tf_op jit(solution)/shard_map/reduce_scatter | solution.py:179
  317.3 2.4 fusion.20
  319.6 69.1 %reduce-scatter.5.cloned.1.call-done = bf16[2,128,768]{2,1,0:T(8,128)(2,1)} async-done(((bf16[2,2048,768]{2,1,0:T(8,128)(2,1)}), bf16[2,128,768]{2,1,0:T(8,128)(2,1)}) %reduce-scatter.5.cloned.1.call-update) | async-done | bytes 393232 | tf_op jit(solution)/shard_map/reduce_scatter | solution.py:185
  388.7 3.0 fusion.34
  392.0 2.8 convolution_bitcast_fusion
  394.8 2.5 fusion.9
  397.3 1.9 convolution_bitcast_fusion.2
  399.2 1.9 convolution_bitcast_fusion.3
  403.2 4.8 collective-permute-start.6
  409.0 6.4 %collective-permute-done.7 = bf16[1,128,768]{2,1,0:T(8,128)(2,1)S(1)} collective-permute-done((bf16[1,128,768]{2,1,0:T(8,128)(2,1)S(1)}, bf16[1,128,768]{2,1,0:T(8,128)(2,1)S(1)}, u32[]{:S(2)}, u32[]{:S(2)}) %collective-permute-start.7) | collective-permute-done | bytes 196640 | tf_op jit(solution)/shard_map/ppermute | solution.py:19
  415.5 8.7 %collective-permute-done.8 = bf16[1,128,768]{2,1,0:T(8,128)(2,1)S(1)} collective-permute-done((bf16[1,128,768]{2,1,0:T(8,128)(2,1)S(1)}, bf16[1,128,768]{2,1,0:T(8,128)(2,1)S(1)}, u32[]{:S(2)}, u32[]{:S(2)}) %collective-permute-start.8) | collective-permute-done | bytes 196640 | tf_op jit(solution)/shard_map/ppermute | solution.py:19
  424.2 6.0 %collective-permute-done.9 = bf16[1,128,768]{2,1,0:T(8,128)(2,1)S(1)} collective-permute-done((bf16[1,128,768]{2,1,0:T(8,128)(2,1)S(1)}, bf16[1,128,768]{2,1,0:T(8,128)(2,1)S(1)}, u32[]{:S(2)}, u32[]{:S(2)}) %collective-permute-start.9) | collective-permute-done | bytes 196640 | tf_op jit(solution)/shard_map/ppermute | solution.py:19
  430.9 148.4 %all-reduce.7.cloned.1.call-done = (f32[5,4,192,192]{2,3,0,1:T(8,128)}, f32[768,768]{1,0:T(8,128)}, f32[768,768]{1,0:T(8,128)}, f32[768,768]{1,0:T(8,128)}, f32[768,768]{1,0:T(8,128)}) async-done(((f32[5,4,192,192]{2,3,0,1:T(8,128)}, f32[768,768]{1,0:T(8,128)}, f32[768,768]{1,0:T(8,128)}, f32[768,768]{1,0:T(8,128)}, f32[768,768]{1,0:T(8,128)}), (f32[5,4,192,192]{2,3,0,1:T(8,128)}, f32[768,768]{1,0:T(8,128)}, ...) | async-done | bytes 12386320 | tf_op jit(solution)/shard_map/psum | solution.py:211
  579.3 5.4 copy.74
  584.7 1.4 copy.93
  587.2 1.4 copy.94
  588.6 1.4 copy.95
  590.2 1.4 copy.96
  (84 shorter events, 13.6 us)
Async XLA Ops:
  7.2 112.1 %copy-start = (bf16[768,768]{1,0:T(8,128)(2,1)S(1)}, bf16[768,768]{1,0:T(8,128)(2,1)}, u32[]{:S(2)}) copy-start(bf16[768,768]{1,0:T(8,128)(2,1)} %param.13) | copy-start | bytes 3538948
  7.2 28.4 %copy-start.16 = (s32[1,16384]{1,0:T(1,128)S(1)}, s32[1,16384]{1,0:T(1,128)}, u32[]{:S(2)}) copy-start(s32[1,16384]{1,0:T(1,128)} %param.9) | copy-start | bytes 196612
  7.2 140.0 %all-gather.5.cloned.1.call-start = ((), (), s32[]{:S(2)}) async-start(), calls=%async_computation.3 | async-start | bytes 6684672 | tf_op jit(solution)/shard_map/all_gather | solution.py:151
  7.2 2.6 collective-permute-start
  9.9 3.9 collective-permute-start.1
  13.7 7.6 %collective-permute-start.2 = (s32[1,16384]{1,0:T(1,128)S(1)}, s32[1,16384]{1,0:T(1,128)S(1)}, u32[]{:S(2)}, u32[]{:S(2)}) collective-permute-start(s32[1,16384]{1,0:T(1,128)S(1)} %collective-permute-done.1), channel_id=1, source_target_pairs={{0,4},{4,0},{1,5},{5,1},{2,6},{6,2},{3,7},{7,3},{8,12},{12,8},{9,1... | collective-permute-start | bytes 196616 | tf_op jit(solution)/shard_map/ppermute | solution.py:19
  21.3 3.1 collective-permute-start.3
  42.3 15.2 %copy-start.13 = (bf16[512,768]{1,0:T(8,128)(2,1)S(1)}, bf16[512,768]{1,0:T(8,128)(2,1)}, u32[]{:S(2)}) copy-start(bf16[512,768]{1,0:T(8,128)(2,1)} %param.11) | copy-start | bytes 2359300
  57.9 8.0 %collective-permute-start.4 = (bf16[2,32,768]{2,1,0:T(8,128)(2,1)S(1)}, bf16[2,32,768]{2,1,0:T(8,128)(2,1)S(1)}, u32[]{:S(2)}, u32[]{:S(2)}) collective-permute-start(bf16[2,32,768]{2,1,0:T(8,128)(2,1)S(1)} %get-tuple-element.23), channel_id=1, source_target_pairs={{0,1},{1,2},{2,3},{3,4},{4,5},{5,6},{6,7},{7,8},{8,9},{9,10},{10,1... | collective-permute-start | bytes 294920 | tf_op jit(solution)/shard_map/ppermute | solution.py:30
  63.4 5.9 collective-permute-start.5
  74.2 5.9 copy-start.17
  85.7 1.7 copy-start.9
  87.1 2.5 copy-start.4
  87.3 6.1 %copy-start.2 = (bf16[768,768]{1,0:T(8,128)(2,1)S(1)}, bf16[768,768]{1,0:T(8,128)(2,1)}, u32[]{:S(2)}) copy-start(bf16[768,768]{1,0:T(8,128)(2,1)} %param.14) | copy-start | bytes 3538948
  89.6 7.6 %copy-start.15 = (bf16[1,128,768]{2,1,0:T(8,128)(2,1)S(1)}, bf16[1,128,768]{2,1,0:T(8,128)(2,1)}, u32[]{:S(2)}) copy-start(bf16[1,128,768]{2,1,0:T(8,128)(2,1)} %param.17) | copy-start | bytes 589828
  94.7 98.4 %all-gather.3.cloned.1.call-start = ((), (), s32[]{:S(2)}) async-start(), calls=%async_computation.2 | async-start | bytes 6684672 | tf_op jit(solution)/shard_map/all_gather | solution.py:152
  97.2 220.0 %reduce-scatter.3.cloned.1.call-start = ((), (), s32[]{:S(2)}) async-start(), calls=%async_computation.4 | async-start | bytes 6684672 | tf_op jit(solution)/shard_map/reduce_scatter | solution.py:179
  97.3 1.5 collective-permute-start.10
  98.8 6.4 %collective-permute-start.11 = (bf16[1,128,768]{2,1,0:T(8,128)(2,1)S(1)}, bf16[1,128,768]{2,1,0:T(8,128)(2,1)S(1)}, u32[]{:S(2)}, u32[]{:S(2)}) collective-permute-start(bf16[1,128,768]{2,1,0:T(8,128)(2,1)S(1)} %collective-permute-done.10), channel_id=1, source_target_pairs={{0,2},{2,0},{1,3},{3,1},{4,6},{6,4},{5,7},{7,5},{8,10},{10,8},{9,1... | collective-permute-start | bytes 589832 | tf_op jit(solution)/shard_map/ppermute | solution.py:19
  105.2 13.9 %collective-permute-start.12 = (bf16[1,128,768]{2,1,0:T(8,128)(2,1)S(1)}, bf16[1,128,768]{2,1,0:T(8,128)(2,1)S(1)}, u32[]{:S(2)}, u32[]{:S(2)}) collective-permute-start(bf16[1,128,768]{2,1,0:T(8,128)(2,1)S(1)} %collective-permute-done.11), channel_id=1, source_target_pairs={{0,4},{4,0},{1,5},{5,1},{2,6},{6,2},{3,7},{7,3},{8,12},{12,8},{9,1... | collective-permute-start | bytes 589832 | tf_op jit(solution)/shard_map/ppermute | solution.py:19
  119.1 10.2 %collective-permute-start.13 = (bf16[1,128,768]{2,1,0:T(8,128)(2,1)S(1)}, bf16[1,128,768]{2,1,0:T(8,128)(2,1)S(1)}, u32[]{:S(2)}, u32[]{:S(2)}) collective-permute-start(bf16[1,128,768]{2,1,0:T(8,128)(2,1)S(1)} %collective-permute-done.12), channel_id=1, source_target_pairs={{0,8},{8,0},{1,9},{9,1},{2,10},{10,2},{3,11},{11,3},{4,12},{12,4},... | collective-permute-start | bytes 589832 | tf_op jit(solution)/shard_map/ppermute | solution.py:19
  129.5 139.4 %copy-start.12 = (bf16[1,128,768]{2,1,0:T(8,128)(2,1)}, bf16[1,128,768]{2,1,0:T(8,128)(2,1)S(1)}, u32[]{:S(2)}) copy-start(bf16[1,128,768]{2,1,0:T(8,128)(2,1)S(1)} %rev.11) | copy-start | bytes 589828
  201.7 10.9 %copy-start.1 = (bf16[2,2048,768]{1,2,0:T(8,128)(2,1)S(1)}, bf16[2,2048,768]{1,2,0:T(8,128)(2,1)}, u32[]{:S(2)}) copy-start(bf16[2,2048,768]{1,2,0:T(8,128)(2,1)} %copy.60) | copy-start | bytes 18874372
  249.4 139.3 %reduce-scatter.5.cloned.1.call-start = ((), (), s32[]{:S(2)}) async-start(), calls=%async_computation.5 | async-start | bytes 6684672 | tf_op jit(solution)/shard_map/reduce_scatter | solution.py:185
  268.9 310.4 %all-reduce.7.cloned.1.call-start = ((), (), s32[]{:S(2)}) async-start(), calls=%async_computation.6 | async-start | bytes 26738688 | tf_op jit(solution)/shard_map/psum | solution.py:211
  282.1 35.2 %copy-start.3 = (bf16[768,768]{1,0:T(8,128)(2,1)S(1)}, bf16[768,768]{1,0:T(8,128)(2,1)}, u32[]{:S(2)}) copy-start(bf16[768,768]{1,0:T(8,128)(2,1)} %param.14) | copy-start | bytes 3538948
  394.7 2.5 copy-start.14
  394.7 4.4 copy-start.10
  401.1 1.3 copy-start.11
  403.2 5.9 collective-permute-start.6
  409.0 6.4 %collective-permute-start.7 = (bf16[1,128,768]{2,1,0:T(8,128)(2,1)S(1)}, bf16[1,128,768]{2,1,0:T(8,128)(2,1)S(1)}, u32[]{:S(2)}, u32[]{:S(2)}) collective-permute-start(bf16[1,128,768]{2,1,0:T(8,128)(2,1)S(1)} %collective-permute-done.6), channel_id=1, source_target_pairs={{0,2},{2,0},{1,3},{3,1},{4,6},{6,4},{5,7},{7,5},{8,10},{10,8},{9,1... | collective-permute-start | bytes 589832 | tf_op jit(solution)/shard_map/ppermute | solution.py:19
  415.5 8.7 %collective-permute-start.8 = (bf16[1,128,768]{2,1,0:T(8,128)(2,1)S(1)}, bf16[1,128,768]{2,1,0:T(8,128)(2,1)S(1)}, u32[]{:S(2)}, u32[]{:S(2)}) collective-permute-start(bf16[1,128,768]{2,1,0:T(8,128)(2,1)S(1)} %collective-permute-done.7), channel_id=1, source_target_pairs={{0,4},{4,0},{1,5},{5,1},{2,6},{6,2},{3,7},{7,3},{8,12},{12,8},{9,1... | collective-permute-start | bytes 589832 | tf_op jit(solution)/shard_map/ppermute | solution.py:19
  424.2 6.0 %collective-permute-start.9 = (bf16[1,128,768]{2,1,0:T(8,128)(2,1)S(1)}, bf16[1,128,768]{2,1,0:T(8,128)(2,1)S(1)}, u32[]{:S(2)}, u32[]{:S(2)}) collective-permute-start(bf16[1,128,768]{2,1,0:T(8,128)(2,1)S(1)} %collective-permute-done.8), channel_id=1, source_target_pairs={{0,8},{8,0},{1,9},{9,1},{2,10},{10,2},{3,11},{11,3},{4,12},{12,4},... | collective-permute-start | bytes 589832 | tf_op jit(solution)/shard_map/ppermute | solution.py:19
  579.3 5.4 copy-start.8
  584.7 2.5 copy-start.7
  584.7 3.9 copy-start.6
  587.2 3.0 copy-start.5
Sparse Core Ops, SparseCore 0:
  94.8 52.4 all-gather.4
  149.5 43.4 all-gather.2
  249.5 67.6 reduce-scatter.2
  319.5 69.1 reduce-scatter.4
  401.3 178.0 all-reduce.6
where the time goes:
time: 604 us; the launch traced here: 598 us
  waiting for transfers between devices  322 us (53%)
  local copies, waits for them, and re-layouts  107 us (18%)
  matrix products  106 us (18%)
  starting transfers between devices  25.6 us (4%)
  other arithmetic  23.9 us (4%)
  between operations  15.1 us (2%)
    psum x1, waiting for transfers between devices, body(): lax.psum((grad_conv_local, grad_q_w, grad_k_w, grad_v_w, grad_out_w), ('d...  148 us
    reduce_scatter x1, waiting for transfers between devices, body(): lax.psum_scatter(value_terms.reshape(members, length, channels).astype(jn...  69.1 us
    ppermute x12, waiting for transfers between devices, swapped(): return lax.ppermute(block, axis, route)  53.2 us
    reduce_scatter x1, waiting for transfers between devices, body(): lax.psum_scatter(key_terms.reshape(members, length, channels).astype(jnp....  31.8 us
    eq x4, local copies, waits for them, and re-layouts, one_hot_rows(): hot_table = (letters_in[..., None] == alphabet).astype(jnp.bfloat16)  21.9 us
    unnamed x46, local copies, waits for them, and re-layouts  19 us
    convert_element_type x1, other arithmetic, attend(): rounded = probabilities(query, keys).astype(jnp.bfloat16)  18.9 us
    sub x1, matrix products, probabilities(): powers = jnp.exp(scores - highest)  18.2 us
  transfers between devices with their start and end apart: 19, of which 16 were waited for; matrix products, arithmetic and copies ran while one was open for 16% of the time, Pallas kernels for 0%

commit v1 on v0

v1 whole, which is shorter than its diff:
```python
import functools
import math

import jax
import jax.numpy as jnp
from jax import lax
from jax.experimental import pallas as pl
from jax.experimental.pallas import tpu as pltpu
from jax.sharding import PartitionSpec as P

H = 16
G = 4
KW = 5
DMAX = 16
MARGIN = 2 * DMAX
C = 768
CG = C // G
HD = C // H
BP = 128
BINS = 2048
ROWS = 256
BLOCKS = BINS // ROWS
PLANES = C // 128
PIECE = BP + HD
SCALE = HD ** (-0.5)
BF = jnp.bfloat16
F32 = jnp.float32
VMEM_LIMIT = 56 * 1024 * 1024
GELU_A = math.sqrt(2.0 / math.pi)
GELU_B = 0.044715
WINDOWS = (0, 1, 3, 4)


def mm(left, right):
    return jnp.dot(left, right, preferred_element_type=F32)


def mm_nt(left, right):
    return lax.dot_general(left, right, (((1,), (1,)), ((), ())), preferred_element_type=F32)


def vmem():
    return pl.BlockSpec(memory_space=pltpu.VMEM)


def smem():
    return pl.BlockSpec(memory_space=pltpu.SMEM)


def params(**extra):
    return pltpu.CompilerParams(vmem_limit_bytes=VMEM_LIMIT, **extra)


def front_kernel(info, pieces, w_stem, conv, hidden, pre_own, emb_own, stem, emb):
    step = info[0]
    core = info[1]
    chip = info[2]
    row = lax.broadcasted_iota(jnp.int32, (4 * BP, 4 * BP), 0)
    col = lax.broadcasted_iota(jnp.int32, (4 * BP, 4 * BP), 1)
    source = 4 * (row & (BP - 1)) + (row >> 7)
    source = jnp.where(core == 1, 4 * BP - 1 - source, source)
    stem[...] = mm((col == source).astype(BF), w_stem[...]).astype(BF)
    edge = jnp.zeros((PLANES, MARGIN, 128), F32)
    emb[:, 0:MARGIN, :] = edge
    emb[:, MARGIN + BINS : MARGIN + BINS + MARGIN, :] = edge

    def embed(block, carry):
        letters = pieces[pl.ds(2 * block, 2), 0:BP, :].astype(F32).reshape(ROWS, BP)
        hot = jnp.concatenate([(letters == float(c)).astype(BF) for c in range(4)], axis=1)
        rows = mm(hot, stem[...]).astype(BF).astype(F32)
        start = pl.multiple_of(MARGIN + block * ROWS, 8)
        for plane in range(PLANES):
            emb[plane, pl.ds(start, ROWS), :] = rows[:, plane * 128 : (plane + 1) * 128]
        return carry

    lax.fori_loop(0, BLOCKS, embed, 0)

    def convolve(block, carry):
        base = MARGIN + block * ROWS
        planes = [
            [
                emb[plane, pl.ds(base + (tap - KW // 2) * step, ROWS), :].astype(BF)
                for tap in range(KW)
            ]
            for plane in range(PLANES)
        ]
        sums = []
        for group in range(G):
            at = WINDOWS[group]
            left = jnp.concatenate(
                [planes[at + half][tap] for tap in range(KW) for half in range(2)], axis=1
            )
            sums.append(mm(left, conv[group]))
        for pair in range(2):
            even, odd = sums[2 * pair], sums[2 * pair + 1]
            thirds = (even[:, :128], even[:, 128:] + odd[:, :128], odd[:, 128:])
            for third in range(3):
                plane = 3 * pair + third
                x = thirds[third]
                lanes = slice(plane * 128, (plane + 1) * 128)

                @pl.when(block == chip)
                def _(x=x, lanes=lanes):
                    pre_own[:, lanes] = x

                th = jnp.tanh(GELU_A * (x + GELU_B * (x * x * x)))
                act = 0.5 * x * (1.0 + th)
                own = emb[plane, pl.ds(pl.multiple_of(base, 8), ROWS), :]
                hidden[pl.ds(pl.multiple_of(block * ROWS, ROWS), ROWS), lanes] = (own + act).astype(BF)
        return carry

    lax.fori_loop(0, BLOCKS, convolve, 0)
    emb_own[...] = emb[:, pl.ds(pl.multiple_of(chip * ROWS, ROWS), ROWS + 2 * MARGIN), :]


def front(info, pieces, w_stem, conv):
    return pl.pallas_call(
        front_kernel,
        out_shape=(
            jax.ShapeDtypeStruct((BINS, C), BF),
            jax.ShapeDtypeStruct((ROWS, C), F32),
            jax.ShapeDtypeStruct((PLANES, ROWS + 2 * MARGIN, 128), F32),
        ),
        in_specs=[smem(), vmem(), vmem(), vmem()],
        out_specs=(vmem(), vmem(), vmem()),
        scratch_shapes=[
            pltpu.VMEM((4 * BP, C), BF),
            pltpu.VMEM((PLANES, BINS + 2 * MARGIN, 128), F32),
        ],
        compiler_params=params(),
        cost_estimate=pl.CostEstimate(flops=2 * 10**10, bytes_accessed=10**7, transcendentals=0),
        name="front",
    )(info, pieces, w_stem, conv)


def heads_kernel(
    hidden, cot, pieces, w_qkv, out, wgrad,
    q_pad, k_nat, v_nat, q_t, k_t, v_t, ga_t, x_t, scores, rounded, kv_sum,
):
    def project(block, carry):
        rows = pl.ds(pl.multiple_of(block * ROWS, ROWS), ROWS)
        y = mm(hidden[rows, :], w_qkv[...]).astype(BF)
        q_pad[rows, :] = y[:, 0:128]
        k_nat[rows, :] = y[:, 128 : 128 + HD]
        v_nat[rows, :] = y[:, 256 : 256 + HD]
        turned = y.astype(F32).T
        q_t[:, rows] = turned[0:HD].astype(BF)
        k_t[:, rows] = turned[128 : 128 + HD].astype(BF)
        v_t[:, rows] = turned[256 : 256 + HD].astype(BF)
        ga_t[:, rows] = jnp.concatenate([pieces[2 * block, BP:, :], pieces[2 * block + 1, BP:, :]], axis=1)
        return carry

    lax.fori_loop(0, BLOCKS, project, 0)
    kv_sum[...] = jnp.zeros_like(kv_sum)

    def attend(block, carry):
        lanes = pl.ds(pl.multiple_of(block * ROWS, ROWS), ROWS)
        qt = q_t[:, lanes]
        gat = ga_t[:, lanes]
        top = None
        for part in range(BLOCKS):
            at = slice(part * ROWS, (part + 1) * ROWS)
            s = mm(k_nat[at, :], qt)
            scores[at, :] = s
            most = jnp.max(s.reshape(ROWS // 8, 8, ROWS), axis=0)
            top = most if top is None else jnp.maximum(top, most)
        top = jnp.max(top, axis=0, keepdims=True)
        total = None
        for part in range(BLOCKS):
            at = slice(part * ROWS, (part + 1) * ROWS)
            e = jnp.exp2((scores[at, :] - top) * (SCALE * math.log2(math.e)))
            scores[at, :] = e
            some = jnp.sum(e.reshape(ROWS // 8, 8, ROWS), axis=0)
            total = some if total is None else total + some
        inverse = 1.0 / jnp.sum(total, axis=0, keepdims=True)
        attn = None
        for part in range(BLOCKS):
            at = slice(part * ROWS, (part + 1) * ROWS)
            pb = (scores[at, :] * inverse).astype(BF)
            rounded[at, :] = pb
            term = mm(v_t[:, at], pb)
            attn = term if attn is None else attn + term
        attn = attn.astype(BF)
        x_t[0:HD, lanes] = attn
        row_dot = jnp.sum(gat.astype(F32) * attn.astype(F32), axis=0, keepdims=True)
        ga_pad = jnp.concatenate(
            [jnp.zeros((HD, ROWS), F32), gat.astype(F32), jnp.zeros((128 - 2 * HD, ROWS), F32)], axis=0
        ).T.astype(BF)
        right = jnp.concatenate([q_pad[lanes, :], ga_pad], axis=0)
        gq = None
        for part in range(BLOCKS):
            at = slice(part * ROWS, (part + 1) * ROWS)
            gp = mm(v_nat[at, :], gat)
            gs = ((scores[at, :] * inverse) * (gp - row_dot)).astype(BF)
            term = mm(k_t[:, at], gs)
            gq = term if gq is None else gq + term
            kv_sum[at, :] += mm(jnp.concatenate([gs, rounded[at, :]], axis=1), right)
        x_t[HD : 2 * HD, lanes] = (gq * SCALE).astype(BF)
        return carry

    lax.fori_loop(0, BLOCKS, attend, 0)

    wgrad[...] = jnp.zeros_like(wgrad)

    def finish(block, carry):
        rows = pl.ds(pl.multiple_of(block * ROWS, ROWS), ROWS)
        turned = kv_sum[rows, :].T
        x_t[2 * HD : 3 * HD, rows] = (turned[0:HD] * SCALE).astype(BF)
        x_t[3 * HD : 4 * HD, rows] = turned[HD : 2 * HD].astype(BF)
        piece = x_t[:, rows]
        out[block] = piece
        wgrad[0:HD, :] += mm(piece[0:HD], cot[rows, :])
        wgrad[HD:, :] += mm(piece[HD:], hidden[rows, :])
        return carry

    lax.fori_loop(0, BLOCKS, finish, 0)


def heads(hidden, cot, pieces, w_qkv):
    return pl.pallas_call(
        heads_kernel,
        out_shape=(
            jax.ShapeDtypeStruct((BLOCKS, 4 * HD, ROWS), BF),
            jax.ShapeDtypeStruct((4 * HD, C), F32),
        ),
        in_specs=[vmem()] * 4,
        out_specs=(vmem(), vmem()),
        scratch_shapes=[
            pltpu.VMEM((BINS, 128), BF),
            pltpu.VMEM((BINS, HD), BF),
            pltpu.VMEM((BINS, HD), BF),
            pltpu.VMEM((HD, BINS), BF),
            pltpu.VMEM((HD, BINS), BF),
            pltpu.VMEM((HD, BINS), BF),
            pltpu.VMEM((HD, BINS), BF),
            pltpu.VMEM((4 * HD, BINS), BF),
            pltpu.VMEM((BINS, ROWS), F32),
            pltpu.VMEM((BINS, ROWS), BF),
            pltpu.VMEM((BINS, 128), F32),
        ],
        compiler_params=params(),
        cost_estimate=pl.CostEstimate(flops=4 * 10**10, bytes_accessed=10**7, transcendentals=0),
        name="heads",
    )(hidden, cot, pieces, w_qkv)


def tail_kernel(
    info, got, hidden, cot, pre, emb, w_query, w_key, w_value, w_out, branch_out, conv_grad
):
    step = info[0]

    def rows_of(which):
        part = got[:, which * HD : (which + 1) * HD, :].reshape(C, ROWS)
        return part.astype(F32).T.astype(BF)

    branch_out[...] = (hidden[...].astype(F32) + mm(rows_of(0), w_out[...])).astype(BF)
    grad = cot[...].astype(F32) + mm_nt(rows_of(1), w_query[...])
    grad = grad + mm_nt(rows_of(2), w_key[...])
    grad = grad + mm_nt(rows_of(3), w_value[...])
    x = pre[...]
    square = x * x
    th = jnp.tanh(GELU_A * (x + GELU_B * (square * x)))
    slope = 0.5 * (1.0 + th) + 0.5 * x * (1.0 - th * th) * (GELU_A * (1.0 + 3.0 * GELU_B * square))
    grad_t = (grad * slope).astype(BF).astype(F32).T.astype(BF)
    low = lax.broadcasted_iota(jnp.int32, (CG, 128), 1) < 64
    for tap in range(KW):
        start = MARGIN + (tap - KW // 2) * step
        planes = [emb[plane, pl.ds(start, ROWS), :].astype(BF) for plane in range(PLANES)]
        for pair in range(2):
            terms = []
            for half in range(2):
                group = 2 * pair + half
                at = WINDOWS[group]
                right = jnp.concatenate([planes[at], planes[at + 1]], axis=1)
                terms.append(mm(grad_t[group * CG : (group + 1) * CG], right))
            even, odd = terms
            thirds = (even[:, :128], jnp.where(low, even[:, 128:], odd[:, :128]), odd[:, 128:])
            for third in range(3):
                plane = 3 * pair + third
                conv_grad[tap * CG : (tap + 1) * CG, plane * 128 : (plane + 1) * 128] = thirds[third].astype(BF)
    conv_grad[KW * CG :, :] = jnp.zeros((64, C), BF)


def tail(info, got, hidden, cot, pre, emb, w_query, w_key, w_value, w_out):
    return pl.pallas_call(
        tail_kernel,
        out_shape=(
            jax.ShapeDtypeStruct((ROWS, C), BF),
            jax.ShapeDtypeStruct((KW * CG + 64, C), BF),
        ),
        in_specs=[smem()] + [vmem()] * 9,
        out_specs=(vmem(), vmem()),
        compiler_params=params(),
        cost_estimate=pl.CostEstimate(flops=5 * 10**9, bytes_accessed=10**7, transcendentals=0),
        name="tail",
    )(info, got, hidden, cot, pre, emb, w_query, w_key, w_value, w_out)


def apart(axis, bit):
    return [(i, i ^ bit) for i in range(lax.axis_size(axis))]


def body(tokens, dilation, w_stem, conv_w, w_query, w_key, w_value, w_out, cotangent):
    me = lax.axis_index("seq")
    core = me & 1
    chip = me >> 1
    step = jnp.where(core == 1, -dilation[0], dilation[0])
    info = jnp.stack([step, core, chip]).astype(jnp.int32)
    own_cot = cotangent[0]
    cot = lax.all_gather(own_cot, "seq", axis=0, tiled=True)
    ga_t = lax.dot_general(w_out, own_cot, (((1,), (1,)), ((), ())), preferred_element_type=F32).astype(BF)
    letters = jnp.broadcast_to(tokens.reshape(1, BP, BP).astype(BF), (H, BP, BP))
    pieces = lax.all_to_all(
        jnp.concatenate([letters, ga_t.reshape(H, HD, BP)], axis=1), "seq", 0, 0, tiled=True
    )
    taps = conv_w.transpose(1, 0, 2, 3)
    conv = jnp.stack(
        [
            jnp.pad(taps[group], ((0, 0), (64, 0), (64, 0)) if group % 2 else ((0, 0), (0, 64), (0, 64)))
            for group in range(G)
        ]
    ).reshape(G, KW * 256, 256)
    w_qkv = jnp.concatenate(
        [
            jnp.pad(lax.dynamic_slice_in_dim(w, me * HD, HD, 1), ((0, 0), (0, 128 - HD)))
            for w in (w_query, w_key, w_value)
        ],
        axis=1,
    )
    hidden, pre_own, emb_own = front(info, pieces, w_stem, conv)
    hidden_other = lax.ppermute(hidden, "seq", apart("seq", 1))
    mine, wgrad_mine = heads(hidden, cot, pieces, w_qkv)
    other, wgrad_other = heads(hidden_other, cot, pieces, w_qkv)
    first = jnp.where(core == 0, mine, other)
    second = jnp.where(core == 0, other, mine)
    got = lax.all_to_all(
        jnp.stack([first, second], axis=1).reshape(H, 4 * HD, ROWS), "seq", 0, 0, tiled=True
    )
    hidden_own = lax.dynamic_slice_in_dim(hidden, chip * ROWS, ROWS, 0)
    cot_own = lax.dynamic_slice_in_dim(cot, chip * ROWS, ROWS, 0)
    branch_out, conv_grad = tail(
        info, got, hidden_own, cot_own, pre_own, emb_own, w_query, w_key, w_value, w_out
    )
    keep = lax.dynamic_slice_in_dim(branch_out, core * BP, BP, 0)
    give = lax.dynamic_slice_in_dim(branch_out, (1 - core) * BP, BP, 0)
    taken = lax.ppermute(give, "seq", apart("seq", 1))
    mixed = (keep.astype(F32) + taken.astype(F32)).astype(BF)[None]

    wgrad = (wgrad_mine + wgrad_other).astype(BF)
    for bit in (1, 2, 4):
        wgrad = (wgrad.astype(F32) + lax.ppermute(wgrad, "dp", apart("dp", bit)).astype(F32)).astype(BF)
    wgrads = lax.all_gather(wgrad, "seq", axis=0, tiled=True).reshape(H, 4, HD, C)
    grad_out = wgrads[:, 0].reshape(C, C).astype(F32)
    grad_query, grad_key, grad_value = (
        wgrads[:, which].reshape(C, C).T.astype(F32) for which in (1, 2, 3)
    )

    parts = lax.all_to_all(conv_grad.reshape(H, 64, C), "seq", 0, 0, tiled=True)
    share = jnp.sum(parts.reshape(H, 64, C).astype(F32), axis=0).astype(BF)
    for bit in (1, 2, 4):
        share = (share.astype(F32) + lax.ppermute(share, "dp", apart("dp", bit)).astype(F32)).astype(BF)
    whole = lax.all_to_all(jnp.broadcast_to(share[None], (H, 64, C)), "seq", 0, 0, tiled=True)
    whole = whole.reshape(H * 64, C)[: KW * CG].reshape(KW, CG, G, CG)
    grad_conv = whole.transpose(0, 2, 3, 1).astype(F32)
    return (mixed, grad_conv, grad_query, grad_key, grad_value, grad_out)


def solution(mesh):
    in_specs = (P("dp", "seq"), P("dp"), P(), P(), P(), P(), P(), P(), P("dp", "seq", None))
    out_specs = (P("dp", "seq", None), P(), P(), P(), P(), P())
    return jax.shard_map(body, mesh=mesh, in_specs=in_specs, out_specs=out_specs, check_vma=False)
```

time: 604 us -> 311 us (0.51)
  waiting for transfers between devices: 322 us -> 83.9 us
  matrix products: 106 us -> 1.75 us
  Pallas kernels: 0 us -> 92.6 us
  local copies, waits for them, and re-layouts: 107 us -> 33.6 us
  blocking collectives: 0 us -> 26 us
  starting transfers between devices: 25.6 us -> 41.2 us
  other arithmetic: 23.9 us -> 15.2 us
    psum x1 -> x0, waiting for transfers between devices: 148 us -> none  [body(): lax.psum((grad_conv_local, grad_q_w, grad_k_w, grad_v_w, grad_out_w), ('d...]
    reduce_scatter x2 -> x0, waiting for transfers between devices: 101 us -> none  [the longest x1 69.1 us: body(): lax.psum_scatter(value_terms.reshape(members, length, channels).astype(jn...]
    pallas_call x0 -> x4, Pallas kernels: none -> 92.6 us  [the longest x2 67.5 us: heads(): pl.pallas_call(heads_kernel, out_shape=(jax.ShapeDtypeStruct((BLOCKS, 4 *...]
    dot_general x20 -> x1, matrix products: 87.4 us -> 1.75 us  [body(): lax.dot_general(w_out, own_cot, (((1,), (1,)), ((), ())), preferred_eleme...]
    all_to_all x0 -> x3, waiting for transfers between devices: none -> 55.5 us  [the longest x1 27.8 us: body(): lax.all_to_all(jnp.stack([first, second], axis=1).reshape(H, 4 * HD, ROWS...]
    ppermute x14 -> x8, waiting for transfers between devices: 56.6 us -> 27.7 us  [the longest x3 19.4 us: body(): lax.ppermute(wgrad, 'dp', apart('dp', bit)).astype(F32)]
    all_to_all x0 -> x1, blocking collectives: none -> 26 us  [body(): parts = lax.all_to_all(conv_grad.reshape(H, 64, C), 'seq', 0, 0, tiled=True)]
    all_to_all x0 -> x3, starting transfers between devices: none -> 24.2 us  [the longest x1 8.76 us: body(): lax.all_to_all(jnp.stack([first, second], axis=1).reshape(H, 4 * HD, ROWS...]
  transfers between devices with their start and end apart: 19 -> 13, of which waited for: 16 -> 10; matrix products, arithmetic and copies ran while one was open for 16% -> 10% of each run, Pallas kernels for 0% -> 19%
where the time goes in v1:
time: 311 us; the launch traced here: 309 us
  Pallas kernels  92.6 us (30%)
  waiting for transfers between devices  83.9 us (27%)
  starting transfers between devices  41.2 us (13%)
  local copies, waits for them, and re-layouts  33.6 us (11%)
  blocking collectives  26 us (8%)
  other arithmetic  15.2 us (5%)
  between operations  14.9 us (5%)
    pallas_call x2, Pallas kernels, heads(): pl.pallas_call(heads_kernel, out_shape=(jax.ShapeDtypeStruct((BLOCKS, 4 *...  67.5 us
    all_to_all x1, waiting for transfers between devices, body(): lax.all_to_all(jnp.stack([first, second], axis=1).reshape(H, 4 * HD, ROWS...  27.8 us
    all_to_all x1, blocking collectives, body(): parts = lax.all_to_all(conv_grad.reshape(H, 64, C), 'seq', 0, 0, tiled=True)  26 us
    all_to_all x1, waiting for transfers between devices, body(): lax.all_to_all(jnp.broadcast_to(share[None], (H, 64, C)), 'seq', 0, 0, ti...  19.7 us
    ppermute x3, waiting for transfers between devices, body(): lax.ppermute(wgrad, 'dp', apart('dp', bit)).astype(F32)  19.4 us
    pallas_call x1, Pallas kernels, front(): pl.pallas_call(front_kernel, out_shape=(jax.ShapeDtypeStruct((BINS, C), B...  17.8 us
    unnamed x20, local copies, waits for them, and re-layouts  15.9 us
    all_to_all x1, starting transfers between devices, body(): lax.all_to_all(jnp.stack([first, second], axis=1).reshape(H, 4 * HD, ROWS...  8.76 us
  transfers between devices with their start and end apart: 13, of which 10 were waited for; matrix products, arithmetic and copies ran while one was open for 10% of the time, Pallas kernels for 19%

profile of v1, /device:TPU:1, one launch (start us, length us, event | category | flops | bytes accessed | tf_op | source)
XLA Modules:
  0.0 309.2 jit_solution(18002179004879523090)
XLA Ops:
  7.2 0.7 all-gather.6.cloned.1.call-update
  7.9 1.0 convert_reduce_fusion
  8.9 1.7 convolution_convert_fusion
  10.7 0.1 broadcast_in_dim.6
  10.8 0.9 pad_maximum_fusion.2
  11.7 7.8 %all-to-all-start = ((bf16[16,176,128]{2,1,0:T(8,128)(2,1)}), bf16[16,176,128]{2,1,0:T(8,128)(2,1)S(1)}, u32[]{:S(2)}, u32[]{:S(2)}) async-start(bf16[16,176,128]{2,1,0:T(8,128)(2,1)} %pad_maximum_fusion.2), calls=%async_computation | async-start | bytes 1441792 | tf_op jit(solution)/shard_map/all_to_all | solution.py:313
  20.2 1.1 constant_dynamic-slice_fusion.4
  21.4 0.2 slice_bitcast_fusion.3
  21.6 0.7 pad_add_fusion.info
  22.2 0.2 pad.27
  22.4 0.1 pad.26
  22.5 0.2 pad.25
  22.9 1.3 constant_dynamic-slice_fusion.2
  24.2 1.0 fusion.5.w_qkv
  25.1 1.8 pad_maximum_fusion.conv
  27.0 8.0 %all-to-all-done.pieces = bf16[16,176,128]{2,1,0:T(8,128)(2,1)S(1)} async-done(((bf16[16,176,128]{2,1,0:T(8,128)(2,1)}), bf16[16,176,128]{2,1,0:T(8,128)(2,1)S(1)}, u32[]{:S(2)}, u32[]{:S(2)}) %all-to-all-start) | async-done | bytes 720928 | tf_op jit(solution)/shard_map/all_to_all | solution.py:313
  34.9 0.9 copy-done.4
  35.8 17.8 %front.1 = (bf16[2048,768]{1,0:T(8,128)(2,1)}, f32[256,768]{1,0:T(8,128)}, f32[6,320,128]{2,1,0:T(8,128)}) custom-call(s32[3]{0:T(128)} %pad_add_fusion.info, bf16[16,176,128]{2,1,0:T(8,128)(2,1)} %copy-done.4, bf16[512,768]{1,0:T(8,128)(2,1)} %w_stem.1, bf16[4,1280,256]{2,1,0:T(8,128)(2,1)} %pad_maximum_fusion.conv), custom_call_target="tpu_custom_call" | custom-call | flops 20000000000 | bytes 10000000 | tf_op jit(solution)/shard_map/front/pallas_call | solution.py:117
  53.6 1.4 collective-permute-start
  55.0 33.7 %heads.2 = (bf16[8,192,256]{2,1,0:T(8,128)(2,1)}, f32[192,768]{1,0:T(8,128)}) custom-call(bf16[2048,768]{1,0:T(8,128)(2,1)} %get-tuple-element.15.hidden, bf16[2048,768]{1,0:T(8,128)(2,1)} %bitcast.72, bf16[16,176,128]{2,1,0:T(8,128)(2,1)} %copy-done.4, bf16[768,384]{1,0:T(8,128)(2,1)} %fusion.5.w_qkv), custom_call_target="tpu_custom_call" | custom-call | flops 40000000000 | bytes 10000000 | tf_op jit(solution)/shard_map/heads/pallas_call | solution.py:220
  88.7 1.6 copy-done.7
  90.3 33.7 %heads.3 = (bf16[8,192,256]{2,1,0:T(8,128)(2,1)}, f32[192,768]{1,0:T(8,128)}) custom-call(bf16[2048,768]{1,0:T(8,128)(2,1)} %copy-done.7, bf16[2048,768]{1,0:T(8,128)(2,1)} %bitcast.73, bf16[16,176,128]{2,1,0:T(8,128)(2,1)} %copy-done.4, bf16[768,384]{1,0:T(8,128)(2,1)} %fusion.5.w_qkv), custom_call_target="tpu_custom_call" | custom-call | flops 40000000000 | bytes 10000000 | tf_op jit(solution)/shard_map/heads/pallas_call | solution.py:220
  124.1 1.1 add_convert_fusion.3
  125.2 2.9 collective-permute-start.5
  128.1 7.3 %collective-permute-done.5 = bf16[192,768]{1,0:T(8,128)(2,1)S(1)} collective-permute-done((bf16[192,768]{1,0:T(8,128)(2,1)S(1)}, bf16[192,768]{1,0:T(8,128)(2,1)S(1)}, u32[]{:S(2)}, u32[]{:S(2)}) %collective-permute-start.5) | collective-permute-done | bytes 294944 | tf_op jit(solution)/shard_map/ppermute | solution.py:351
  135.5 1.4 collective-permute-start.6
  136.9 6.6 %collective-permute-done.6 = bf16[192,768]{1,0:T(8,128)(2,1)S(1)} collective-permute-done((bf16[192,768]{1,0:T(8,128)(2,1)S(1)}, bf16[192,768]{1,0:T(8,128)(2,1)S(1)}, u32[]{:S(2)}, u32[]{:S(2)}) %collective-permute-start.6) | collective-permute-done | bytes 294944 | tf_op jit(solution)/shard_map/ppermute | solution.py:351
  143.6 2.9 collective-permute-start.7
  146.5 5.5 %collective-permute-done.7 = bf16[192,768]{1,0:T(8,128)(2,1)S(1)} collective-permute-done((bf16[192,768]{1,0:T(8,128)(2,1)S(1)}, bf16[192,768]{1,0:T(8,128)(2,1)S(1)}, u32[]{:S(2)}, u32[]{:S(2)}) %collective-permute-start.7) | collective-permute-done | bytes 294944 | tf_op jit(solution)/shard_map/ppermute | solution.py:351
  152.0 0.8 add_convert_fusion
  152.8 0.1 select_bitcast_fusion.1
  153.0 0.1 pad_maximum_fusion.1
  153.1 1.3 copy.19
  154.4 8.8 %all-to-all-start.1 = ((bf16[16,192,256]{2,1,0:T(8,128)(2,1)}), bf16[16,192,256]{2,1,0:T(8,128)(2,1)S(1)}, u32[]{:S(2)}, u32[]{:S(2)}) async-start(bf16[16,192,256]{2,1,0:T(8,128)(2,1)} %bitcast.18), calls=%async_computation.1 | async-start | bytes 3145728 | tf_op jit(solution)/shard_map/all_to_all | solution.py:336
  163.1 1.8 constant_dynamic-slice_fusion.1.hidden
  164.9 1.8 dynamic-slice_bitcast_fusion.cot
  166.7 27.8 %all-to-all-done.1.got = bf16[16,192,256]{2,1,0:T(8,128)(2,1)S(1)} async-done(((bf16[16,192,256]{2,1,0:T(8,128)(2,1)}), bf16[16,192,256]{2,1,0:T(8,128)(2,1)S(1)}, u32[]{:S(2)}, u32[]{:S(2)}) %all-to-all-start.1) | async-done | bytes 1572896 | tf_op jit(solution)/shard_map/all_to_all | solution.py:336
  194.5 1.1 copy-done.1
  195.7 7.4 %tail.1 = (bf16[256,768]{1,0:T(8,128)(2,1)}, bf16[1024,768]{1,0:T(8,128)(2,1)}) custom-call(s32[3]{0:T(128)} %pad_add_fusion.info, bf16[16,192,256]{2,1,0:T(8,128)(2,1)} %copy-done.1, bf16[256,768]{1,0:T(8,128)(2,1)} %constant_dynamic-slice_fusion.1.hidden, bf16[256,768]{1,0:T(8,128)(2,1)} %dynamic-slice_bitcast_fusion.cot, ...), custom_call_target="tpu_custom_call" | custom-call | flops 5000000000 | bytes 10000000 | tf_op jit(solution)/shard_map/tail/pallas_call | solution.py:285
  203.1 26.0 %all_to_all.20 = bf16[16,64,768]{2,1,0:T(8,128)(2,1)S(1)} all-to-all(bf16[16,64,768]{2,1,0:T(8,128)(2,1)} %bitcast.69), channel_id=1, replica_groups=mesh['dp'=8,'seq'=16] {'seq'}, dimensions={0} | all-to-all | bytes 3145728 | tf_op jit(solution)/shard_map/all_to_all | solution.py:358
  229.0 0.2 reduce_sum.12
  229.3 3.5 %collective-permute-start.2 = (bf16[64,768]{1,0:T(8,128)(2,1)S(1)}, bf16[64,768]{1,0:T(8,128)(2,1)S(1)}, u32[]{:S(2)}, u32[]{:S(2)}) collective-permute-start(bf16[64,768]{1,0:T(8,128)(2,1)S(1)} %reduce_sum.12), channel_id=1, source_target_pairs={{0,16},{16,0},{32,48},{48,32},{64,80},{80,64},{96,112},{112,96},{1... | collective-permute-start | bytes 294920 | tf_op jit(solution)/shard_map/ppermute | solution.py:361
  232.7 2.0 collective-permute-done.2
  234.8 1.6 collective-permute-start.3
  236.4 2.0 collective-permute-done.3
  238.4 2.9 collective-permute-start.4
  241.3 3.1 %collective-permute-done.4 = bf16[64,768]{1,0:T(8,128)(2,1)S(1)} collective-permute-done((bf16[64,768]{1,0:T(8,128)(2,1)S(1)}, bf16[64,768]{1,0:T(8,128)(2,1)S(1)}, u32[]{:S(2)}, u32[]{:S(2)}) %collective-permute-start.4) | collective-permute-done | bytes 98336 | tf_op jit(solution)/shard_map/ppermute | solution.py:361
  244.5 1.3 broadcast_in_dim.16
  245.8 7.6 %all-to-all-start.3 = ((bf16[16,64,768]{2,1,0:T(8,128)(2,1)}), bf16[16,64,768]{2,1,0:T(8,128)(2,1)}, u32[]{:S(2)}, u32[]{:S(2)}) async-start(bf16[16,64,768]{2,1,0:T(8,128)(2,1)} %broadcast_in_dim.16), calls=%async_computation.3 | async-start | bytes 3145728 | tf_op jit(solution)/shard_map/all_to_all | solution.py:362
  253.4 0.4 collective-permute-start.1
  253.8 1.2 collective-permute-done.1
  254.9 0.7 fusion.6
  255.7 19.7 %all-to-all-done.3 = bf16[16,64,768]{2,1,0:T(8,128)(2,1)} async-done(((bf16[16,64,768]{2,1,0:T(8,128)(2,1)}), bf16[16,64,768]{2,1,0:T(8,128)(2,1)}, u32[]{:S(2)}, u32[]{:S(2)}) %all-to-all-start.3) | async-done | bytes 1572896 | tf_op jit(solution)/shard_map/all_to_all | solution.py:362
  275.4 1.7 slice_convert_fusion
  277.1 4.2 %reshape.62 = f32[5,192,4,192]{3,2,1,0:T(4,128)} reshape(f32[15,64,768]{2,1,0:T(8,128)S(1)} %slice_convert_fusion) | data formatting | bytes 5898240 | tf_op jit(solution)/shard_map/convert_element_type | solution.py:364
  281.3 6.4 %copy.23 = f32[5,4,192,192]{3,2,1,0:T(8,128)} copy(f32[5,4,192,192]{2,1,3,0:T(4,128)} %bitcast.62) | data formatting | bytes 5898240
  287.7 4.1 %fusion.8 = (bf16[16,1,48,768]{3,2,1,0:T(8,128)(2,1)S(1)}, bf16[16,1,48,768]{3,2,1,0:T(8,128)(2,1)}, bf16[16,1,48,768]{3,2,1,0:T(8,128)(2,1)S(1)}, bf16[16,1,48,768]{3,2,1,0:T(8,128)(2,1)}) fusion(bf16[16,4,48,768]{3,2,1,0:T(8,128)(2,1)} %bitcast.63), kind=kLoop, calls=%fused_computation.43 | loop fusion | bytes 9437184 | tf_op jit(solution)/shard_map/slice | solution.py:353
  291.7 0.2 convert_bitcast_fusion.2
  292.0 2.0 copy.24
  293.9 1.4 convert_bitcast_fusion.1
  295.4 2.0 copy.25
  297.3 1.4 convert_bitcast_fusion
  298.8 2.0 copy.26
  300.7 1.7 bitcast_convert_fusion
  (26 shorter events, 0.5 us)
Async XLA Ops:
  7.2 47.8 %all-gather.6.cloned.1.call-start = ((), (), s32[]{:S(2)}) async-start(), calls=%async_computation.5 | async-start | bytes 3342336 | tf_op jit(solution)/shard_map/all_gather | solution.py:310
  10.8 10.6 %copy-start = (bf16[5,4,192,192]{3,2,1,0:T(8,128)(2,1)S(1)}, bf16[5,4,192,192]{3,2,1,0:T(8,128)(2,1)}, u32[]{:S(2)}) copy-start(bf16[5,4,192,192]{3,2,1,0:T(8,128)(2,1)} %param.12) | copy-start | bytes 4423684
  11.7 23.2 %all-to-all-start = ((bf16[16,176,128]{2,1,0:T(8,128)(2,1)}), bf16[16,176,128]{2,1,0:T(8,128)(2,1)S(1)}, u32[]{:S(2)}, u32[]{:S(2)}) async-start(bf16[16,176,128]{2,1,0:T(8,128)(2,1)} %pad_maximum_fusion.2), calls=%async_computation | async-start | bytes 1441792 | tf_op jit(solution)/shard_map/all_to_all | solution.py:313
  19.5 268.1 %all-gather.4.cloned.1.call-start = ((), (), s32[]{:S(2)}) async-start(), calls=%async_computation.4 | async-start | bytes 5013504 | tf_op jit(solution)/shard_map/all_gather | solution.py:352
  34.9 0.9 copy-start.4
  53.6 35.1 %collective-permute-start = (bf16[2048,768]{1,0:T(8,128)(2,1)}, bf16[2048,768]{1,0:T(8,128)(2,1)S(1)}, u32[]{:S(2)}, u32[]{:S(2)}) collective-permute-start(bf16[2048,768]{1,0:T(8,128)(2,1)} %get-tuple-element.15.hidden), channel_id=1, source_target_pairs={{0,1},{1,0},{2,3},{3,2},{4,5},{5,4},{6,7},{7,6},{8,9},{9,8},{10,11... | collective-permute-start | bytes 9437192 | tf_op jit(solution)/shard_map/ppermute | solution.py:331
  88.7 35.4 %copy-start.5 = (f32[192,768]{1,0:T(8,128)S(1)}, f32[192,768]{1,0:T(8,128)}, u32[]{:S(2)}) copy-start(f32[192,768]{1,0:T(8,128)} %get-tuple-element.22) | copy-start | bytes 1769476
  88.7 1.6 copy-start.7
  125.2 27.6 %copy-start.2 = (bf16[8,192,256]{2,1,0:T(8,128)(2,1)S(1)}, bf16[8,192,256]{2,1,0:T(8,128)(2,1)}, u32[]{:S(2)}) copy-start(bf16[8,192,256]{2,1,0:T(8,128)(2,1)} %get-tuple-element.16) | copy-start | bytes 2359300
  125.2 27.6 %copy-start.3 = (bf16[8,192,256]{2,1,0:T(8,128)(2,1)S(1)}, bf16[8,192,256]{2,1,0:T(8,128)(2,1)}, u32[]{:S(2)}) copy-start(bf16[8,192,256]{2,1,0:T(8,128)(2,1)} %get-tuple-element.17) | copy-start | bytes 2359300
  125.2 10.2 %collective-permute-start.5 = (bf16[192,768]{1,0:T(8,128)(2,1)S(1)}, bf16[192,768]{1,0:T(8,128)(2,1)S(1)}, u32[]{:S(2)}, u32[]{:S(2)}) collective-permute-start(bf16[192,768]{1,0:T(8,128)(2,1)S(1)} %add_convert_fusion.3), channel_id=1, source_target_pairs={{0,16},{16,0},{32,48},{48,32},{64,80},{80,64},{96,112},{112,96},{1... | collective-permute-start | bytes 884744 | tf_op jit(solution)/shard_map/ppermute | solution.py:351
  135.5 8.0 %collective-permute-start.6 = (bf16[192,768]{1,0:T(8,128)(2,1)S(1)}, bf16[192,768]{1,0:T(8,128)(2,1)S(1)}, u32[]{:S(2)}, u32[]{:S(2)}) collective-permute-start(bf16[192,768]{1,0:T(8,128)(2,1)S(1)} %add_convert_fusion.2), channel_id=1, source_target_pairs={{0,32},{16,48},{32,0},{48,16},{64,96},{80,112},{96,64},{112,80},{1... | collective-permute-start | bytes 884744 | tf_op jit(solution)/shard_map/ppermute | solution.py:351
  143.6 8.4 %collective-permute-start.7 = (bf16[192,768]{1,0:T(8,128)(2,1)S(1)}, bf16[192,768]{1,0:T(8,128)(2,1)S(1)}, u32[]{:S(2)}, u32[]{:S(2)}) collective-permute-start(bf16[192,768]{1,0:T(8,128)(2,1)S(1)} %add_convert_fusion.1), channel_id=1, source_target_pairs={{0,64},{16,80},{32,96},{48,112},{64,0},{80,16},{96,32},{112,48},{1... | collective-permute-start | bytes 884744 | tf_op jit(solution)/shard_map/ppermute | solution.py:351
  154.4 40.1 %all-to-all-start.1 = ((bf16[16,192,256]{2,1,0:T(8,128)(2,1)}), bf16[16,192,256]{2,1,0:T(8,128)(2,1)S(1)}, u32[]{:S(2)}, u32[]{:S(2)}) async-start(bf16[16,192,256]{2,1,0:T(8,128)(2,1)} %bitcast.18), calls=%async_computation.1 | async-start | bytes 3145728 | tf_op jit(solution)/shard_map/all_to_all | solution.py:336
  194.5 1.1 copy-start.1
  229.3 5.5 %collective-permute-start.2 = (bf16[64,768]{1,0:T(8,128)(2,1)S(1)}, bf16[64,768]{1,0:T(8,128)(2,1)S(1)}, u32[]{:S(2)}, u32[]{:S(2)}) collective-permute-start(bf16[64,768]{1,0:T(8,128)(2,1)S(1)} %reduce_sum.12), channel_id=1, source_target_pairs={{0,16},{16,0},{32,48},{48,32},{64,80},{80,64},{96,112},{112,96},{1... | collective-permute-start | bytes 294920 | tf_op jit(solution)/shard_map/ppermute | solution.py:361
  234.8 3.6 %collective-permute-start.3 = (bf16[64,768]{1,0:T(8,128)(2,1)S(1)}, bf16[64,768]{1,0:T(8,128)(2,1)S(1)}, u32[]{:S(2)}, u32[]{:S(2)}) collective-permute-start(bf16[64,768]{1,0:T(8,128)(2,1)S(1)} %add_convert_fusion.7), channel_id=1, source_target_pairs={{0,32},{16,48},{32,0},{48,16},{64,96},{80,112},{96,64},{112,80},{1... | collective-permute-start | bytes 294920 | tf_op jit(solution)/shard_map/ppermute | solution.py:361
  238.4 6.0 %collective-permute-start.4 = (bf16[64,768]{1,0:T(8,128)(2,1)S(1)}, bf16[64,768]{1,0:T(8,128)(2,1)S(1)}, u32[]{:S(2)}, u32[]{:S(2)}) collective-permute-start(bf16[64,768]{1,0:T(8,128)(2,1)S(1)} %add_convert_fusion.6), channel_id=1, source_target_pairs={{0,64},{16,80},{32,96},{48,112},{64,0},{80,16},{96,32},{112,48},{1... | collective-permute-start | bytes 294920 | tf_op jit(solution)/shard_map/ppermute | solution.py:361
  245.8 7.6 %copy-start.6 = (bf16[256,768]{1,0:T(8,128)(2,1)S(1)}, bf16[256,768]{1,0:T(8,128)(2,1)}, u32[]{:S(2)}) copy-start(bf16[256,768]{1,0:T(8,128)(2,1)} %get-tuple-element.20) | copy-start | bytes 1179652
  245.8 29.6 %all-to-all-start.3 = ((bf16[16,64,768]{2,1,0:T(8,128)(2,1)}), bf16[16,64,768]{2,1,0:T(8,128)(2,1)}, u32[]{:S(2)}, u32[]{:S(2)}) async-start(bf16[16,64,768]{2,1,0:T(8,128)(2,1)} %broadcast_in_dim.16), calls=%async_computation.3 | async-start | bytes 3145728 | tf_op jit(solution)/shard_map/all_to_all | solution.py:362
  253.4 1.5 collective-permute-start.1
Sparse Core Ops, SparseCore 0:
  9.7 44.4 all-gather.5
  152.9 56.2 all-gather.3

commit v2 on v1

--- a/solution.py
+++ b/solution.py
@@ -29,6 +29,7 @@
 GELU_A = math.sqrt(2.0 / math.pi)
 GELU_B = 0.044715
 WINDOWS = (0, 1, 3, 4)
+HALF = 512
 
 
 def mm(left, right):
@@ -134,7 +135,7 @@
 
 
 def heads_kernel(
-    hidden, cot, pieces, w_qkv, out, wgrad,
+    hidden, pieces, w_qkv, out,
     q_pad, k_nat, v_nat, q_t, k_t, v_t, ga_t, x_t, scores, rounded, kv_sum,
 ):
     def project(block, carry):
@@ -200,31 +201,23 @@
 
     lax.fori_loop(0, BLOCKS, attend, 0)
 
-    wgrad[...] = jnp.zeros_like(wgrad)
-
     def finish(block, carry):
         rows = pl.ds(pl.multiple_of(block * ROWS, ROWS), ROWS)
         turned = kv_sum[rows, :].T
         x_t[2 * HD : 3 * HD, rows] = (turned[0:HD] * SCALE).astype(BF)
         x_t[3 * HD : 4 * HD, rows] = turned[HD : 2 * HD].astype(BF)
-        piece = x_t[:, rows]
-        out[block] = piece
-        wgrad[0:HD, :] += mm(piece[0:HD], cot[rows, :])
-        wgrad[HD:, :] += mm(piece[HD:], hidden[rows, :])
+        out[block] = x_t[:, rows]
         return carry
 
     lax.fori_loop(0, BLOCKS, finish, 0)
 
 
-def heads(hidden, cot, pieces, w_qkv):
+def heads(hidden, pieces, w_qkv):
     return pl.pallas_call(
         heads_kernel,
-        out_shape=(
-            jax.ShapeDtypeStruct((BLOCKS, 4 * HD, ROWS), BF),
-            jax.ShapeDtypeStruct((4 * HD, C), F32),
-        ),
-        in_specs=[vmem()] * 4,
-        out_specs=(vmem(), vmem()),
+        out_shape=jax.ShapeDtypeStruct((BLOCKS, 4 * HD, ROWS), BF),
+        in_specs=[vmem()] * 3,
+        out_specs=vmem(),
         scratch_shapes=[
             pltpu.VMEM((BINS, 128), BF),
             pltpu.VMEM((BINS, HD), BF),
@@ -241,19 +234,56 @@
         compiler_params=params(),
         cost_estimate=pl.CostEstimate(flops=4 * 10**10, bytes_accessed=10**7, transcendentals=0),
         name="heads",
-    )(hidden, cot, pieces, w_qkv)
+    )(hidden, pieces, w_qkv)
+
+
+def weights_kernel(mine, other, hidden_mine, hidden_other, cot, out, from_cot, from_hidden):
+    from_cot[...] = jnp.zeros_like(from_cot)
+    from_hidden[...] = jnp.zeros_like(from_hidden)
+
+    def add(block, carry):
+        rows = pl.ds(pl.multiple_of(block * ROWS, ROWS), ROWS)
+        one, two = mine[block], other[block]
+        from_cot[...] += mm(jnp.concatenate([one[:HD], two[:HD]], axis=0), cot[rows, :])
+        from_hidden[...] += mm(one[HD:], hidden_mine[rows, :]) + mm(two[HD:], hidden_other[rows, :])
+        return carry
+
+    lax.fori_loop(0, BLOCKS, add, 0)
+    out[0:HD, :] = (from_cot[0:HD, :] + from_cot[HD:, :]).astype(BF)
+    out[HD:, :] = from_hidden[...].astype(BF)
+
+
+def weights(mine, other, hidden_mine, hidden_other, cot):
+    return pl.pallas_call(
+        weights_kernel,
+        out_shape=jax.ShapeDtypeStruct((4 * HD, C), BF),
+        in_specs=[vmem()] * 5,
+        out_specs=vmem(),
+        scratch_shapes=[pltpu.VMEM((2 * HD, C), F32), pltpu.VMEM((3 * HD, C), F32)],
+        compiler_params=params(),
+        cost_estimate=pl.CostEstimate(flops=2 * 10**9, bytes_accessed=10**7, transcendentals=0),
+        name="weights",
+    )(mine, other, hidden_mine, hidden_other, cot)
 
 
 def tail_kernel(
-    info, got, hidden, cot, pre, emb, w_query, w_key, w_value, w_out, branch_out, conv_grad
+    info, got_same, got_cross, hidden, cot, pre, emb, w_query, w_key, w_value, w_out,
+    out_keep, out_give, conv_keep, conv_give, branch_out, conv_grad,
 ):
     step = info[0]
+    core = info[1]
+    same, cross = got_same[...], got_cross[...]
+    even = jnp.where(core == 0, same, cross)
+    odd = jnp.where(core == 0, cross, same)
 
     def rows_of(which):
-        part = got[:, which * HD : (which + 1) * HD, :].reshape(C, ROWS)
+        at = slice(which * HD, (which + 1) * HD)
+        part = jnp.concatenate([x[chip, at] for chip in range(H // 2) for x in (even, odd)], axis=0)
         return part.astype(F32).T.astype(BF)
 
-    branch_out[...] = (hidden[...].astype(F32) + mm(rows_of(0), w_out[...])).astype(BF)
+    branch_out[...] = hidden[...].astype(F32) + mm(rows_of(0), w_out[...])
+    out_keep[...] = branch_out[pl.ds(pl.multiple_of(core * BP, BP), BP), :].astype(BF)
+    out_give[...] = branch_out[pl.ds(pl.multiple_of((1 - core) * BP, BP), BP), :].astype(BF)
     grad = cot[...].astype(F32) + mm_nt(rows_of(1), w_query[...])
     grad = grad + mm_nt(rows_of(2), w_key[...])
     grad = grad + mm_nt(rows_of(3), w_value[...])
@@ -273,46 +303,100 @@
                 at = WINDOWS[group]
                 right = jnp.concatenate([planes[at], planes[at + 1]], axis=1)
                 terms.append(mm(grad_t[group * CG : (group + 1) * CG], right))
-            even, odd = terms
-            thirds = (even[:, :128], jnp.where(low, even[:, 128:], odd[:, :128]), odd[:, 128:])
+            first, last = terms
+            thirds = (first[:, :128], jnp.where(low, first[:, 128:], last[:, :128]), last[:, 128:])
             for third in range(3):
                 plane = 3 * pair + third
-                conv_grad[tap * CG : (tap + 1) * CG, plane * 128 : (plane + 1) * 128] = thirds[third].astype(BF)
-    conv_grad[KW * CG :, :] = jnp.zeros((64, C), BF)
-
-
-def tail(info, got, hidden, cot, pre, emb, w_query, w_key, w_value, w_out):
+                conv_grad[tap * CG : (tap + 1) * CG, plane * 128 : (plane + 1) * 128] = thirds[third]
+    conv_grad[KW * CG :, :] = jnp.zeros((HALF * 2 - KW * CG, C), F32)
+    conv_keep[...] = conv_grad[pl.ds(pl.multiple_of(core * HALF, HALF), HALF), :].astype(BF)
+    conv_give[...] = conv_grad[pl.ds(pl.multiple_of((1 - core) * HALF, HALF), HALF), :].astype(BF)
+
+
+def tail(info, got_same, got_cross, hidden, cot, pre, emb, w_query, w_key, w_value, w_out):
+    def whole(x):
+        return pl.BlockSpec(x.shape, lambda i, info: (0,) * x.ndim)
+
+    own = pl.BlockSpec((ROWS, C), lambda i, info: (info[2], 0))
+    outs = [jax.ShapeDtypeStruct(s, BF) for s in ((BP, C), (BP, C), (HALF, C), (HALF, C))]
     return pl.pallas_call(
         tail_kernel,
-        out_shape=(
-            jax.ShapeDtypeStruct((ROWS, C), BF),
-            jax.ShapeDtypeStruct((KW * CG + 64, C), BF),
+        out_shape=outs,
+        grid_spec=pltpu.PrefetchScalarGridSpec(
+            num_scalar_prefetch=1,
+            grid=(1,),
+            in_specs=[whole(got_same), whole(got_cross), own, own]
+            + [whole(x) for x in (pre, emb, w_query, w_key, w_value, w_out)],
+            out_specs=[whole(x) for x in outs],
+            scratch_shapes=[pltpu.VMEM((ROWS, C), F32), pltpu.VMEM((2 * HALF, C), F32)],
         ),
-        in_specs=[smem()] + [vmem()] * 9,
-        out_specs=(vmem(), vmem()),
         compiler_params=params(),
         cost_estimate=pl.CostEstimate(flops=5 * 10**9, bytes_accessed=10**7, transcendentals=0),
         name="tail",
-    )(info, got, hidden, cot, pre, emb, w_query, w_key, w_value, w_out)
-
-
-def apart(axis, bit):
-    return [(i, i ^ bit) for i in range(lax.axis_size(axis))]
+    )(info, got_same, got_cross, hidden, cot, pre, emb, w_query, w_key, w_value, w_out)
+
+
+def unpack_weights_kernel(parts, *outs):
+    for which in range(4):
+        part = parts[:, which * HD : (which + 1) * HD, :].reshape(C, C).astype(F32)
+        outs[which][...] = part if which == 0 else part.T
+
+
+def unpack_weights(parts):
+    return pl.pallas_call(
+        unpack_weights_kernel,
+        out_shape=[jax.ShapeDtypeStruct((C, C), F32)] * 4,
+        in_specs=[vmem()],
+        out_specs=[vmem()] * 4,
+        compiler_params=params(),
+        cost_estimate=pl.CostEstimate(flops=10**7, bytes_accessed=14 * 10**6, transcendentals=0),
+        name="unpack_weights",
+    )(parts)
+
+
+def unpack_conv_kernel(info, mine, other, out):
+    core = info[1]
+    mine, other = mine[...], other[...]
+    low = jnp.where(core == 0, mine, other)
+    high = jnp.where(core == 0, other, mine)
+    full = jnp.concatenate([low, high], axis=0)
+    for tap in range(KW):
+        out[tap] = full[tap * CG : (tap + 1) * CG].astype(F32).T.reshape(G, CG, CG)
+
+
+def unpack_conv(info, mine, other):
+    return pl.pallas_call(
+        unpack_conv_kernel,
+        out_shape=jax.ShapeDtypeStruct((KW, G, CG, CG), F32),
+        in_specs=[smem(), vmem(), vmem()],
+        out_specs=vmem(),
+        compiler_params=params(),
+        cost_estimate=pl.CostEstimate(flops=10**7, bytes_accessed=5 * 10**6, transcendentals=0),
+        name="unpack_conv",
+    )(info, mine, other)
+
+
+SWAP = [(0, 1), (1, 0)]
+SEQ = ("chip", "core")
+ALL_CHIPS = ("dp", "chip")
+
+
+def to_chips(x, axes):
+    return lax.all_to_all(x, axes, 0, 0, tiled=True)
 
 
 def body(tokens, dilation, w_stem, conv_w, w_query, w_key, w_value, w_out, cotangent):
-    me = lax.axis_index("seq")
-    core = me & 1
-    chip = me >> 1
+    core = lax.axis_index("core")
+    chip = lax.axis_index("chip")
+    me = lax.axis_index(SEQ)
     step = jnp.where(core == 1, -dilation[0], dilation[0])
     info = jnp.stack([step, core, chip]).astype(jnp.int32)
     own_cot = cotangent[0]
-    cot = lax.all_gather(own_cot, "seq", axis=0, tiled=True)
     ga_t = lax.dot_general(w_out, own_cot, (((1,), (1,)), ((), ())), preferred_element_type=F32).astype(BF)
     letters = jnp.broadcast_to(tokens.reshape(1, BP, BP).astype(BF), (H, BP, BP))
-    pieces = lax.all_to_all(
-        jnp.concatenate([letters, ga_t.reshape(H, HD, BP)], axis=1), "seq", 0, 0, tiled=True
-    )
+    pieces = to_chips(jnp.concatenate([letters, ga_t.reshape(H, HD, BP)], axis=1), SEQ)
+    pieces, own_cot = lax.optimization_barrier((pieces, own_cot))
+    cot = lax.all_gather(own_cot, SEQ, axis=0, tiled=True)
     taps = conv_w.transpose(1, 0, 2, 3)
     conv = jnp.stack(
         [
@@ -328,44 +412,35 @@
         axis=1,
     )
     hidden, pre_own, emb_own = front(info, pieces, w_stem, conv)
-    hidden_other = lax.ppermute(hidden, "seq", apart("seq", 1))
-    mine, wgrad_mine = heads(hidden, cot, pieces, w_qkv)
-    other, wgrad_other = heads(hidden_other, cot, pieces, w_qkv)
-    first = jnp.where(core == 0, mine, other)
-    second = jnp.where(core == 0, other, mine)
-    got = lax.all_to_all(
-        jnp.stack([first, second], axis=1).reshape(H, 4 * HD, ROWS), "seq", 0, 0, tiled=True
+    hidden_other = lax.ppermute(hidden, "core", SWAP)
+    mine = heads(hidden, pieces, w_qkv)
+    got_same = to_chips(mine, "chip")
+    other = heads(hidden_other, pieces, w_qkv)
+    got_cross = to_chips(lax.ppermute(other, "core", SWAP), "chip")
+
+    wgrad = weights(mine, other, hidden, hidden_other, cot)
+    wgrad = to_chips(wgrad, "dp").reshape(8, 24, C)
+    wgrad = jnp.sum(wgrad.astype(F32), axis=0).astype(BF)
+    wgrad = to_chips(jnp.broadcast_to(wgrad[None], (8, 24, C)), "dp").reshape(4 * HD, C)
+    grad_out, grad_query, grad_key, grad_value = unpack_weights(lax.all_gather(wgrad, SEQ, axis=0))
+
+    out_keep, out_give, conv_keep, conv_give = tail(
+        info, got_same, got_cross, hidden, cot, pre_own, emb_own, w_query, w_key, w_value, w_out
     )
-    hidden_own = lax.dynamic_slice_in_dim(hidden, chip * ROWS, ROWS, 0)
-    cot_own = lax.dynamic_slice_in_dim(cot, chip * ROWS, ROWS, 0)
-    branch_out, conv_grad = tail(
-        info, got, hidden_own, cot_own, pre_own, emb_own, w_query, w_key, w_value, w_out
-    )
-    keep = lax.dynamic_slice_in_dim(branch_out, core * BP, BP, 0)
-    give = lax.dynamic_slice_in_dim(branch_out, (1 - core) * BP, BP, 0)
-    taken = lax.ppermute(give, "seq", apart("seq", 1))
-    mixed = (keep.astype(F32) + taken.astype(F32)).astype(BF)[None]
-
-    wgrad = (wgrad_mine + wgrad_other).astype(BF)
-    for bit in (1, 2, 4):
-        wgrad = (wgrad.astype(F32) + lax.ppermute(wgrad, "dp", apart("dp", bit)).astype(F32)).astype(BF)
-    wgrads = lax.all_gather(wgrad, "seq", axis=0, tiled=True).reshape(H, 4, HD, C)
-    grad_out = wgrads[:, 0].reshape(C, C).astype(F32)
-    grad_query, grad_key, grad_value = (
-        wgrads[:, which].reshape(C, C).T.astype(F32) for which in (1, 2, 3)
-    )
-
-    parts = lax.all_to_all(conv_grad.reshape(H, 64, C), "seq", 0, 0, tiled=True)
-    share = jnp.sum(parts.reshape(H, 64, C).astype(F32), axis=0).astype(BF)
-    for bit in (1, 2, 4):
-        share = (share.astype(F32) + lax.ppermute(share, "dp", apart("dp", bit)).astype(F32)).astype(BF)
-    whole = lax.all_to_all(jnp.broadcast_to(share[None], (H, 64, C)), "seq", 0, 0, tiled=True)
-    whole = whole.reshape(H * 64, C)[: KW * CG].reshape(KW, CG, G, CG)
-    grad_conv = whole.transpose(0, 2, 3, 1).astype(F32)
+    conv_taken = lax.ppermute(conv_give, "core", SWAP)
+    share = (conv_keep.astype(F32) + conv_taken.astype(F32)).astype(BF)
+    parts = to_chips(share, ALL_CHIPS).reshape(64, HALF // 64, C)
+    share = jnp.sum(parts.astype(F32), axis=0).astype(BF)
+    conv_mine = to_chips(jnp.broadcast_to(share[None], (64, HALF // 64, C)), ALL_CHIPS).reshape(HALF, C)
+    grad_conv = unpack_conv(info, conv_mine, lax.ppermute(conv_mine, "core", SWAP))
+
+    taken = lax.ppermute(out_give, "core", SWAP)
+    mixed = (out_keep.astype(F32) + taken.astype(F32)).astype(BF)[None]
     return (mixed, grad_conv, grad_query, grad_key, grad_value, grad_out)
 
 
 def solution(mesh):
-    in_specs = (P("dp", "seq"), P("dp"), P(), P(), P(), P(), P(), P(), P("dp", "seq", None))
-    out_specs = (P("dp", "seq", None), P(), P(), P(), P(), P())
-    return jax.shard_map(body, mesh=mesh, in_specs=in_specs, out_specs=out_specs, check_vma=False)
+    split = jax.sharding.Mesh(mesh.devices.reshape(8, 8, 2), ("dp", "chip", "core"))
+    in_specs = (P("dp", SEQ), P("dp"), P(), P(), P(), P(), P(), P(), P("dp", SEQ, None))
+    out_specs = (P("dp", SEQ, None), P(), P(), P(), P(), P())
+    return jax.shard_map(body, mesh=split, in_specs=in_specs, out_specs=out_specs, check_vma=False)

time: 311 us -> 269 us (0.86)
  blocking collectives: 26 us -> 105 us
  waiting for transfers between devices: 83.9 us -> 7.5 us
  local copies, waits for them, and re-layouts: 33.6 us -> 7.72 us
  starting transfers between devices: 41.2 us -> 16.8 us
  Pallas kernels: 92.6 us -> 107 us
  other arithmetic: 15.2 us -> 7.57 us
    all_to_all x1 -> x6, blocking collectives: 26 us -> 105 us  [to_chips(): return lax.all_to_all(x, axes, 0, 0, tiled=True)]
    all_to_all x3 -> x1, waiting for transfers between devices: 55.5 us -> 3.23 us  [to_chips(): return lax.all_to_all(x, axes, 0, 0, tiled=True)]
    ppermute x8 -> x5, waiting for transfers between devices: 27.7 us -> 4.24 us  [the longest x1 2.12 us: body(): conv_taken = lax.ppermute(conv_give, 'core', SWAP)]
    all_to_all x3 -> x1, starting transfers between devices: 24.2 us -> 7.84 us  [to_chips(): return lax.all_to_all(x, axes, 0, 0, tiled=True)]
    pallas_call x3 -> x6, Pallas kernels: 74.9 us -> 88.7 us  [the longest x2 62.5 us: heads(): pl.pallas_call(heads_kernel, out_shape=jax.ShapeDtypeStruct((BLOCKS, 4 *...]
    unnamed x20 -> x16, local copies, waits for them, and re-layouts: 15.9 us -> 2.56 us
    convert_element_type x12 -> x0, other arithmetic: 8.59 us -> none  [the longest x3 3.12 us: body(): wgrads[:, which].reshape(C, C).T.astype(F32)]
    ppermute x8 -> x5, starting transfers between devices: 16.9 us -> 8.9 us  [the longest x1 3.71 us: body(): lax.ppermute(conv_mine, 'core', SWAP)]
  transfers between devices with their start and end apart: 13 -> 8, of which waited for: 10 -> 3; matrix products, arithmetic and copies ran while one was open for 10% -> 4% of each run, Pallas kernels for 19% -> 34%
where the time goes in v2:
time: 269 us; the launch traced here: 268 us
  Pallas kernels  107 us (40%)
  blocking collectives  105 us (39%)
  starting transfers between devices  16.8 us (6%)
  between operations  14.8 us (6%)
  local copies, waits for them, and re-layouts  7.72 us (3%)
  other arithmetic  7.57 us (3%)
  waiting for transfers between devices  7.5 us (3%)
    all_to_all x6, blocking collectives, to_chips(): return lax.all_to_all(x, axes, 0, 0, tiled=True)  105 us
    pallas_call x2, Pallas kernels, heads(): pl.pallas_call(heads_kernel, out_shape=jax.ShapeDtypeStruct((BLOCKS, 4 *...  62.5 us
    pallas_call x1, Pallas kernels, front(): pl.pallas_call(front_kernel, out_shape=(jax.ShapeDtypeStruct((BINS, C), B...  17.9 us
    pallas_call x1, Pallas kernels, tail(): pl.pallas_call(tail_kernel, out_shape=outs, grid_spec=pltpu.PrefetchScala...  8.13 us
    all_to_all x1, starting transfers between devices, to_chips(): return lax.all_to_all(x, axes, 0, 0, tiled=True)  7.84 us
    pallas_call x1, Pallas kernels, weights(): pl.pallas_call(weights_kernel, out_shape=jax.ShapeDtypeStruct((4 * HD, C)...  7.8 us
    pallas_call x1, Pallas kernels, unpack_weights(): pl.pallas_call(unpack_weights_kernel, out_shape=[jax.ShapeDtypeStruct((C,...  6.38 us
  transfers between devices with their start and end apart: 8, of which 3 were waited for; matrix products, arithmetic and copies ran while one was open for 4% of the time, Pallas kernels for 34%

profile of v2, /device:TPU:1, one launch (start us, length us, event | category | flops | bytes accessed | tf_op | source)
XLA Modules:
  0.0 268.0 jit_solution(3820544657198209173)
XLA Ops:
  7.2 1.0 convert_reduce_fusion
  8.2 1.7 convolution_convert_fusion
  9.9 0.1 broadcast_in_dim.8
  10.0 0.0 copy-start.3
  10.1 0.9 pad_maximum_fusion.1
  11.0 7.8 %all-to-all-start = ((bf16[16,176,128]{2,1,0:T(8,128)(2,1)}), bf16[16,176,128]{2,1,0:T(8,128)(2,1)}, u32[]{:S(2)}, u32[]{:S(2)}) async-start(bf16[16,176,128]{2,1,0:T(8,128)(2,1)} %pad_maximum_fusion.1), calls=%async_computation | async-start | bytes 1441792 | tf_op jit(solution)/shard_map/all_to_all | solution.py:385
  18.8 0.0 all-gather.3.cloned.1.call-start
  19.5 0.0 copy-done.3
  19.5 1.0 slice_bitcast_fusion.3
  20.5 1.1 constant_dynamic-slice_fusion.2
  21.6 0.7 pad_add_fusion.info
  22.3 1.1 pad.24
  23.4 0.2 pad.27
  23.6 0.1 pad.26
  23.7 0.2 pad.25
  23.9 1.3 constant_dynamic-slice_fusion
  25.2 0.9 fusion.6.w_qkv
  26.1 1.8 pad_maximum_fusion.conv
  28.0 3.2 %all-to-all-done.pieces = bf16[16,176,128]{2,1,0:T(8,128)(2,1)} async-done(((bf16[16,176,128]{2,1,0:T(8,128)(2,1)}), bf16[16,176,128]{2,1,0:T(8,128)(2,1)}, u32[]{:S(2)}, u32[]{:S(2)}) %all-to-all-start) | async-done | bytes 720928 | tf_op jit(solution)/shard_map/all_to_all | solution.py:385
  31.2 0.0 all-gather.3.cloned.1.call-update
  31.2 0.0 all-gather.5.cloned.1.call-start
  31.3 17.9 %front.1 = (bf16[2048,768]{1,0:T(8,128)(2,1)}, f32[256,768]{1,0:T(8,128)}, f32[6,320,128]{2,1,0:T(8,128)}) custom-call(s32[3]{0:T(128)} %pad_add_fusion.info, bf16[16,176,128]{2,1,0:T(8,128)(2,1)} %all-to-all-done.pieces, bf16[512,768]{1,0:T(8,128)(2,1)} %w_stem.1, bf16[4,1280,256]{2,1,0:T(8,128)(2,1)} %pad_maximum_fusion.conv), custom_call_target="tpu_custom_call" | custom-call | flops 20000000000 | bytes 10000000 | tf_op jit(solution)/shard_map/front/pallas_call | solution.py:118
  49.2 0.8 collective-permute-start
  50.0 31.3 %heads.2.mine = bf16[8,192,256]{2,1,0:T(8,128)(2,1)} custom-call(bf16[2048,768]{1,0:T(8,128)(2,1)} %get-tuple-element.20.hidden.hidden_mine, bf16[16,176,128]{2,1,0:T(8,128)(2,1)} %all-to-all-done.pieces, bf16[768,384]{1,0:T(8,128)(2,1)} %fusion.6.w_qkv), custom_call_target="tpu_custom_call" | custom-call | flops 40000000000 | bytes 10000000 | tf_op jit(solution)/shard_map/heads/pallas_call | solution.py:216
  81.3 0.0 collective-permute-done.hidden.hidden_other
  81.3 0.0 copy-start
  81.3 1.6 copy-done
  82.9 31.2 %heads.3.other = bf16[8,192,256]{2,1,0:T(8,128)(2,1)} custom-call(bf16[2048,768]{1,0:T(8,128)(2,1)} %copy-done, bf16[16,176,128]{2,1,0:T(8,128)(2,1)} %all-to-all-done.pieces, bf16[768,384]{1,0:T(8,128)(2,1)} %fusion.6.w_qkv), custom_call_target="tpu_custom_call" | custom-call | flops 40000000000 | bytes 10000000 | tf_op jit(solution)/shard_map/heads/pallas_call | solution.py:216
  114.1 0.0 all-gather.3.cloned.1.call-done.cot
  114.1 7.8 %weights.1 = bf16[192,768]{1,0:T(8,128)(2,1)} custom-call(bf16[8,192,256]{2,1,0:T(8,128)(2,1)} %heads.2.mine, bf16[8,192,256]{2,1,0:T(8,128)(2,1)} %heads.3.other, bf16[2048,768]{1,0:T(8,128)(2,1)} %get-tuple-element.20.hidden.hidden_mine, bf16[2048,768]{1,0:T(8,128)(2,1)} %copy-done, bf16[2048,768]{1,0:T(8,128)(2,1)} %all-gather.3.cloned.1.call-done.cot), custom_call_target="tpu_custom_call" | custom-call | flops 2000000000 | bytes 10000000 | tf_op jit(solution)/shard_map/weights/pallas_call | solution.py:257
  121.9 0.0 copy-start.5
  121.9 0.0 copy-start.2
  121.9 15.1 %all_to_all.43 = bf16[8,24,768]{2,1,0:T(8,128)(2,1)S(1)} all-to-all(bf16[8,24,768]{2,1,0:T(8,128)(2,1)} %bitcast.39), channel_id=1, replica_groups=mesh['dp'=8,'chip'=8,'core'=2] {'dp'}, dimensions={0} | all-to-all | bytes 589824 | tf_op jit(solution)/shard_map/all_to_all | solution.py:385
  137.1 11.1 %all_to_all.44 = bf16[8,24,768]{2,1,0:T(8,128)(2,1)} all-to-all(bf16[8,24,768]{2,1,0:T(8,128)(2,1)S(1)} %broadcast_in_dim.11), channel_id=1, replica_groups=mesh['dp'=8,'chip'=8,'core'=2] {'dp'}, dimensions={0} | all-to-all | bytes 589824 | tf_op jit(solution)/shard_map/all_to_all | solution.py:385
  148.2 0.0 all-gather.5.cloned.1.call-update
  148.2 0.0 copy-done.5
  148.2 2.7 collective-permute-start.1
  150.9 0.0 copy-done.2
  150.9 21.5 %all_to_all.45.got_same = bf16[8,192,256]{2,1,0:T(8,128)(2,1)} all-to-all(bf16[8,192,256]{2,1,0:T(8,128)(2,1)S(1)} %copy-done.2), channel_id=1, replica_groups=mesh['dp'=8,'chip'=8,'core'=2] {'chip'}, dimensions={0} | all-to-all | bytes 1572864 | tf_op jit(solution)/shard_map/all_to_all | solution.py:385
  172.3 0.0 collective-permute-done.1
  172.4 21.1 %all_to_all.46.got_cross = bf16[8,192,256]{2,1,0:T(8,128)(2,1)} all-to-all(bf16[8,192,256]{2,1,0:T(8,128)(2,1)S(1)} %collective-permute-done.1), channel_id=1, replica_groups=mesh['dp'=8,'chip'=8,'core'=2] {'chip'}, dimensions={0} | all-to-all | bytes 1572864 | tf_op jit(solution)/shard_map/all_to_all | solution.py:385
  193.4 8.1 %tail.1 = (bf16[128,768]{1,0:T(8,128)(2,1)}, bf16[128,768]{1,0:T(8,128)(2,1)}, bf16[512,768]{1,0:T(8,128)(2,1)}, bf16[512,768]{1,0:T(8,128)(2,1)}) custom-call(s32[3]{0:T(128)} %pad_add_fusion.info, bf16[8,192,256]{2,1,0:T(8,128)(2,1)} %all_to_all.45.got_same, bf16[8,192,256]{2,1,0:T(8,128)(2,1)} %all_to_all.46.got_cross, ...), custom_call_target="tpu_custom_call" | custom-call | flops 5000000000 | bytes 10000000 | tf_op jit(solution)/shard_map/tail/pallas_call | solution.py:322
  201.5 1.6 collective-permute-start.3
  203.2 2.1 collective-permute-done.3
  205.3 1.3 fusion.4
  206.6 18.7 %all_to_all.47 = bf16[64,8,768]{2,1,0:T(8,128)(2,1)S(1)} all-to-all(bf16[64,8,768]{2,1,0:T(8,128)(2,1)S(1)} %fusion.4), channel_id=1, replica_groups=mesh['dp'=8,'chip'=8,'core'=2] {'dp','chip'}, dimensions={0} | all-to-all | bytes 1572864 | tf_op jit(solution)/shard_map/all_to_all | solution.py:385
  225.3 0.0 copy-start.7
  225.3 0.0 copy-start.6
  225.3 0.1 reduce_sum.24
  225.4 0.1 broadcast_in_dim.10
  225.5 17.8 %all_to_all.48 = bf16[64,8,768]{2,1,0:T(8,128)(2,1)S(1)} all-to-all(bf16[64,8,768]{2,1,0:T(8,128)(2,1)S(1)} %broadcast_in_dim.10), channel_id=1, replica_groups=mesh['dp'=8,'chip'=8,'core'=2] {'dp','chip'}, dimensions={0} | all-to-all | bytes 1572864 | tf_op jit(solution)/shard_map/all_to_all | solution.py:385
  243.3 0.0 copy-start.1
  243.3 3.7 %collective-permute-start.4 = (bf16[512,768]{1,0:T(8,128)(2,1)S(1)}, bf16[512,768]{1,0:T(8,128)(2,1)S(1)}, u32[]{:S(2)}, u32[]{:S(2)}) collective-permute-start(bf16[512,768]{1,0:T(8,128)(2,1)S(1)} %bitcast.32), channel_id=1, source_target_pairs={{0,1},{1,0},{2,3},{3,2},{4,5},{5,4},{6,7},{7,6},{8,9},{9,8},{10,11... | collective-permute-start | bytes 2359304 | tf_op jit(solution)/shard_map/ppermute | solution.py:435
  247.0 0.0 copy-done.7
  247.0 0.1 collective-permute-start.2
  247.1 2.1 collective-permute-done.2
  249.2 0.0 copy-done.6
  249.2 0.7 fusion.7
  250.0 0.0 collective-permute-done.4.other
  250.0 0.0 copy-done.1
  250.0 0.0 copy-start.4
  250.0 0.9 copy-done.4
  250.9 3.9 %unpack_conv.1 = f32[5,4,192,192]{3,2,1,0:T(8,128)} custom-call(s32[3]{0:T(128)} %pad_add_fusion.info, bf16[512,768]{1,0:T(8,128)(2,1)} %bitcast.33, bf16[512,768]{1,0:T(8,128)(2,1)} %copy-done.4), custom_call_target="tpu_custom_call" | custom-call | flops 10000000 | bytes 5000000 | tf_op jit(solution)/shard_map/unpack_conv/pallas_call | solution.py:368
  254.7 6.4 %unpack_weights.1 = (f32[768,768]{1,0:T(8,128)}, f32[768,768]{1,0:T(8,128)}, f32[768,768]{1,0:T(8,128)}, f32[768,768]{1,0:T(8,128)}) custom-call(bf16[16,192,768]{2,1,0:T(8,128)(2,1)} %all-gather.5.cloned.1.call-done.parts), custom_call_target="tpu_custom_call" | custom-call | flops 10000000 | bytes 14000000 | tf_op jit(solution)/shard_map/unpack_weights/pallas_call | solution.py:346
  (3 shorter events, 0.1 us)
Async XLA Ops:
  10.0 9.5 %copy-start.3 = (bf16[5,4,192,192]{3,2,1,0:T(8,128)(2,1)S(1)}, bf16[5,4,192,192]{3,2,1,0:T(8,128)(2,1)}, u32[]{:S(2)}) copy-start(bf16[5,4,192,192]{3,2,1,0:T(8,128)(2,1)} %param.12) | copy-start | bytes 4423684
  11.0 20.2 %all-to-all-start = ((bf16[16,176,128]{2,1,0:T(8,128)(2,1)}), bf16[16,176,128]{2,1,0:T(8,128)(2,1)}, u32[]{:S(2)}, u32[]{:S(2)}) async-start(bf16[16,176,128]{2,1,0:T(8,128)(2,1)} %pad_maximum_fusion.1), calls=%async_computation | async-start | bytes 1441792 | tf_op jit(solution)/shard_map/all_to_all | solution.py:385
  18.8 95.3 %all-gather.3.cloned.1.call-start = ((), (), s32[]{:S(2)}) async-start(), calls=%async_computation.7 | async-start | bytes 3342336 | tf_op jit(solution)/shard_map/all_gather | solution.py:399
  31.2 223.5 %all-gather.5.cloned.1.call-start = ((), (), s32[]{:S(2)}) async-start(), calls=%async_computation.8 | async-start | bytes 5013504 | tf_op jit(solution)/shard_map/all_gather | solution.py:425
  49.2 32.1 %collective-permute-start = (bf16[2048,768]{1,0:T(8,128)(2,1)}, bf16[2048,768]{1,0:T(8,128)(2,1)S(1)}, u32[]{:S(2)}, u32[]{:S(2)}) collective-permute-start(bf16[2048,768]{1,0:T(8,128)(2,1)} %get-tuple-element.20.hidden.hidden_mine), channel_id=1, source_target_pairs={{0,1},{1,0},{2,3},{3,2},{4,5},{5,4},{6,7},{7,6},{8,9},{9,8},{10,11... | collective-permute-start | bytes 9437192 | tf_op jit(solution)/shard_map/ppermute | solution.py:415
  81.3 1.7 copy-start
  121.9 26.3 %copy-start.5 = (bf16[8,192,256]{2,1,0:T(8,128)(2,1)S(1)}, bf16[8,192,256]{2,1,0:T(8,128)(2,1)}, u32[]{:S(2)}) copy-start(bf16[8,192,256]{2,1,0:T(8,128)(2,1)} %heads.3.other) | copy-start | bytes 2359300
  121.9 29.0 %copy-start.2 = (bf16[8,192,256]{2,1,0:T(8,128)(2,1)S(1)}, bf16[8,192,256]{2,1,0:T(8,128)(2,1)}, u32[]{:S(2)}) copy-start(bf16[8,192,256]{2,1,0:T(8,128)(2,1)} %heads.2.mine) | copy-start | bytes 2359300
  148.2 24.1 %collective-permute-start.1 = (bf16[8,192,256]{2,1,0:T(8,128)(2,1)S(1)}, bf16[8,192,256]{2,1,0:T(8,128)(2,1)S(1)}, u32[]{:S(2)}, u32[]{:S(2)}) collective-permute-start(bf16[8,192,256]{2,1,0:T(8,128)(2,1)S(1)} %copy-done.5), channel_id=1, source_target_pairs={{0,1},{1,0},{2,3},{3,2},{4,5},{5,4},{6,7},{7,6},{8,9},{9,8},{10,11... | collective-permute-start | bytes 2359304 | tf_op jit(solution)/shard_map/ppermute | solution.py:419
  201.5 3.8 %collective-permute-start.3 = (bf16[512,768]{1,0:T(8,128)(2,1)}, bf16[512,768]{1,0:T(8,128)(2,1)S(1)}, u32[]{:S(2)}, u32[]{:S(2)}) collective-permute-start(bf16[512,768]{1,0:T(8,128)(2,1)} %get-tuple-element.27), channel_id=1, source_target_pairs={{0,1},{1,0},{2,3},{3,2},{4,5},{5,4},{6,7},{7,6},{8,9},{9,8},{10,11... | collective-permute-start | bytes 2359304 | tf_op jit(solution)/shard_map/ppermute | solution.py:430
  225.3 21.8 %copy-start.7 = (bf16[128,768]{1,0:T(8,128)(2,1)S(1)}, bf16[128,768]{1,0:T(8,128)(2,1)}, u32[]{:S(2)}) copy-start(bf16[128,768]{1,0:T(8,128)(2,1)} %get-tuple-element.25) | copy-start | bytes 589828
  225.3 23.9 %copy-start.6 = (bf16[128,768]{1,0:T(8,128)(2,1)S(1)}, bf16[128,768]{1,0:T(8,128)(2,1)}, u32[]{:S(2)}) copy-start(bf16[128,768]{1,0:T(8,128)(2,1)} %get-tuple-element.24) | copy-start | bytes 589828
  243.3 6.6 %copy-start.1 = (bf16[64,8,768]{2,1,0:T(8,128)(2,1)}, bf16[64,8,768]{2,1,0:T(8,128)(2,1)S(1)}, u32[]{:S(2)}) copy-start(bf16[64,8,768]{2,1,0:T(8,128)(2,1)S(1)} %all_to_all.48) | copy-start | bytes 2359300
  243.3 6.6 %collective-permute-start.4 = (bf16[512,768]{1,0:T(8,128)(2,1)S(1)}, bf16[512,768]{1,0:T(8,128)(2,1)S(1)}, u32[]{:S(2)}, u32[]{:S(2)}) collective-permute-start(bf16[512,768]{1,0:T(8,128)(2,1)S(1)} %bitcast.32), channel_id=1, source_target_pairs={{0,1},{1,0},{2,3},{3,2},{4,5},{5,4},{6,7},{7,6},{8,9},{9,8},{10,11... | collective-permute-start | bytes 2359304 | tf_op jit(solution)/shard_map/ppermute | solution.py:435
  247.0 2.2 collective-permute-start.2
  250.0 0.9 copy-start.4
Sparse Core Ops, SparseCore 0:
  31.3 35.6 all-gather.2
  148.3 51.1 all-gather.4

commit v3 on v2

--- a/solution.py
+++ b/solution.py
@@ -238,28 +238,31 @@
 
 
 def weights_kernel(mine, other, hidden_mine, hidden_other, cot, out, from_cot, from_hidden):
-    from_cot[...] = jnp.zeros_like(from_cot)
-    from_hidden[...] = jnp.zeros_like(from_hidden)
-
-    def add(block, carry):
-        rows = pl.ds(pl.multiple_of(block * ROWS, ROWS), ROWS)
-        one, two = mine[block], other[block]
-        from_cot[...] += mm(jnp.concatenate([one[:HD], two[:HD]], axis=0), cot[rows, :])
-        from_hidden[...] += mm(one[HD:], hidden_mine[rows, :]) + mm(two[HD:], hidden_other[rows, :])
-        return carry
-
-    lax.fori_loop(0, BLOCKS, add, 0)
-    out[0:HD, :] = (from_cot[0:HD, :] + from_cot[HD:, :]).astype(BF)
-    out[HD:, :] = from_hidden[...].astype(BF)
+    @pl.when(pl.program_id(0) == 0)
+    def _():
+        from_cot[...] = jnp.zeros_like(from_cot)
+        from_hidden[...] = jnp.zeros_like(from_hidden)
+
+    one, two = mine[0], other[0]
+    from_cot[...] += mm(one[:HD], cot[...]) + mm(two[:HD], cot[...])
+    from_hidden[...] += mm(one[HD:], hidden_mine[...]) + mm(two[HD:], hidden_other[...])
+
+    @pl.when(pl.program_id(0) == BLOCKS - 1)
+    def _():
+        out[0:HD, :] = from_cot[...].astype(BF)
+        out[HD:, :] = from_hidden[...].astype(BF)
 
 
 def weights(mine, other, hidden_mine, hidden_other, cot):
+    piece = pl.BlockSpec((1, 4 * HD, ROWS), lambda i: (i, 0, 0))
+    rows = pl.BlockSpec((ROWS, C), lambda i: (i, 0))
     return pl.pallas_call(
         weights_kernel,
         out_shape=jax.ShapeDtypeStruct((4 * HD, C), BF),
-        in_specs=[vmem()] * 5,
-        out_specs=vmem(),
-        scratch_shapes=[pltpu.VMEM((2 * HD, C), F32), pltpu.VMEM((3 * HD, C), F32)],
+        grid=(BLOCKS,),
+        in_specs=[piece, piece, rows, rows, rows],
+        out_specs=pl.BlockSpec((4 * HD, C), lambda i: (0, 0)),
+        scratch_shapes=[pltpu.VMEM((HD, C), F32), pltpu.VMEM((3 * HD, C), F32)],
         compiler_params=params(),
         cost_estimate=pl.CostEstimate(flops=2 * 10**9, bytes_accessed=10**7, transcendentals=0),
         name="weights",
@@ -379,6 +382,10 @@
 SWAP = [(0, 1), (1, 0)]
 SEQ = ("chip", "core")
 ALL_CHIPS = ("dp", "chip")
+
+
+def apart(axis, bit):
+    return [(i, i ^ bit) for i in range(lax.axis_size(axis))]
 
 
 def to_chips(x, axes):
@@ -416,24 +423,30 @@
     mine = heads(hidden, pieces, w_qkv)
     got_same = to_chips(mine, "chip")
     other = heads(hidden_other, pieces, w_qkv)
+    mine, other, got_same = lax.optimization_barrier((mine, other, got_same))
     got_cross = to_chips(lax.ppermute(other, "core", SWAP), "chip")
-
     wgrad = weights(mine, other, hidden, hidden_other, cot)
-    wgrad = to_chips(wgrad, "dp").reshape(8, 24, C)
-    wgrad = jnp.sum(wgrad.astype(F32), axis=0).astype(BF)
-    wgrad = to_chips(jnp.broadcast_to(wgrad[None], (8, 24, C)), "dp").reshape(4 * HD, C)
-    grad_out, grad_query, grad_key, grad_value = unpack_weights(lax.all_gather(wgrad, SEQ, axis=0))
-
+    once = lax.ppermute(wgrad, "dp", apart("dp", 1))
+    once, got_cross = lax.optimization_barrier((once, got_cross))
+    wgrad = (wgrad.astype(F32) + once.astype(F32)).astype(BF)
+    twice = lax.ppermute(wgrad, "dp", apart("dp", 2))
     out_keep, out_give, conv_keep, conv_give = tail(
         info, got_same, got_cross, hidden, cot, pre_own, emb_own, w_query, w_key, w_value, w_out
     )
+    twice, conv_give, out_give = lax.optimization_barrier((twice, conv_give, out_give))
+    wgrad = (wgrad.astype(F32) + twice.astype(F32)).astype(BF)
+    thrice = lax.ppermute(wgrad, "dp", apart("dp", 4))
     conv_taken = lax.ppermute(conv_give, "core", SWAP)
     share = (conv_keep.astype(F32) + conv_taken.astype(F32)).astype(BF)
     parts = to_chips(share, ALL_CHIPS).reshape(64, HALF // 64, C)
+    thrice, parts = lax.optimization_barrier((thrice, parts))
+    wgrad = (wgrad.astype(F32) + thrice.astype(F32)).astype(BF)
+    wgrads = lax.all_gather(wgrad, SEQ, axis=0)
     share = jnp.sum(parts.astype(F32), axis=0).astype(BF)
     conv_mine = to_chips(jnp.broadcast_to(share[None], (64, HALF // 64, C)), ALL_CHIPS).reshape(HALF, C)
     grad_conv = unpack_conv(info, conv_mine, lax.ppermute(conv_mine, "core", SWAP))
 
+    grad_out, grad_query, grad_key, grad_value = unpack_weights(wgrads)
     taken = lax.ppermute(out_give, "core", SWAP)
     mixed = (out_keep.astype(F32) + taken.astype(F32)).astype(BF)[None]
     return (mixed, grad_conv, grad_query, grad_key, grad_value, grad_out)

time: 269 us -> 249 us (0.926)
  blocking collectives: 105 us -> 21.4 us
  waiting for transfers between devices: 7.5 us -> 45.7 us
  starting transfers between devices: 16.8 us -> 39.2 us
  other arithmetic: 7.57 us -> 10.3 us
    all_to_all x6 -> x1, blocking collectives: 105 us -> 21.4 us  [to_chips(): return lax.all_to_all(x, axes, 0, 0, tiled=True)]
    ppermute x0 -> x3, waiting for transfers between devices: none -> 20.8 us  [the longest x1 14.5 us: body(): thrice = lax.ppermute(wgrad, 'dp', apart('dp', 4))]
    all_to_all x1 -> x4, starting transfers between devices: 7.84 us -> 26.8 us  [to_chips(): return lax.all_to_all(x, axes, 0, 0, tiled=True)]
    all_gather x1, waiting for transfers between devices: 0.01 us -> 13.9 us  [body(): wgrads = lax.all_gather(wgrad, SEQ, axis=0)]
    ppermute x0 -> x3, starting transfers between devices: none -> 6.5 us  [the longest x1 2.69 us: body(): thrice = lax.ppermute(wgrad, 'dp', apart('dp', 4))]
  transfers between devices with their start and end apart: 8 -> 14, of which waited for: 3 -> 8; matrix products, arithmetic and copies ran while one was open for 4% -> 4% of each run, Pallas kernels for 34% -> 33%
where the time goes in v3:
time: 249 us; the launch traced here: 248 us
  Pallas kernels  107 us (43%)
  waiting for transfers between devices  45.7 us (18%)
  starting transfers between devices  39.2 us (16%)
  blocking collectives  21.4 us (9%)
  between operations  14.9 us (6%)
  other arithmetic  10.3 us (4%)
  local copies, waits for them, and re-layouts  7.72 us (3%)
    pallas_call x2, Pallas kernels, heads(): pl.pallas_call(heads_kernel, out_shape=jax.ShapeDtypeStruct((BLOCKS, 4 *...  62.4 us
    all_to_all x4, starting transfers between devices, to_chips(): return lax.all_to_all(x, axes, 0, 0, tiled=True)  26.8 us
    all_to_all x1, blocking collectives, to_chips(): return lax.all_to_all(x, axes, 0, 0, tiled=True)  21.4 us
    pallas_call x1, Pallas kernels, front(): pl.pallas_call(front_kernel, out_shape=(jax.ShapeDtypeStruct((BINS, C), B...  17.8 us
    ppermute x1, waiting for transfers between devices, body(): thrice = lax.ppermute(wgrad, 'dp', apart('dp', 4))  14.5 us
    all_gather x1, waiting for transfers between devices, body(): wgrads = lax.all_gather(wgrad, SEQ, axis=0)  13.9 us
    pallas_call x1, Pallas kernels, weights(): pl.pallas_call(weights_kernel, out_shape=jax.ShapeDtypeStruct((4 * HD, C)...  8.46 us
    pallas_call x1, Pallas kernels, tail(): pl.pallas_call(tail_kernel, out_shape=outs, grid_spec=pltpu.PrefetchScala...  8.05 us
  transfers between devices with their start and end apart: 14, of which 8 were waited for; matrix products, arithmetic and copies ran while one was open for 4% of the time, Pallas kernels for 33%

profile of v3, /device:TPU:1, one launch (start us, length us, event | category | flops | bytes accessed | tf_op | source)
XLA Modules:
  0.0 248.1 jit_solution(798359262047622959)
XLA Ops:
  7.2 1.0 convert_reduce_fusion
  8.2 1.7 convolution_convert_fusion
  9.9 0.1 broadcast_in_dim.6
  10.0 0.0 copy-start.2
  10.1 0.9 pad_maximum_fusion.1
  11.0 7.8 %all-to-all-start = ((bf16[16,176,128]{2,1,0:T(8,128)(2,1)}), bf16[16,176,128]{2,1,0:T(8,128)(2,1)}, u32[]{:S(2)}, u32[]{:S(2)}) async-start(bf16[16,176,128]{2,1,0:T(8,128)(2,1)} %pad_maximum_fusion.1), calls=%async_computation | async-start | bytes 1441792 | tf_op jit(solution)/shard_map/all_to_all | solution.py:392
  18.8 0.0 all-gather.4.cloned.1.call-start
  18.9 0.0 copy-done.2
  18.9 1.0 slice_bitcast_fusion.3
  20.5 1.1 constant_dynamic-slice_fusion.2
  21.6 0.6 pad_add_fusion.info
  22.2 1.2 pad.25
  23.5 0.1 pad.26
  23.6 0.2 pad.27
  23.8 0.1 pad.24
  23.9 1.3 constant_dynamic-slice_fusion
  25.2 1.0 fusion.6.w_qkv
  26.2 1.8 pad_maximum_fusion.conv
  28.0 3.2 %all-to-all-done.pieces = bf16[16,176,128]{2,1,0:T(8,128)(2,1)} async-done(((bf16[16,176,128]{2,1,0:T(8,128)(2,1)}), bf16[16,176,128]{2,1,0:T(8,128)(2,1)}, u32[]{:S(2)}, u32[]{:S(2)}) %all-to-all-start) | async-done | bytes 720928 | tf_op jit(solution)/shard_map/all_to_all | solution.py:392
  31.2 17.8 %front.1 = (bf16[2048,768]{1,0:T(8,128)(2,1)}, f32[256,768]{1,0:T(8,128)}, f32[6,320,128]{2,1,0:T(8,128)}) custom-call(s32[3]{0:T(128)} %pad_add_fusion.info, bf16[16,176,128]{2,1,0:T(8,128)(2,1)} %all-to-all-done.pieces, bf16[512,768]{1,0:T(8,128)(2,1)} %w_stem.1, bf16[4,1280,256]{2,1,0:T(8,128)(2,1)} %pad_maximum_fusion.conv), custom_call_target="tpu_custom_call" | custom-call | flops 20000000000 | bytes 10000000 | tf_op jit(solution)/shard_map/front/pallas_call | solution.py:118
  49.0 0.9 collective-permute-start
  49.9 0.0 all-gather.4.cloned.1.call-update
  49.9 31.2 %heads.2.mine = bf16[8,192,256]{2,1,0:T(8,128)(2,1)} custom-call(bf16[2048,768]{1,0:T(8,128)(2,1)} %get-tuple-element.30.hidden.hidden_mine, bf16[16,176,128]{2,1,0:T(8,128)(2,1)} %all-to-all-done.pieces, bf16[768,384]{1,0:T(8,128)(2,1)} %fusion.6.w_qkv), custom_call_target="tpu_custom_call" | custom-call | flops 40000000000 | bytes 10000000 | tf_op jit(solution)/shard_map/heads/pallas_call | solution.py:216
  81.1 4.2 %all-to-all-start.1 = ((bf16[8,192,256]{2,1,0:T(8,128)(2,1)}), bf16[8,192,256]{2,1,0:T(8,128)(2,1)}, u32[]{:S(2)}, u32[]{:S(2)}) async-start(bf16[8,192,256]{2,1,0:T(8,128)(2,1)} %heads.2.mine), calls=%async_computation.1 | async-start | bytes 1572864 | tf_op jit(solution)/shard_map/all_to_all | solution.py:392
  85.3 0.0 collective-permute-done.hidden.hidden_other
  85.3 1.7 copy-done
  87.0 31.2 %heads.3.other = bf16[8,192,256]{2,1,0:T(8,128)(2,1)} custom-call(bf16[2048,768]{1,0:T(8,128)(2,1)} %copy-done, bf16[16,176,128]{2,1,0:T(8,128)(2,1)} %all-to-all-done.pieces, bf16[768,384]{1,0:T(8,128)(2,1)} %fusion.6.w_qkv), custom_call_target="tpu_custom_call" | custom-call | flops 40000000000 | bytes 10000000 | tf_op jit(solution)/shard_map/heads/pallas_call | solution.py:216
  118.2 0.0 all-to-all-done.1.got_same
  118.2 0.0 collective-permute-start.2
  118.2 2.6 %collective-permute-done.2 = bf16[8,192,256]{2,1,0:T(8,128)(2,1)} collective-permute-done((bf16[8,192,256]{2,1,0:T(8,128)(2,1)}, bf16[8,192,256]{2,1,0:T(8,128)(2,1)}, u32[]{:S(2)}, u32[]{:S(2)}) %collective-permute-start.2) | collective-permute-done | bytes 786464 | tf_op jit(solution)/shard_map/ppermute | solution.py:427
  120.8 5.0 %all-to-all-start.2 = ((bf16[8,192,256]{2,1,0:T(8,128)(2,1)}), bf16[8,192,256]{2,1,0:T(8,128)(2,1)S(1)}, u32[]{:S(2)}, u32[]{:S(2)}) async-start(bf16[8,192,256]{2,1,0:T(8,128)(2,1)} %collective-permute-done.2), calls=%async_computation.2 | async-start | bytes 1572864 | tf_op jit(solution)/shard_map/all_to_all | solution.py:392
  125.9 0.0 all-gather.4.cloned.1.call-done.cot
  125.9 8.5 %weights.1 = bf16[192,768]{1,0:T(8,128)(2,1)} custom-call(bf16[8,192,256]{2,1,0:T(8,128)(2,1)} %heads.2.mine, bf16[8,192,256]{2,1,0:T(8,128)(2,1)} %heads.3.other, bf16[2048,768]{1,0:T(8,128)(2,1)} %get-tuple-element.30.hidden.hidden_mine, bf16[2048,768]{1,0:T(8,128)(2,1)} %copy-done, bf16[2048,768]{1,0:T(8,128)(2,1)} %all-gather.4.cloned.1.call-done.cot), custom_call_target="tpu_custom_call" | custom-call | flops 2000000000 | bytes 10000000 | tf_op jit(solution)/shard_map/weights/pallas_call | solution.py:259
  134.4 2.6 %collective-permute-start.1 = (bf16[192,768]{1,0:T(8,128)(2,1)}, bf16[192,768]{1,0:T(8,128)(2,1)S(1)}, u32[]{:S(2)}, u32[]{:S(2)}) collective-permute-start(bf16[192,768]{1,0:T(8,128)(2,1)} %weights.1), channel_id=1, source_target_pairs={{0,16},{16,0},{32,48},{48,32},{64,80},{80,64},{96,112},{112,96},{1... | collective-permute-start | bytes 884744 | tf_op jit(solution)/shard_map/ppermute | solution.py:429
  137.0 0.8 all-to-all-done.2.got_cross
  137.8 6.3 %collective-permute-done.1 = bf16[192,768]{1,0:T(8,128)(2,1)S(1)} collective-permute-done((bf16[192,768]{1,0:T(8,128)(2,1)}, bf16[192,768]{1,0:T(8,128)(2,1)S(1)}, u32[]{:S(2)}, u32[]{:S(2)}) %collective-permute-start.1) | collective-permute-done | bytes 294944 | tf_op jit(solution)/shard_map/ppermute | solution.py:429
  144.1 1.0 add_convert_fusion.3
  145.1 1.2 collective-permute-start.3
  146.3 8.1 %tail.1 = (bf16[128,768]{1,0:T(8,128)(2,1)}, bf16[128,768]{1,0:T(8,128)(2,1)}, bf16[512,768]{1,0:T(8,128)(2,1)}, bf16[512,768]{1,0:T(8,128)(2,1)}) custom-call(s32[3]{0:T(128)} %pad_add_fusion.info, bf16[8,192,256]{2,1,0:T(8,128)(2,1)} %all-to-all-done.1.got_same, bf16[8,192,256]{2,1,0:T(8,128)(2,1)} %copy-done.3, ...), custom_call_target="tpu_custom_call" | custom-call | flops 5000000000 | bytes 10000000 | tf_op jit(solution)/shard_map/tail/pallas_call | solution.py:325
  154.3 0.0 collective-permute-done.3
  154.4 1.7 collective-permute-start.6
  156.0 2.1 collective-permute-done.6
  158.2 2.2 fusion.4
  160.4 9.7 %all-to-all-start.3 = ((bf16[64,8,768]{2,1,0:T(8,128)(2,1)}), bf16[64,8,768]{2,1,0:T(8,128)(2,1)S(1)}, u32[]{:S(2)}, u32[]{:S(2)}) async-start(bf16[64,8,768]{2,1,0:T(8,128)(2,1)} %fusion.4), calls=%async_computation.3 | async-start | bytes 1572864 | tf_op jit(solution)/shard_map/all_to_all | solution.py:392
  170.1 0.0 all-gather.6.cloned.1.call-start
  170.1 0.1 add_convert_fusion.2
  170.2 2.7 %collective-permute-start.5 = (bf16[192,768]{1,0:T(8,128)(2,1)S(1)}, bf16[192,768]{1,0:T(8,128)(2,1)S(1)}, u32[]{:S(2)}, u32[]{:S(2)}) collective-permute-start(bf16[192,768]{1,0:T(8,128)(2,1)S(1)} %add_convert_fusion.2), channel_id=1, source_target_pairs={{0,64},{16,80},{32,96},{48,112},{64,0},{80,16},{96,32},{112,48},{1... | collective-permute-start | bytes 884744 | tf_op jit(solution)/shard_map/ppermute | solution.py:438
  172.9 14.5 %collective-permute-done.5 = bf16[192,768]{1,0:T(8,128)(2,1)S(1)} collective-permute-done((bf16[192,768]{1,0:T(8,128)(2,1)S(1)}, bf16[192,768]{1,0:T(8,128)(2,1)S(1)}, u32[]{:S(2)}, u32[]{:S(2)}) %collective-permute-start.5) | collective-permute-done | bytes 294944 | tf_op jit(solution)/shard_map/ppermute | solution.py:438
  187.4 0.0 all-to-all-done.3
  187.4 0.8 add_convert_fusion.1
  188.2 0.0 all-gather.6.cloned.1.call-update
  188.2 0.0 copy-start.5
  188.2 0.1 reduce_sum.12
  188.4 0.1 broadcast_in_dim.16
  188.4 21.4 %all_to_all.29 = bf16[64,8,768]{2,1,0:T(8,128)(2,1)S(1)} all-to-all(bf16[64,8,768]{2,1,0:T(8,128)(2,1)S(1)} %broadcast_in_dim.16), channel_id=1, replica_groups=mesh['dp'=8,'chip'=8,'core'=2] {'dp','chip'}, dimensions={0} | all-to-all | bytes 1572864 | tf_op jit(solution)/shard_map/all_to_all | solution.py:392
  209.8 3.2 %collective-permute-start.7 = (bf16[512,768]{1,0:T(8,128)(2,1)S(1)}, bf16[512,768]{1,0:T(8,128)(2,1)S(1)}, u32[]{:S(2)}, u32[]{:S(2)}) collective-permute-start(bf16[512,768]{1,0:T(8,128)(2,1)S(1)} %bitcast.32), channel_id=1, source_target_pairs={{0,1},{1,0},{2,3},{3,2},{4,5},{5,4},{6,7},{7,6},{8,9},{9,8},{10,11... | collective-permute-start | bytes 2359304 | tf_op jit(solution)/shard_map/ppermute | solution.py:447
  213.0 0.1 collective-permute-start.4
  213.1 2.3 collective-permute-done.4
  215.4 0.7 fusion.7
  216.1 0.0 collective-permute-done.7.other
  216.1 0.9 copy-done.4
  217.0 3.9 %unpack_conv.1 = f32[5,4,192,192]{3,2,1,0:T(8,128)} custom-call(s32[3]{0:T(128)} %pad_add_fusion.info, bf16[512,768]{1,0:T(8,128)(2,1)} %bitcast.33, bf16[512,768]{1,0:T(8,128)(2,1)} %copy-done.4), custom_call_target="tpu_custom_call" | custom-call | flops 10000000 | bytes 5000000 | tf_op jit(solution)/shard_map/unpack_conv/pallas_call | solution.py:371
  220.9 13.9 %all-gather.6.cloned.1.call-done = bf16[3072,768]{1,0:T(8,128)(2,1)} async-done(((bf16[192,768]{1,0:T(8,128)(2,1)}), bf16[3072,768]{1,0:T(8,128)(2,1)}) %all-gather.6.cloned.1.call-update) | async-done | bytes 4718608 | tf_op jit(solution)/shard_map/all_gather | solution.py:444
  234.8 6.4 %unpack_weights.1 = (f32[768,768]{1,0:T(8,128)}, f32[768,768]{1,0:T(8,128)}, f32[768,768]{1,0:T(8,128)}, f32[768,768]{1,0:T(8,128)}) custom-call(bf16[16,192,768]{2,1,0:T(8,128)(2,1)} %bitcast.31), custom_call_target="tpu_custom_call" | custom-call | flops 10000000 | bytes 14000000 | tf_op jit(solution)/shard_map/unpack_weights/pallas_call | solution.py:349
  (9 shorter events, 0.0 us)
Async XLA Ops:
  10.0 8.8 %copy-start.2 = (bf16[5,4,192,192]{3,2,1,0:T(8,128)(2,1)S(1)}, bf16[5,4,192,192]{3,2,1,0:T(8,128)(2,1)}, u32[]{:S(2)}) copy-start(bf16[5,4,192,192]{3,2,1,0:T(8,128)(2,1)} %param.12) | copy-start | bytes 4423684
  11.0 20.2 %all-to-all-start = ((bf16[16,176,128]{2,1,0:T(8,128)(2,1)}), bf16[16,176,128]{2,1,0:T(8,128)(2,1)}, u32[]{:S(2)}, u32[]{:S(2)}) async-start(bf16[16,176,128]{2,1,0:T(8,128)(2,1)} %pad_maximum_fusion.1), calls=%async_computation | async-start | bytes 1441792 | tf_op jit(solution)/shard_map/all_to_all | solution.py:392
  18.8 107.1 %all-gather.4.cloned.1.call-start = ((), (), s32[]{:S(2)}) async-start(), calls=%async_computation.5 | async-start | bytes 3342336 | tf_op jit(solution)/shard_map/all_gather | solution.py:406
  49.0 36.3 %collective-permute-start = (bf16[2048,768]{1,0:T(8,128)(2,1)}, bf16[2048,768]{1,0:T(8,128)(2,1)S(1)}, u32[]{:S(2)}, u32[]{:S(2)}) collective-permute-start(bf16[2048,768]{1,0:T(8,128)(2,1)} %get-tuple-element.30.hidden.hidden_mine), channel_id=1, source_target_pairs={{0,1},{1,0},{2,3},{3,2},{4,5},{5,4},{6,7},{7,6},{8,9},{9,8},{10,11... | collective-permute-start | bytes 9437192 | tf_op jit(solution)/shard_map/ppermute | solution.py:422
  81.1 37.1 %all-to-all-start.1 = ((bf16[8,192,256]{2,1,0:T(8,128)(2,1)}), bf16[8,192,256]{2,1,0:T(8,128)(2,1)}, u32[]{:S(2)}, u32[]{:S(2)}) async-start(bf16[8,192,256]{2,1,0:T(8,128)(2,1)} %heads.2.mine), calls=%async_computation.1 | async-start | bytes 1572864 | tf_op jit(solution)/shard_map/all_to_all | solution.py:392
  85.3 1.7 copy-start
  118.2 2.6 %collective-permute-start.2 = (bf16[8,192,256]{2,1,0:T(8,128)(2,1)}, bf16[8,192,256]{2,1,0:T(8,128)(2,1)}, u32[]{:S(2)}, u32[]{:S(2)}) collective-permute-start(bf16[8,192,256]{2,1,0:T(8,128)(2,1)} %heads.3.other), channel_id=1, source_target_pairs={{0,1},{1,0},{2,3},{3,2},{4,5},{5,4},{6,7},{7,6},{8,9},{9,8},{10,11... | collective-permute-start | bytes 2359304 | tf_op jit(solution)/shard_map/ppermute | solution.py:427
  120.8 17.0 %all-to-all-start.2 = ((bf16[8,192,256]{2,1,0:T(8,128)(2,1)}), bf16[8,192,256]{2,1,0:T(8,128)(2,1)S(1)}, u32[]{:S(2)}, u32[]{:S(2)}) async-start(bf16[8,192,256]{2,1,0:T(8,128)(2,1)} %collective-permute-done.2), calls=%async_computation.2 | async-start | bytes 1572864 | tf_op jit(solution)/shard_map/all_to_all | solution.py:392
  134.4 9.7 %collective-permute-start.1 = (bf16[192,768]{1,0:T(8,128)(2,1)}, bf16[192,768]{1,0:T(8,128)(2,1)S(1)}, u32[]{:S(2)}, u32[]{:S(2)}) collective-permute-start(bf16[192,768]{1,0:T(8,128)(2,1)} %weights.1), channel_id=1, source_target_pairs={{0,16},{16,0},{32,48},{48,32},{64,80},{80,64},{96,112},{112,96},{1... | collective-permute-start | bytes 884744 | tf_op jit(solution)/shard_map/ppermute | solution.py:429
  137.8 8.5 %copy-start.3 = (bf16[8,192,256]{2,1,0:T(8,128)(2,1)}, bf16[8,192,256]{2,1,0:T(8,128)(2,1)S(1)}, u32[]{:S(2)}) copy-start(bf16[8,192,256]{2,1,0:T(8,128)(2,1)S(1)} %all-to-all-done.2.got_cross) | copy-start | bytes 2359300
  145.1 9.2 %collective-permute-start.3 = (bf16[192,768]{1,0:T(8,128)(2,1)S(1)}, bf16[192,768]{1,0:T(8,128)(2,1)S(1)}, u32[]{:S(2)}, u32[]{:S(2)}) collective-permute-start(bf16[192,768]{1,0:T(8,128)(2,1)S(1)} %add_convert_fusion.3), channel_id=1, source_target_pairs={{0,32},{16,48},{32,0},{48,16},{64,96},{80,112},{96,64},{112,80},{1... | collective-permute-start | bytes 884744 | tf_op jit(solution)/shard_map/ppermute | solution.py:432
  154.4 3.8 %collective-permute-start.6 = (bf16[512,768]{1,0:T(8,128)(2,1)}, bf16[512,768]{1,0:T(8,128)(2,1)S(1)}, u32[]{:S(2)}, u32[]{:S(2)}) collective-permute-start(bf16[512,768]{1,0:T(8,128)(2,1)} %get-tuple-element.45), channel_id=1, source_target_pairs={{0,1},{1,0},{2,3},{3,2},{4,5},{5,4},{6,7},{7,6},{8,9},{9,8},{10,11... | collective-permute-start | bytes 2359304 | tf_op jit(solution)/shard_map/ppermute | solution.py:439
  160.4 27.0 %all-to-all-start.3 = ((bf16[64,8,768]{2,1,0:T(8,128)(2,1)}), bf16[64,8,768]{2,1,0:T(8,128)(2,1)S(1)}, u32[]{:S(2)}, u32[]{:S(2)}) async-start(bf16[64,8,768]{2,1,0:T(8,128)(2,1)} %fusion.4), calls=%async_computation.3 | async-start | bytes 1572864 | tf_op jit(solution)/shard_map/all_to_all | solution.py:392
  170.1 64.8 %all-gather.6.cloned.1.call-start = ((), (), s32[]{:S(2)}) async-start(), calls=%async_computation.6 | async-start | bytes 5013504 | tf_op jit(solution)/shard_map/all_gather | solution.py:444
  170.2 17.2 %collective-permute-start.5 = (bf16[192,768]{1,0:T(8,128)(2,1)S(1)}, bf16[192,768]{1,0:T(8,128)(2,1)S(1)}, u32[]{:S(2)}, u32[]{:S(2)}) collective-permute-start(bf16[192,768]{1,0:T(8,128)(2,1)S(1)} %add_convert_fusion.2), channel_id=1, source_target_pairs={{0,64},{16,80},{32,96},{48,112},{64,0},{80,16},{96,32},{112,48},{1... | collective-permute-start | bytes 884744 | tf_op jit(solution)/shard_map/ppermute | solution.py:438
  188.2 24.8 %copy-start.6 = (bf16[128,768]{1,0:T(8,128)(2,1)S(1)}, bf16[128,768]{1,0:T(8,128)(2,1)}, u32[]{:S(2)}) copy-start(bf16[128,768]{1,0:T(8,128)(2,1)} %get-tuple-element.42) | copy-start | bytes 589828
  188.2 27.2 %copy-start.5 = (bf16[128,768]{1,0:T(8,128)(2,1)S(1)}, bf16[128,768]{1,0:T(8,128)(2,1)}, u32[]{:S(2)}) copy-start(bf16[128,768]{1,0:T(8,128)(2,1)} %get-tuple-element.38) | copy-start | bytes 589828
  209.8 6.3 %copy-start.1 = (bf16[64,8,768]{2,1,0:T(8,128)(2,1)}, bf16[64,8,768]{2,1,0:T(8,128)(2,1)S(1)}, u32[]{:S(2)}) copy-start(bf16[64,8,768]{2,1,0:T(8,128)(2,1)S(1)} %all_to_all.29) | copy-start | bytes 2359300
  209.8 6.3 %collective-permute-start.7 = (bf16[512,768]{1,0:T(8,128)(2,1)S(1)}, bf16[512,768]{1,0:T(8,128)(2,1)S(1)}, u32[]{:S(2)}, u32[]{:S(2)}) collective-permute-start(bf16[512,768]{1,0:T(8,128)(2,1)S(1)} %bitcast.32), channel_id=1, source_target_pairs={{0,1},{1,0},{2,3},{3,2},{4,5},{5,4},{6,7},{7,6},{8,9},{9,8},{10,11... | collective-permute-start | bytes 2359304 | tf_op jit(solution)/shard_map/ppermute | solution.py:447
  213.0 2.4 collective-permute-start.4
  216.1 0.9 copy-start.4
Sparse Core Ops, SparseCore 0:
  50.0 34.9 all-gather.3
  188.3 46.4 all-gather.5

commit v4 on v2

v4 whole, which is shorter than its diff:
```python
import functools
import math

import jax
import jax.numpy as jnp
from jax import lax
from jax.experimental import pallas as pl
from jax.experimental.pallas import tpu as pltpu
from jax.sharding import PartitionSpec as P

H = 16
G = 4
KW = 5
DMAX = 16
MARGIN = 2 * DMAX
C = 768
CG = C // G
HD = C // H
BP = 128
BINS = 2048
ROWS = 256
BLOCKS = BINS // ROWS
WIDE = 1024
PLANES = C // 128
PIECE = BP + HD
SCALE = HD ** (-0.5)
BF = jnp.bfloat16
F32 = jnp.float32
VMEM_LIMIT = 56 * 1024 * 1024
GELU_A = math.sqrt(2.0 / math.pi)
GELU_B = 0.044715
WINDOWS = (0, 1, 3, 4)
HALF = 512


def mm(left, right):
    return jnp.dot(left, right, preferred_element_type=F32)


def mm_nt(left, right):
    return lax.dot_general(left, right, (((1,), (1,)), ((), ())), preferred_element_type=F32)


def vmem():
    return pl.BlockSpec(memory_space=pltpu.VMEM)


def smem():
    return pl.BlockSpec(memory_space=pltpu.SMEM)


def params(**extra):
    return pltpu.CompilerParams(vmem_limit_bytes=VMEM_LIMIT, **extra)


def front_kernel(info, pieces, w_stem, conv, hidden, pre_own, emb_own, stem, emb, pre):
    step = info[0]
    core = info[1]
    chip = info[2]
    block = pl.program_id(0)

    @pl.when(block == 0)
    def _():
        row = lax.broadcasted_iota(jnp.int32, (4 * BP, 4 * BP), 0)
        col = lax.broadcasted_iota(jnp.int32, (4 * BP, 4 * BP), 1)
        source = 4 * (row & (BP - 1)) + (row >> 7)
        source = jnp.where(core == 1, 4 * BP - 1 - source, source)
        stem[...] = mm((col == source).astype(BF), w_stem[...]).astype(BF)
        edge = jnp.zeros((PLANES, MARGIN, 128), F32)
        emb[:, 0:MARGIN, :] = edge
        emb[:, MARGIN + BINS : MARGIN + BINS + MARGIN, :] = edge

        def embed(block, carry):
            letters = pieces[pl.ds((WIDE // BP) * block, WIDE // BP), 0:BP, :].astype(F32).reshape(WIDE, BP)
            hot = jnp.concatenate([(letters == float(c)).astype(BF) for c in range(4)], axis=1)
            rows = mm(hot, stem[...]).astype(BF).astype(F32)
            start = pl.multiple_of(MARGIN + block * WIDE, 8)
            for plane in range(PLANES):
                emb[plane, pl.ds(start, WIDE), :] = rows[:, plane * 128 : (plane + 1) * 128]
            return carry

        lax.fori_loop(0, BINS // WIDE, embed, 0)

    base = MARGIN + block * WIDE
    for pair in range(2):
        planes = [
            [
                emb[3 * pair + third, pl.ds(base + (tap - KW // 2) * step, WIDE), :].astype(BF)
                for tap in range(KW)
            ]
            for third in range(3)
        ]
        even, odd = (
            mm(
                jnp.concatenate([planes[at + half][tap] for tap in range(KW) for half in range(2)], axis=1),
                conv[2 * pair + at],
            )
            for at in range(2)
        )
        thirds = (even[:, :128], even[:, 128:] + odd[:, :128], odd[:, 128:])
        for third in range(3):
            plane = 3 * pair + third
            x = thirds[third]
            lanes = slice(plane * 128, (plane + 1) * 128)
            pre[pl.ds(pl.multiple_of(block * WIDE, WIDE), WIDE), lanes] = x
            th = jnp.tanh(GELU_A * (x + GELU_B * (x * x * x)))
            act = 0.5 * x * (1.0 + th)
            own = emb[plane, pl.ds(pl.multiple_of(base, 8), WIDE), :]
            hidden[:, lanes] = (own + act).astype(BF)

    @pl.when(block == BINS // WIDE - 1)
    def _():
        pre_own[...] = pre[pl.ds(pl.multiple_of(chip * ROWS, ROWS), ROWS), :]
        emb_own[...] = emb[:, pl.ds(pl.multiple_of(chip * ROWS, ROWS), ROWS + 2 * MARGIN), :]


def front(info, pieces, w_stem, conv):
    return pl.pallas_call(
        front_kernel,
        out_shape=(
            jax.ShapeDtypeStruct((BINS, C), BF),
            jax.ShapeDtypeStruct((ROWS, C), F32),
            jax.ShapeDtypeStruct((PLANES, ROWS + 2 * MARGIN, 128), F32),
        ),
        grid=(BINS // WIDE,),
        in_specs=[
            smem(),
            pl.BlockSpec(pieces.shape, lambda i: (0, 0, 0)),
            pl.BlockSpec(w_stem.shape, lambda i: (0, 0)),
            pl.BlockSpec(conv.shape, lambda i: (0, 0, 0)),
        ],
        out_specs=(
            pl.BlockSpec((WIDE, C), lambda i: (i, 0)),
            pl.BlockSpec((ROWS, C), lambda i: (0, 0)),
            pl.BlockSpec((PLANES, ROWS + 2 * MARGIN, 128), lambda i: (0, 0, 0)),
        ),
        scratch_shapes=[
            pltpu.VMEM((4 * BP, C), BF),
            pltpu.VMEM((PLANES, BINS + 2 * MARGIN, 128), F32),
            pltpu.VMEM((BINS, C), F32),
        ],
        compiler_params=params(),
        cost_estimate=pl.CostEstimate(flops=2 * 10**10, bytes_accessed=10**7, transcendentals=0),
        name="front",
    )(info, pieces, w_stem, conv)


def heads_kernel(
    last, hidden, pieces, w_qkv, *refs
):
    if last:
        cot, mine, from_mine, out, wgrad = refs[:5]
    else:
        out, wgrad = refs[:2]
    q_pad, k_nat, v_nat, q_t, k_t, v_t, ga_t, x_t, scores, both, kv_sum = refs[5 if last else 2 :]

    def project(block, carry):
        rows = pl.ds(pl.multiple_of(block * ROWS, ROWS), ROWS)
        y = mm(hidden[rows, :], w_qkv[...]).astype(BF)
        q_pad[rows, :] = y[:, 0:128]
        k_nat[rows, :] = y[:, 128 : 128 + HD]
        v_nat[rows, :] = y[:, 256 : 256 + HD]
        turned = y.astype(F32).T
        q_t[:, rows] = turned[0:HD].astype(BF)
        k_t[:, rows] = turned[128 : 128 + HD].astype(BF)
        v_t[:, rows] = turned[256 : 256 + HD].astype(BF)
        ga_t[:, rows] = jnp.concatenate([pieces[2 * block, BP:, :], pieces[2 * block + 1, BP:, :]], axis=1)
        return carry

    lax.fori_loop(0, BLOCKS, project, 0)
    kv_sum[...] = jnp.zeros_like(kv_sum)

    def span(block):
        return pl.ds(pl.multiple_of(block * ROWS, ROWS), ROWS)

    def products(slot, block):
        scores[slot] = mm(k_nat[...], q_t[:, span(block)])

    def softmax(slot):
        top = None
        for part in range(BLOCKS):
            at = slice(part * ROWS, (part + 1) * ROWS)
            most = jnp.max(scores[slot, at, :].reshape(ROWS // 8, 8, ROWS), axis=0)
            top = most if top is None else jnp.maximum(top, most)
        top = jnp.max(top, axis=0, keepdims=True)
        total = None
        for part in range(BLOCKS):
            at = slice(part * ROWS, (part + 1) * ROWS)
            e = jnp.exp2((scores[slot, at, :] - top) * (SCALE * math.log2(math.e)))
            scores[slot, at, :] = e
            some = jnp.sum(e.reshape(ROWS // 8, 8, ROWS), axis=0)
            total = some if total is None else total + some
        inverse = 1.0 / jnp.sum(total, axis=0, keepdims=True)
        for part in range(BLOCKS):
            at = slice(part * ROWS, (part + 1) * ROWS)
            both[slot, at, ROWS:] = (scores[slot, at, :] * inverse).astype(BF)
        return inverse

    def mix(slot, block):
        attn = mm(v_t[...], both[slot, :, ROWS:]).astype(BF)
        x_t[0:HD, span(block)] = attn
        return jnp.sum(ga_t[:, span(block)].astype(F32) * attn.astype(F32), axis=0, keepdims=True)

    def score_grads(slot, inverse, row_dot, block):
        gat = ga_t[:, span(block)]
        for part in range(BLOCKS // 2):
            at = slice(part * 2 * ROWS, (part + 1) * 2 * ROWS)
            gp = mm(v_nat[at, :], gat)
            both[slot, at, :ROWS] = ((scores[slot, at, :] * inverse) * (gp - row_dot)).astype(BF)

    def backward(slot, block):
        ga_pad = jnp.concatenate(
            [
                jnp.zeros((HD, ROWS), F32),
                ga_t[:, span(block)].astype(F32),
                jnp.zeros((128 - 2 * HD, ROWS), F32),
            ],
            axis=0,
        ).T.astype(BF)
        right = jnp.concatenate([q_pad[span(block), :], ga_pad], axis=0)
        x_t[HD : 2 * HD, span(block)] = (mm(k_t[...], both[slot, :, :ROWS]) * SCALE).astype(BF)
        kv_sum[...] += mm(both[slot], right)

    both[1] = jnp.zeros((BINS, 2 * ROWS), BF)
    products(0, 0)

    def attend(pair, carry):
        a, b = 2 * pair, 2 * pair + 1
        inv = softmax(0)
        backward(1, jnp.maximum(b - 2, 0))
        dot = mix(0, a)
        products(1, b)
        score_grads(0, inv, dot, a)
        inv = softmax(1)
        backward(0, a)
        dot = mix(1, b)
        products(0, jnp.minimum(b + 1, BLOCKS - 1))
        score_grads(1, inv, dot, b)
        return carry

    lax.fori_loop(0, BLOCKS // 2, attend, 0)
    backward(1, BLOCKS - 1)

    def finish(block, carry):
        rows = pl.ds(pl.multiple_of(block * ROWS, ROWS), ROWS)
        turned = kv_sum[rows, :].T
        x_t[2 * HD : 3 * HD, rows] = (turned[0:HD] * SCALE).astype(BF)
        x_t[3 * HD : 4 * HD, rows] = turned[HD : 2 * HD].astype(BF)
        out[block] = x_t[:, rows]
        return carry

    lax.fori_loop(0, BLOCKS, finish, 0)
    from_hidden = mm(x_t[HD:, :], hidden[...])
    if not last:
        wgrad[...] = from_hidden
        return
    wgrad[HD:, :] = (from_hidden + from_mine[...]).astype(BF)
    attn_mine = jnp.concatenate([mine[block, 0:HD, :] for block in range(BLOCKS)], axis=1)
    from_cot = mm(jnp.concatenate([x_t[0:HD, :], attn_mine], axis=0), cot[...])
    wgrad[0:HD, :] = (from_cot[0:HD] + from_cot[HD:]).astype(BF)


def heads(hidden, pieces, w_qkv, *before):
    last = bool(before)
    return pl.pallas_call(
        functools.partial(heads_kernel, last),
        out_shape=(
            jax.ShapeDtypeStruct((BLOCKS, 4 * HD, ROWS), BF),
            jax.ShapeDtypeStruct((4 * HD, C), BF) if last else jax.ShapeDtypeStruct((3 * HD, C), F32),
        ),
        in_specs=[vmem()] * (3 + len(before)),
        out_specs=(vmem(), vmem()),
        scratch_shapes=[
            pltpu.VMEM((BINS, 128), BF),
            pltpu.VMEM((BINS, HD), BF),
            pltpu.VMEM((BINS, HD), BF),
            pltpu.VMEM((HD, BINS), BF),
            pltpu.VMEM((HD, BINS), BF),
            pltpu.VMEM((HD, BINS), BF),
            pltpu.VMEM((HD, BINS), BF),
            pltpu.VMEM((4 * HD, BINS), BF),
            pltpu.VMEM((2, BINS, ROWS), F32),
            pltpu.VMEM((2, BINS, 2 * ROWS), BF),
            pltpu.VMEM((BINS, 128), F32),
        ],
        compiler_params=params(),
        cost_estimate=pl.CostEstimate(flops=3 * 10**10, bytes_accessed=10**7, transcendentals=0),
        name="heads",
    )(hidden, pieces, w_qkv, *before)


def tail_kernel(
    info, got_same, got_cross, hidden, cot, pre, emb, w_query, w_key, w_value, w_out,
    out_keep, out_give, conv_keep, conv_give, branch_out, conv_grad,
):
    step = info[0]
    core = info[1]
    same, cross = got_same[...], got_cross[...]
    even = jnp.where(core == 0, same, cross)
    odd = jnp.where(core == 0, cross, same)

    def rows_of(which):
        at = slice(which * HD, (which + 1) * HD)
        part = jnp.concatenate([x[chip, at] for chip in range(H // 2) for x in (even, odd)], axis=0)
        return part.astype(F32).T.astype(BF)

    branch_out[...] = hidden[...].astype(F32) + mm(rows_of(0), w_out[...])
    out_keep[...] = branch_out[pl.ds(pl.multiple_of(core * BP, BP), BP), :].astype(BF)
    out_give[...] = branch_out[pl.ds(pl.multiple_of((1 - core) * BP, BP), BP), :].astype(BF)
    grad = cot[...].astype(F32) + mm_nt(rows_of(1), w_query[...])
    grad = grad + mm_nt(rows_of(2), w_key[...])
    grad = grad + mm_nt(rows_of(3), w_value[...])
    x = pre[...]
    square = x * x
    th = jnp.tanh(GELU_A * (x + GELU_B * (square * x)))
    slope = 0.5 * (1.0 + th) + 0.5 * x * (1.0 - th * th) * (GELU_A * (1.0 + 3.0 * GELU_B * square))
    grad_t = (grad * slope).astype(BF).astype(F32).T.astype(BF)
    low = lax.broadcasted_iota(jnp.int32, (CG, 128), 1) < 64
    for tap in range(KW):
        start = MARGIN + (tap - KW // 2) * step
        planes = [emb[plane, pl.ds(start, ROWS), :].astype(BF) for plane in range(PLANES)]
        for pair in range(2):
            terms = []
            for half in range(2):
                group = 2 * pair + half
                at = WINDOWS[group]
                right = jnp.concatenate([planes[at], planes[at + 1]], axis=1)
                terms.append(mm(grad_t[group * CG : (group + 1) * CG], right))
            first, last = terms
            thirds = (first[:, :128], jnp.where(low, first[:, 128:], last[:, :128]), last[:, 128:])
            for third in range(3):
                plane = 3 * pair + third
                conv_grad[tap * CG : (tap + 1) * CG, plane * 128 : (plane + 1) * 128] = thirds[third]
    conv_grad[KW * CG :, :] = jnp.zeros((HALF * 2 - KW * CG, C), F32)
    conv_keep[...] = conv_grad[pl.ds(pl.multiple_of(core * HALF, HALF), HALF), :].astype(BF)
    conv_give[...] = conv_grad[pl.ds(pl.multiple_of((1 - core) * HALF, HALF), HALF), :].astype(BF)


def tail(info, got_same, got_cross, hidden, cot, pre, emb, w_query, w_key, w_value, w_out):
    def whole(x):
        return pl.BlockSpec(x.shape, lambda i, info: (0,) * x.ndim)

    own = pl.BlockSpec((ROWS, C), lambda i, info: (info[2], 0))
    outs = [jax.ShapeDtypeStruct(s, BF) for s in ((BP, C), (BP, C), (HALF, C), (HALF, C))]
    return pl.pallas_call(
        tail_kernel,
        out_shape=outs,
        grid_spec=pltpu.PrefetchScalarGridSpec(
            num_scalar_prefetch=1,
            grid=(1,),
            in_specs=[whole(got_same), whole(got_cross), own, own]
            + [whole(x) for x in (pre, emb, w_query, w_key, w_value, w_out)],
            out_specs=[whole(x) for x in outs],
            scratch_shapes=[pltpu.VMEM((ROWS, C), F32), pltpu.VMEM((2 * HALF, C), F32)],
        ),
        compiler_params=params(),
        cost_estimate=pl.CostEstimate(flops=5 * 10**9, bytes_accessed=10**7, transcendentals=0),
        name="tail",
    )(info, got_same, got_cross, hidden, cot, pre, emb, w_query, w_key, w_value, w_out)


def unpack_weights_kernel(parts, *outs):
    for which in range(4):
        part = parts[:, which * HD : (which + 1) * HD, :].reshape(C, 256).astype(F32)
        outs[which][...] = part if which == 0 else part.T


def unpack_weights(parts):
    turned = pl.BlockSpec((256, C), lambda i: (i, 0))
    return pl.pallas_call(
        unpack_weights_kernel,
        out_shape=[jax.ShapeDtypeStruct((C, C), F32)] * 4,
        grid=(C // 256,),
        in_specs=[pl.BlockSpec((H, 4 * HD, 256), lambda i: (0, 0, i))],
        out_specs=[pl.BlockSpec((C, 256), lambda i: (0, i)), turned, turned, turned],
        compiler_params=params(),
        cost_estimate=pl.CostEstimate(flops=10**7, bytes_accessed=14 * 10**6, transcendentals=0),
        name="unpack_weights",
    )(parts)


def unpack_conv_kernel(info, mine, other, out, full):
    core = info[1]
    tap = pl.program_id(0)

    @pl.when(tap == 0)
    def _():
        full[pl.ds(pl.multiple_of(core * HALF, HALF), HALF), :] = mine[...].astype(F32)
        full[pl.ds(pl.multiple_of((1 - core) * HALF, HALF), HALF), :] = other[...].astype(F32)

    rows = full[pl.ds(pl.multiple_of(tap * CG, 8), CG), :]
    out[0] = rows.T.reshape(G, CG, CG)


def unpack_conv(info, mine, other):
    half = pl.BlockSpec((HALF, C), lambda i: (0, 0))
    return pl.pallas_call(
        unpack_conv_kernel,
        out_shape=jax.ShapeDtypeStruct((KW, G, CG, CG), F32),
        grid=(KW,),
        in_specs=[smem(), half, half],
        out_specs=pl.BlockSpec((1, G, CG, CG), lambda i: (i, 0, 0, 0)),
        scratch_shapes=[pltpu.VMEM((2 * HALF, C), F32)],
        compiler_params=params(),
        cost_estimate=pl.CostEstimate(flops=10**7, bytes_accessed=5 * 10**6, transcendentals=0),
        name="unpack_conv",
    )(info, mine, other)


SWAP = [(0, 1), (1, 0)]
SEQ = ("chip", "core")
ALL_CHIPS = ("dp", "chip")


def apart(axis, bit):
    return [(i, i ^ bit) for i in range(lax.axis_size(axis))]


def to_chips(x, axes):
    return lax.all_to_all(x, axes, 0, 0, tiled=True)


def body(tokens, dilation, w_stem, conv_w, w_query, w_key, w_value, w_out, cotangent):
    core = lax.axis_index("core")
    chip = lax.axis_index("chip")
    me = lax.axis_index(SEQ)
    step = jnp.where(core == 1, -dilation[0], dilation[0])
    info = jnp.stack([step, core, chip]).astype(jnp.int32)
    own_cot = cotangent[0]
    ga_t = lax.dot_general(w_out, own_cot, (((1,), (1,)), ((), ())), preferred_element_type=F32).astype(BF)
    letters = jnp.broadcast_to(tokens.reshape(1, BP, BP).astype(BF), (H, BP, BP))
    pieces = to_chips(jnp.concatenate([letters, ga_t.reshape(H, HD, BP)], axis=1), SEQ)
    taps = conv_w.transpose(1, 0, 2, 3)
    conv = jnp.stack(
        [
            jnp.pad(taps[group], ((0, 0), (64, 0), (64, 0)) if group % 2 else ((0, 0), (0, 64), (0, 64)))
            for group in range(G)
        ]
    ).reshape(G, KW * 256, 256)
    w_qkv = jnp.concatenate(
        [
            jnp.pad(lax.dynamic_slice_in_dim(w, me * HD, HD, 1), ((0, 0), (0, 128 - HD)))
            for w in (w_query, w_key, w_value)
        ],
        axis=1,
    )
    pieces, own_cot, conv, w_qkv, info = lax.optimization_barrier((pieces, own_cot, conv, w_qkv, info))
    cot = lax.all_gather(own_cot, SEQ, axis=0, tiled=True)
    hidden, pre_own, emb_own = front(info, pieces, w_stem, conv)
    hidden_other = lax.ppermute(hidden, "core", SWAP)
    mine, from_mine = heads(hidden, pieces, w_qkv)
    got_same = to_chips(mine, "chip")
    other, wgrad = heads(hidden_other, pieces, w_qkv, cot, mine, from_mine)
    other, wgrad, got_same = lax.optimization_barrier((other, wgrad, got_same))
    got_cross = to_chips(lax.ppermute(other, "core", SWAP), "chip")
    once = lax.ppermute(wgrad, "dp", apart("dp", 1))
    wgrad = (wgrad.astype(F32) + once.astype(F32)).astype(BF)
    twice = lax.ppermute(wgrad, "dp", apart("dp", 2))
    twice, got_cross = lax.optimization_barrier((twice, got_cross))
    wgrad = (wgrad.astype(F32) + twice.astype(F32)).astype(BF)
    thrice = lax.ppermute(wgrad, "dp", apart("dp", 4))
    out_keep, out_give, conv_keep, conv_give = tail(
        info, got_same, got_cross, hidden, cot, pre_own, emb_own, w_query, w_key, w_value, w_out
    )
    thrice, conv_give, out_give = lax.optimization_barrier((thrice, conv_give, out_give))
    wgrad = (wgrad.astype(F32) + thrice.astype(F32)).astype(BF)
    wgrads = lax.all_gather(wgrad, SEQ, axis=0)
    conv_taken = lax.ppermute(conv_give, "core", SWAP)
    share = (conv_keep.astype(F32) + conv_taken.astype(F32)).astype(BF)
    parts = to_chips(share, ALL_CHIPS).reshape(64, HALF // 64, C)
    share = jnp.sum(parts.astype(F32), axis=0).astype(BF)
    conv_mine = to_chips(jnp.broadcast_to(share[None], (64, HALF // 64, C)), ALL_CHIPS).reshape(HALF, C)
    grad_conv = unpack_conv(info, conv_mine, lax.ppermute(conv_mine, "core", SWAP))

    grad_out, grad_query, grad_key, grad_value = unpack_weights(wgrads)
    taken = lax.ppermute(out_give, "core", SWAP)
    mixed = (out_keep.astype(F32) + taken.astype(F32)).astype(BF)[None]
    return (mixed, grad_conv, grad_query, grad_key, grad_value, grad_out)


def solution(mesh):
    split = jax.sharding.Mesh(mesh.devices.reshape(8, 8, 2), ("dp", "chip", "core"))
    in_specs = (P("dp", SEQ), P("dp"), P(), P(), P(), P(), P(), P(), P("dp", SEQ, None))
    out_specs = (P("dp", SEQ, None), P(), P(), P(), P(), P())
    return jax.shard_map(body, mesh=split, in_specs=in_specs, out_specs=out_specs, check_vma=False)
```

time: 269 us -> 206 us (0.77)
  blocking collectives: 105 us -> 43.3 us
  Pallas kernels: 107 us -> 85.1 us
  starting transfers between devices: 16.8 us -> 28.8 us
  waiting for transfers between devices: 7.5 us -> 17.8 us
    all_to_all x6 -> x2, blocking collectives: 105 us -> 43.3 us  [to_chips(): return lax.all_to_all(x, axes, 0, 0, tiled=True)]
    pallas_call x3 -> x2, Pallas kernels: 70.3 us -> 51.7 us  [heads(): pl.pallas_call(functools.partial(heads_kernel, last), out_shape=(jax.Shap...]
    all_to_all x1 -> x3, starting transfers between devices: 7.84 us -> 16.4 us  [to_chips(): return lax.all_to_all(x, axes, 0, 0, tiled=True)]
    ppermute x0 -> x3, waiting for transfers between devices: none -> 8.52 us  [the longest x1 6.04 us: body(): twice = lax.ppermute(wgrad, 'dp', apart('dp', 2))]
    ppermute x0 -> x3, starting transfers between devices: none -> 6.77 us  [the longest x1 2.88 us: body(): thrice = lax.ppermute(wgrad, 'dp', apart('dp', 4))]
    pallas_call x1, Pallas kernels: 17.9 us -> 13.9 us  [front(): pl.pallas_call(front_kernel, out_shape=(jax.ShapeDtypeStruct((BINS, C), B...]
  transfers between devices with their start and end apart: 8 -> 13, of which waited for: 3 -> 6; matrix products, arithmetic and copies ran while one was open for 4% -> 5% of each run, Pallas kernels for 34% -> 38%
where the time goes in v4:
time: 206 us; the launch traced here: 205 us
  Pallas kernels  85.1 us (41%)
  blocking collectives  43.3 us (21%)
  starting transfers between devices  28.8 us (14%)
  waiting for transfers between devices  17.8 us (9%)
  between operations  14.9 us (7%)
  other arithmetic  7.33 us (4%)
  local copies, waits for them, and re-layouts  6.08 us (3%)
    pallas_call x2, Pallas kernels, heads(): pl.pallas_call(functools.partial(heads_kernel, last), out_shape=(jax.Shap...  51.7 us
    all_to_all x2, blocking collectives, to_chips(): return lax.all_to_all(x, axes, 0, 0, tiled=True)  43.3 us
    all_to_all x3, starting transfers between devices, to_chips(): return lax.all_to_all(x, axes, 0, 0, tiled=True)  16.4 us
    pallas_call x1, Pallas kernels, front(): pl.pallas_call(front_kernel, out_shape=(jax.ShapeDtypeStruct((BINS, C), B...  13.9 us
    pallas_call x1, Pallas kernels, tail(): pl.pallas_call(tail_kernel, out_shape=outs, grid_spec=pltpu.PrefetchScala...  8.11 us
    pallas_call x1, Pallas kernels, unpack_weights(): pl.pallas_call(unpack_weights_kernel, out_shape=[jax.ShapeDtypeStruct((C,...  6.29 us
    ppermute x1, waiting for transfers between devices, body(): twice = lax.ppermute(wgrad, 'dp', apart('dp', 2))  6.04 us
    pallas_call x1, Pallas kernels, unpack_conv(): pl.pallas_call(unpack_conv_kernel, out_shape=jax.ShapeDtypeStruct((KW, G,...  5.07 us
  transfers between devices with their start and end apart: 13, of which 6 were waited for; matrix products, arithmetic and copies ran while one was open for 5% of the time, Pallas kernels for 38%

profile of v4, /device:TPU:1, one launch (start us, length us, event | category | flops | bytes accessed | tf_op | source)
XLA Modules:
  0.0 205.0 jit_solution(4802224860519773951)
XLA Ops:
  7.2 1.0 convert_reduce_fusion
  8.2 1.7 convolution_convert_fusion
  9.9 0.1 broadcast_in_dim.6
  10.0 0.0 copy-start.1
  10.1 0.9 pad_maximum_fusion.1
  11.0 7.8 %all-to-all-start = ((bf16[16,176,128]{2,1,0:T(8,128)(2,1)}), bf16[16,176,128]{2,1,0:T(8,128)(2,1)}, u32[]{:S(2)}, u32[]{:S(2)}) async-start(bf16[16,176,128]{2,1,0:T(8,128)(2,1)} %pad_maximum_fusion.1), calls=%async_computation | async-start | bytes 1441792 | tf_op jit(solution)/shard_map/all_to_all | solution.py:420
  18.8 0.0 all-gather.4.cloned.1.call-start
  18.9 0.0 copy-done.1
  18.9 1.0 slice_bitcast_fusion.3
  20.5 1.1 constant_dynamic-slice_fusion.2
  21.6 0.7 pad_add_fusion.info
  22.3 1.2 pad.27
  23.5 0.1 pad.24
  23.6 0.2 pad.25
  23.8 0.1 pad.26
  23.9 1.3 constant_dynamic-slice_fusion
  25.2 0.9 fusion.6.w_qkv
  26.2 1.8 pad_maximum_fusion.conv
  28.0 3.2 %all-to-all-done.pieces = bf16[16,176,128]{2,1,0:T(8,128)(2,1)} async-done(((bf16[16,176,128]{2,1,0:T(8,128)(2,1)}), bf16[16,176,128]{2,1,0:T(8,128)(2,1)}, u32[]{:S(2)}, u32[]{:S(2)}) %all-to-all-start) | async-done | bytes 720928 | tf_op jit(solution)/shard_map/all_to_all | solution.py:420
  31.2 0.0 all-gather.4.cloned.1.call-update
  31.2 13.9 %front.1 = (bf16[2048,768]{1,0:T(8,128)(2,1)}, f32[256,768]{1,0:T(8,128)}, f32[6,320,128]{2,1,0:T(8,128)}) custom-call(s32[3]{0:T(128)} %pad_add_fusion.info, bf16[16,176,128]{2,1,0:T(8,128)(2,1)} %all-to-all-done.pieces, bf16[512,768]{1,0:T(8,128)(2,1)} %w_stem.1, bf16[4,1280,256]{2,1,0:T(8,128)(2,1)} %pad_maximum_fusion.conv), custom_call_target="tpu_custom_call" | custom-call | flops 20000000000 | bytes 10000000 | tf_op jit(solution)/shard_map/front/pallas_call | solution.py:118
  45.1 0.9 collective-permute-start
  46.0 25.2 %heads.2 = (bf16[8,192,256]{2,1,0:T(8,128)(2,1)}, f32[144,768]{1,0:T(8,128)}) custom-call(bf16[2048,768]{1,0:T(8,128)(2,1)} %get-tuple-element.37.hidden, bf16[16,176,128]{2,1,0:T(8,128)(2,1)} %all-to-all-done.pieces, bf16[768,384]{1,0:T(8,128)(2,1)} %fusion.6.w_qkv), custom_call_target="tpu_custom_call" | custom-call | flops 30000001024 | bytes 10000000 | tf_op jit(solution)/shard_map/heads/pallas_call | solution.py:265
  71.1 3.8 %all-to-all-start.1 = ((bf16[8,192,256]{2,1,0:T(8,128)(2,1)}), bf16[8,192,256]{2,1,0:T(8,128)(2,1)S(1)}, u32[]{:S(2)}, u32[]{:S(2)}) async-start(bf16[8,192,256]{2,1,0:T(8,128)(2,1)} %get-tuple-element.40.refs_1_), calls=%async_computation.1 | async-start | bytes 1572864 | tf_op jit(solution)/shard_map/all_to_all | solution.py:420
  74.9 0.0 collective-permute-done.hidden
  74.9 0.0 all-gather.4.cloned.1.call-done.refs_0_.cot
  75.0 26.5 %heads.3 = (bf16[8,192,256]{2,1,0:T(8,128)(2,1)}, bf16[192,768]{1,0:T(8,128)(2,1)}) custom-call(bf16[2048,768]{1,0:T(8,128)(2,1)} %collective-permute-done.hidden, bf16[16,176,128]{2,1,0:T(8,128)(2,1)} %all-to-all-done.pieces, bf16[768,384]{1,0:T(8,128)(2,1)} %fusion.6.w_qkv, bf16[2048,768]{1,0:T(8,128)(2,1)} %all-gather.4.cloned.1.call-done.refs_0_.cot, ...), custom_call_target="tpu_custom_call" | custom-call | flops 30000001024 | bytes 10000000 | tf_op jit(solution)/shard_map/heads/pallas_call | solution.py:265
  101.5 0.0 all-to-all-done.1.got_same
  101.5 0.1 collective-permute-start.3
  101.6 2.6 %collective-permute-start.1 = (bf16[192,768]{1,0:T(8,128)(2,1)}, bf16[192,768]{1,0:T(8,128)(2,1)S(1)}, u32[]{:S(2)}, u32[]{:S(2)}) collective-permute-start(bf16[192,768]{1,0:T(8,128)(2,1)} %get-tuple-element.45), channel_id=1, source_target_pairs={{0,16},{16,0},{32,48},{48,32},{64,80},{80,64},{96,112},{112,96},{1... | collective-permute-start | bytes 884744 | tf_op jit(solution)/shard_map/ppermute | solution.py:456
  104.2 0.0 collective-permute-done.3
  104.2 4.8 %all-to-all-start.2 = ((bf16[8,192,256]{2,1,0:T(8,128)(2,1)}), bf16[8,192,256]{2,1,0:T(8,128)(2,1)S(1)}, u32[]{:S(2)}, u32[]{:S(2)}) async-start(bf16[8,192,256]{2,1,0:T(8,128)(2,1)} %collective-permute-done.3), calls=%async_computation.2 | async-start | bytes 1572864 | tf_op jit(solution)/shard_map/all_to_all | solution.py:420
  109.0 0.0 all-gather.6.cloned.1.call-start
  109.1 2.5 %collective-permute-done.1 = bf16[192,768]{1,0:T(8,128)(2,1)S(1)} collective-permute-done((bf16[192,768]{1,0:T(8,128)(2,1)}, bf16[192,768]{1,0:T(8,128)(2,1)S(1)}, u32[]{:S(2)}, u32[]{:S(2)}) %collective-permute-start.1) | collective-permute-done | bytes 294944 | tf_op jit(solution)/shard_map/ppermute | solution.py:456
  111.6 0.0 copy-done.6
  111.6 0.1 add_convert_fusion.3
  111.6 1.3 collective-permute-start.2
  112.9 6.0 %collective-permute-done.2 = bf16[192,768]{1,0:T(8,128)(2,1)S(1)} collective-permute-done((bf16[192,768]{1,0:T(8,128)(2,1)S(1)}, bf16[192,768]{1,0:T(8,128)(2,1)S(1)}, u32[]{:S(2)}, u32[]{:S(2)}) %collective-permute-start.2) | collective-permute-done | bytes 294944 | tf_op jit(solution)/shard_map/ppermute | solution.py:458
  119.0 1.6 all-to-all-done.2.got_cross
  120.5 0.1 add_convert_fusion.2
  120.6 0.0 copy-done.2
  120.6 2.9 %collective-permute-start.4 = (bf16[192,768]{1,0:T(8,128)(2,1)S(1)}, bf16[192,768]{1,0:T(8,128)(2,1)S(1)}, u32[]{:S(2)}, u32[]{:S(2)}) collective-permute-start(bf16[192,768]{1,0:T(8,128)(2,1)S(1)} %add_convert_fusion.2), channel_id=1, source_target_pairs={{0,64},{16,80},{32,96},{48,112},{64,0},{80,16},{96,32},{112,48},{1... | collective-permute-start | bytes 884744 | tf_op jit(solution)/shard_map/ppermute | solution.py:461
  123.5 0.0 copy-done.3
  123.5 8.1 %tail.1 = (bf16[128,768]{1,0:T(8,128)(2,1)}, bf16[128,768]{1,0:T(8,128)(2,1)}, bf16[512,768]{1,0:T(8,128)(2,1)}, bf16[512,768]{1,0:T(8,128)(2,1)}) custom-call(s32[3]{0:T(128)} %pad_add_fusion.info, bf16[8,192,256]{2,1,0:T(8,128)(2,1)} %copy-done.2, bf16[8,192,256]{2,1,0:T(8,128)(2,1)} %copy-done.3, bf16[2048,768]{1,0:T(8,128)(2,1)} %get-tuple-element.37.hidden, ...), custom_call_target="tpu_custom_call" | custom-call | flops 5000000000 | bytes 10000000 | tf_op jit(solution)/shard_map/tail/pallas_call | solution.py:345
  131.6 0.0 collective-permute-done.4
  131.6 0.8 add_convert_fusion.1
  132.4 0.0 all-gather.6.cloned.1.call-update
  132.4 2.1 %collective-permute-start.6 = (bf16[512,768]{1,0:T(8,128)(2,1)}, bf16[512,768]{1,0:T(8,128)(2,1)S(1)}, u32[]{:S(2)}, u32[]{:S(2)}) collective-permute-start(bf16[512,768]{1,0:T(8,128)(2,1)} %get-tuple-element.56), channel_id=1, source_target_pairs={{0,1},{1,0},{2,3},{3,2},{4,5},{5,4},{6,7},{7,6},{8,9},{9,8},{10,11... | collective-permute-start | bytes 2359304 | tf_op jit(solution)/shard_map/ppermute | solution.py:468
  134.6 2.1 %collective-permute-done.6 = bf16[512,768]{1,0:T(8,128)(2,1)S(1)} collective-permute-done((bf16[512,768]{1,0:T(8,128)(2,1)}, bf16[512,768]{1,0:T(8,128)(2,1)S(1)}, u32[]{:S(2)}, u32[]{:S(2)}) %collective-permute-start.6) | collective-permute-done | bytes 786464 | tf_op jit(solution)/shard_map/ppermute | solution.py:468
  136.7 0.0 copy-done.4
  136.7 0.2 fusion.4
  136.9 21.6 %all_to_all.29 = bf16[64,8,768]{2,1,0:T(8,128)(2,1)S(1)} all-to-all(bf16[64,8,768]{2,1,0:T(8,128)(2,1)S(1)} %fusion.4), channel_id=1, replica_groups=mesh['dp'=8,'chip'=8,'core'=2] {'dp','chip'}, dimensions={0} | all-to-all | bytes 1572864 | tf_op jit(solution)/shard_map/all_to_all | solution.py:420
  158.4 0.1 reduce_sum.12
  158.6 0.1 broadcast_in_dim.16
  158.6 21.8 %all_to_all.30 = bf16[64,8,768]{2,1,0:T(8,128)(2,1)S(1)} all-to-all(bf16[64,8,768]{2,1,0:T(8,128)(2,1)S(1)} %broadcast_in_dim.16), channel_id=1, replica_groups=mesh['dp'=8,'chip'=8,'core'=2] {'dp','chip'}, dimensions={0} | all-to-all | bytes 1572864 | tf_op jit(solution)/shard_map/all_to_all | solution.py:420
  180.4 2.4 %collective-permute-start.7 = (bf16[512,768]{1,0:T(8,128)(2,1)S(1)}, bf16[512,768]{1,0:T(8,128)(2,1)S(1)}, u32[]{:S(2)}, u32[]{:S(2)}) collective-permute-start(bf16[512,768]{1,0:T(8,128)(2,1)S(1)} %bitcast.32), channel_id=1, source_target_pairs={{0,1},{1,0},{2,3},{3,2},{4,5},{5,4},{6,7},{7,6},{8,9},{9,8},{10,11... | collective-permute-start | bytes 2359304 | tf_op jit(solution)/shard_map/ppermute | solution.py:473
  182.8 0.0 copy-done.8
  182.8 0.1 collective-permute-start.5
  182.9 2.3 %collective-permute-done.5 = bf16[128,768]{1,0:T(8,128)(2,1)S(1)} collective-permute-done((bf16[128,768]{1,0:T(8,128)(2,1)S(1)}, bf16[128,768]{1,0:T(8,128)(2,1)S(1)}, u32[]{:S(2)}, u32[]{:S(2)}) %collective-permute-start.5) | collective-permute-done | bytes 196640 | tf_op jit(solution)/shard_map/ppermute | solution.py:476
  185.2 0.7 fusion.7
  186.0 0.0 collective-permute-done.7.other
  186.0 0.9 copy-done.5
  186.8 5.1 %unpack_conv.1 = f32[5,4,192,192]{3,2,1,0:T(8,128)} custom-call(s32[3]{0:T(128)} %pad_add_fusion.info, bf16[512,768]{1,0:T(8,128)(2,1)} %bitcast.33, bf16[512,768]{1,0:T(8,128)(2,1)} %copy-done.5), custom_call_target="tpu_custom_call" | custom-call | flops 10000000 | bytes 5000000 | tf_op jit(solution)/shard_map/unpack_conv/pallas_call | solution.py:397
  191.9 6.3 %unpack_weights.1 = (f32[768,768]{1,0:T(8,128)}, f32[768,768]{1,0:T(8,128)}, f32[768,768]{1,0:T(8,128)}, f32[768,768]{1,0:T(8,128)}) custom-call(bf16[16,192,768]{2,1,0:T(8,128)(2,1)} %bitcast.31), custom_call_target="tpu_custom_call" | custom-call | flops 10000000 | bytes 14000000 | tf_op jit(solution)/shard_map/unpack_weights/pallas_call | solution.py:370
  (11 shorter events, 0.0 us)
Async XLA Ops:
  10.0 8.8 %copy-start.1 = (bf16[5,4,192,192]{3,2,1,0:T(8,128)(2,1)S(1)}, bf16[5,4,192,192]{3,2,1,0:T(8,128)(2,1)}, u32[]{:S(2)}) copy-start(bf16[5,4,192,192]{3,2,1,0:T(8,128)(2,1)} %param.12) | copy-start | bytes 4423684
  11.0 20.2 %all-to-all-start = ((bf16[16,176,128]{2,1,0:T(8,128)(2,1)}), bf16[16,176,128]{2,1,0:T(8,128)(2,1)}, u32[]{:S(2)}, u32[]{:S(2)}) async-start(bf16[16,176,128]{2,1,0:T(8,128)(2,1)} %pad_maximum_fusion.1), calls=%async_computation | async-start | bytes 1441792 | tf_op jit(solution)/shard_map/all_to_all | solution.py:420
  18.8 56.1 %all-gather.4.cloned.1.call-start = ((), (), s32[]{:S(2)}) async-start(), calls=%async_computation.5 | async-start | bytes 3342336 | tf_op jit(solution)/shard_map/all_gather | solution.py:448
  45.1 29.8 %collective-permute-start = (bf16[2048,768]{1,0:T(8,128)(2,1)}, bf16[2048,768]{1,0:T(8,128)(2,1)}, u32[]{:S(2)}, u32[]{:S(2)}) collective-permute-start(bf16[2048,768]{1,0:T(8,128)(2,1)} %get-tuple-element.37.hidden), channel_id=1, source_target_pairs={{0,1},{1,0},{2,3},{3,2},{4,5},{5,4},{6,7},{7,6},{8,9},{9,8},{10,11... | collective-permute-start | bytes 9437192 | tf_op jit(solution)/shard_map/ppermute | solution.py:450
  71.1 30.3 %all-to-all-start.1 = ((bf16[8,192,256]{2,1,0:T(8,128)(2,1)}), bf16[8,192,256]{2,1,0:T(8,128)(2,1)S(1)}, u32[]{:S(2)}, u32[]{:S(2)}) async-start(bf16[8,192,256]{2,1,0:T(8,128)(2,1)} %get-tuple-element.40.refs_1_), calls=%async_computation.1 | async-start | bytes 1572864 | tf_op jit(solution)/shard_map/all_to_all | solution.py:420
  101.5 10.1 %copy-start.6 = (bf16[192,768]{1,0:T(8,128)(2,1)S(1)}, bf16[192,768]{1,0:T(8,128)(2,1)}, u32[]{:S(2)}) copy-start(bf16[192,768]{1,0:T(8,128)(2,1)} %get-tuple-element.45) | copy-start | bytes 884740
  101.5 19.1 %copy-start.2 = (bf16[8,192,256]{2,1,0:T(8,128)(2,1)}, bf16[8,192,256]{2,1,0:T(8,128)(2,1)S(1)}, u32[]{:S(2)}) copy-start(bf16[8,192,256]{2,1,0:T(8,128)(2,1)S(1)} %all-to-all-done.1.got_same) | copy-start | bytes 2359300
  101.5 2.7 %collective-permute-start.3 = (bf16[8,192,256]{2,1,0:T(8,128)(2,1)}, bf16[8,192,256]{2,1,0:T(8,128)(2,1)}, u32[]{:S(2)}, u32[]{:S(2)}) collective-permute-start(bf16[8,192,256]{2,1,0:T(8,128)(2,1)} %get-tuple-element.46), channel_id=1, source_target_pairs={{0,1},{1,0},{2,3},{3,2},{4,5},{5,4},{6,7},{7,6},{8,9},{9,8},{10,11... | collective-permute-start | bytes 2359304 | tf_op jit(solution)/shard_map/ppermute | solution.py:455
  101.6 10.0 %collective-permute-start.1 = (bf16[192,768]{1,0:T(8,128)(2,1)}, bf16[192,768]{1,0:T(8,128)(2,1)S(1)}, u32[]{:S(2)}, u32[]{:S(2)}) collective-permute-start(bf16[192,768]{1,0:T(8,128)(2,1)} %get-tuple-element.45), channel_id=1, source_target_pairs={{0,16},{16,0},{32,48},{48,32},{64,80},{80,64},{96,112},{112,96},{1... | collective-permute-start | bytes 884744 | tf_op jit(solution)/shard_map/ppermute | solution.py:456
  104.2 16.3 %all-to-all-start.2 = ((bf16[8,192,256]{2,1,0:T(8,128)(2,1)}), bf16[8,192,256]{2,1,0:T(8,128)(2,1)S(1)}, u32[]{:S(2)}, u32[]{:S(2)}) async-start(bf16[8,192,256]{2,1,0:T(8,128)(2,1)} %collective-permute-done.3), calls=%async_computation.2 | async-start | bytes 1572864 | tf_op jit(solution)/shard_map/all_to_all | solution.py:420
  109.0 82.9 %all-gather.6.cloned.1.call-start = ((), (), s32[]{:S(2)}) async-start(), calls=%async_computation.6 | async-start | bytes 5013504 | tf_op jit(solution)/shard_map/all_gather | solution.py:467
  111.6 7.3 %collective-permute-start.2 = (bf16[192,768]{1,0:T(8,128)(2,1)S(1)}, bf16[192,768]{1,0:T(8,128)(2,1)S(1)}, u32[]{:S(2)}, u32[]{:S(2)}) collective-permute-start(bf16[192,768]{1,0:T(8,128)(2,1)S(1)} %add_convert_fusion.3), channel_id=1, source_target_pairs={{0,32},{16,48},{32,0},{48,16},{64,96},{80,112},{96,64},{112,80},{1... | collective-permute-start | bytes 884744 | tf_op jit(solution)/shard_map/ppermute | solution.py:458
  120.5 3.0 %copy-start.3 = (bf16[8,192,256]{2,1,0:T(8,128)(2,1)}, bf16[8,192,256]{2,1,0:T(8,128)(2,1)S(1)}, u32[]{:S(2)}) copy-start(bf16[8,192,256]{2,1,0:T(8,128)(2,1)S(1)} %all-to-all-done.2.got_cross) | copy-start | bytes 2359300
  120.6 11.0 %collective-permute-start.4 = (bf16[192,768]{1,0:T(8,128)(2,1)S(1)}, bf16[192,768]{1,0:T(8,128)(2,1)S(1)}, u32[]{:S(2)}, u32[]{:S(2)}) collective-permute-start(bf16[192,768]{1,0:T(8,128)(2,1)S(1)} %add_convert_fusion.2), channel_id=1, source_target_pairs={{0,64},{16,80},{32,96},{48,112},{64,0},{80,16},{96,32},{112,48},{1... | collective-permute-start | bytes 884744 | tf_op jit(solution)/shard_map/ppermute | solution.py:461
  131.6 5.1 %copy-start.4 = (bf16[512,768]{1,0:T(8,128)(2,1)S(1)}, bf16[512,768]{1,0:T(8,128)(2,1)}, u32[]{:S(2)}) copy-start(bf16[512,768]{1,0:T(8,128)(2,1)} %get-tuple-element.55) | copy-start | bytes 2359300
  132.4 4.2 %collective-permute-start.6 = (bf16[512,768]{1,0:T(8,128)(2,1)}, bf16[512,768]{1,0:T(8,128)(2,1)S(1)}, u32[]{:S(2)}, u32[]{:S(2)}) collective-permute-start(bf16[512,768]{1,0:T(8,128)(2,1)} %get-tuple-element.56), channel_id=1, source_target_pairs={{0,1},{1,0},{2,3},{3,2},{4,5},{5,4},{6,7},{7,6},{8,9},{9,8},{10,11... | collective-permute-start | bytes 2359304 | tf_op jit(solution)/shard_map/ppermute | solution.py:468
  158.4 24.4 %copy-start.8 = (bf16[128,768]{1,0:T(8,128)(2,1)S(1)}, bf16[128,768]{1,0:T(8,128)(2,1)}, u32[]{:S(2)}) copy-start(bf16[128,768]{1,0:T(8,128)(2,1)} %get-tuple-element.54) | copy-start | bytes 589828
  158.4 26.8 %copy-start.7 = (bf16[128,768]{1,0:T(8,128)(2,1)S(1)}, bf16[128,768]{1,0:T(8,128)(2,1)}, u32[]{:S(2)}) copy-start(bf16[128,768]{1,0:T(8,128)(2,1)} %get-tuple-element.50) | copy-start | bytes 589828
  180.4 5.6 %copy-start = (bf16[64,8,768]{2,1,0:T(8,128)(2,1)}, bf16[64,8,768]{2,1,0:T(8,128)(2,1)S(1)}, u32[]{:S(2)}) copy-start(bf16[64,8,768]{2,1,0:T(8,128)(2,1)S(1)} %all_to_all.30) | copy-start | bytes 2359300
  180.4 5.5 %collective-permute-start.7 = (bf16[512,768]{1,0:T(8,128)(2,1)S(1)}, bf16[512,768]{1,0:T(8,128)(2,1)S(1)}, u32[]{:S(2)}, u32[]{:S(2)}) collective-permute-start(bf16[512,768]{1,0:T(8,128)(2,1)S(1)} %bitcast.32), channel_id=1, source_target_pairs={{0,1},{1,0},{2,3},{3,2},{4,5},{5,4},{6,7},{7,6},{8,9},{9,8},{10,11... | collective-permute-start | bytes 2359304 | tf_op jit(solution)/shard_map/ppermute | solution.py:473
  182.8 2.4 %collective-permute-start.5 = (bf16[128,768]{1,0:T(8,128)(2,1)S(1)}, bf16[128,768]{1,0:T(8,128)(2,1)S(1)}, u32[]{:S(2)}, u32[]{:S(2)}) collective-permute-start(bf16[128,768]{1,0:T(8,128)(2,1)S(1)} %copy-done.8), channel_id=1, source_target_pairs={{0,1},{1,0},{2,3},{3,2},{4,5},{5,4},{6,7},{7,6},{8,9},{9,8},{10,11... | collective-permute-start | bytes 589832 | tf_op jit(solution)/shard_map/ppermute | solution.py:476
  186.0 0.9 copy-start.5
Sparse Core Ops, SparseCore 0:
  31.3 35.6 all-gather.3
  132.5 54.7 all-gather.5

commit v5 on v4

--- a/solution.py
+++ b/solution.py
@@ -47,6 +47,10 @@
 
 def smem():
     return pl.BlockSpec(memory_space=pltpu.SMEM)
+
+
+def hbm():
+    return pl.BlockSpec(memory_space=pl.ANY)
 
 
 def params(**extra):
@@ -154,20 +158,22 @@
         out, wgrad = refs[:2]
     q_pad, k_nat, v_nat, q_t, k_t, v_t, ga_t, x_t, scores, both, kv_sum = refs[5 if last else 2 :]
 
+    span_rows = 1024
+
     def project(block, carry):
-        rows = pl.ds(pl.multiple_of(block * ROWS, ROWS), ROWS)
-        y = mm(hidden[rows, :], w_qkv[...]).astype(BF)
-        q_pad[rows, :] = y[:, 0:128]
-        k_nat[rows, :] = y[:, 128 : 128 + HD]
-        v_nat[rows, :] = y[:, 256 : 256 + HD]
-        turned = y.astype(F32).T
-        q_t[:, rows] = turned[0:HD].astype(BF)
-        k_t[:, rows] = turned[128 : 128 + HD].astype(BF)
-        v_t[:, rows] = turned[256 : 256 + HD].astype(BF)
-        ga_t[:, rows] = jnp.concatenate([pieces[2 * block, BP:, :], pieces[2 * block + 1, BP:, :]], axis=1)
+        rows = pl.ds(pl.multiple_of(block * span_rows, span_rows), span_rows)
+        y = mm(hidden[rows, :], w_qkv[...])
+        q_pad[rows, :] = y[:, 0:128].astype(BF)
+        k_nat[rows, :] = y[:, 128 : 128 + HD].astype(BF)
+        v_nat[rows, :] = y[:, 256 : 256 + HD].astype(BF)
+        for at, turned in ((0, q_t), (128, k_t), (256, v_t)):
+            turned[:, rows] = y[:, at : at + 128].T[0:HD].astype(BF)
+        for piece in range(span_rows // BP):
+            lanes = pl.ds(pl.multiple_of(block * span_rows + piece * BP, BP), BP)
+            ga_t[:, lanes] = pieces[(span_rows // BP) * block + piece, BP:, :]
         return carry
 
-    lax.fori_loop(0, BLOCKS, project, 0)
+    lax.fori_loop(0, BINS // span_rows, project, 0)
     kv_sum[...] = jnp.zeros_like(kv_sum)
 
     def span(block):
@@ -289,12 +295,24 @@
     )(hidden, pieces, w_qkv, *before)
 
 
-def tail_kernel(
-    info, got_same, got_cross, hidden, cot, pre, emb, w_query, w_key, w_value, w_out,
-    out_keep, out_give, conv_keep, conv_give, branch_out, conv_grad,
-):
+def tail_kernel(info, *refs):
+    sources, refs = refs[:10], refs[10:]
+    (out_keep, out_give, conv_keep, conv_give), refs = refs[:4], refs[4:]
+    held, (branch_out, conv_grad, arrive) = refs[:10], refs[10:]
+    got_same, got_cross, hidden, cot, w_out, w_query, w_key, w_value, pre, emb = held
     step = info[0]
     core = info[1]
+    chip = info[2]
+    loads = []
+    for at in range(10):
+        source = sources[at]
+        if at in (2, 3):
+            source = source.at[pl.ds(pl.multiple_of(chip * ROWS, ROWS), ROWS), :]
+        loads.append(pltpu.make_async_copy(source, held[at], arrive.at[at]))
+    for load in loads:
+        load.start()
+    loads[0].wait()
+    loads[1].wait()
     same, cross = got_same[...], got_cross[...]
     even = jnp.where(core == 0, same, cross)
     odd = jnp.where(core == 0, cross, same)
@@ -304,12 +322,17 @@
         part = jnp.concatenate([x[chip, at] for chip in range(H // 2) for x in (even, odd)], axis=0)
         return part.astype(F32).T.astype(BF)
 
+    for at in (2, 3, 4):
+        loads[at].wait()
     branch_out[...] = hidden[...].astype(F32) + mm(rows_of(0), w_out[...])
     out_keep[...] = branch_out[pl.ds(pl.multiple_of(core * BP, BP), BP), :].astype(BF)
     out_give[...] = branch_out[pl.ds(pl.multiple_of((1 - core) * BP, BP), BP), :].astype(BF)
-    grad = cot[...].astype(F32) + mm_nt(rows_of(1), w_query[...])
-    grad = grad + mm_nt(rows_of(2), w_key[...])
-    grad = grad + mm_nt(rows_of(3), w_value[...])
+    grad = cot[...].astype(F32)
+    for which, weight in ((1, w_query), (2, w_key), (3, w_value)):
+        loads[4 + which].wait()
+        grad = grad + mm_nt(rows_of(which), weight[...])
+    loads[8].wait()
+    loads[9].wait()
     x = pre[...]
     square = x * x
     th = jnp.tanh(GELU_A * (x + GELU_B * (square * x)))
@@ -336,71 +359,84 @@
     conv_give[...] = conv_grad[pl.ds(pl.multiple_of((1 - core) * HALF, HALF), HALF), :].astype(BF)
 
 
-def tail(info, got_same, got_cross, hidden, cot, pre, emb, w_query, w_key, w_value, w_out):
-    def whole(x):
-        return pl.BlockSpec(x.shape, lambda i, info: (0,) * x.ndim)
-
-    own = pl.BlockSpec((ROWS, C), lambda i, info: (info[2], 0))
+def tail(info, got_same, got_cross, hidden, cot, w_out, w_query, w_key, w_value, pre, emb):
+    operands = (got_same, got_cross, hidden, cot, w_out, w_query, w_key, w_value, pre, emb)
     outs = [jax.ShapeDtypeStruct(s, BF) for s in ((BP, C), (BP, C), (HALF, C), (HALF, C))]
+    held = [
+        pltpu.VMEM((ROWS, C) if at in (2, 3) else x.shape, x.dtype) for at, x in enumerate(operands)
+    ]
     return pl.pallas_call(
         tail_kernel,
         out_shape=outs,
-        grid_spec=pltpu.PrefetchScalarGridSpec(
-            num_scalar_prefetch=1,
-            grid=(1,),
-            in_specs=[whole(got_same), whole(got_cross), own, own]
-            + [whole(x) for x in (pre, emb, w_query, w_key, w_value, w_out)],
-            out_specs=[whole(x) for x in outs],
-            scratch_shapes=[pltpu.VMEM((ROWS, C), F32), pltpu.VMEM((2 * HALF, C), F32)],
-        ),
+        in_specs=[smem()] + [hbm()] * 10,
+        out_specs=[vmem()] * 4,
+        scratch_shapes=held
+        + [pltpu.VMEM((ROWS, C), F32), pltpu.VMEM((2 * HALF, C), F32), pltpu.SemaphoreType.DMA((10,))],
         compiler_params=params(),
         cost_estimate=pl.CostEstimate(flops=5 * 10**9, bytes_accessed=10**7, transcendentals=0),
         name="tail",
-    )(info, got_same, got_cross, hidden, cot, pre, emb, w_query, w_key, w_value, w_out)
-
-
-def unpack_weights_kernel(parts, *outs):
+    )(info, *operands)
+
+
+def unpack_weights_kernel(parts, *refs):
+    outs, held, full, arrive, leave = refs[:4], refs[4], refs[5], refs[6], refs[7]
+    loads = [
+        pltpu.make_async_copy(parts.at[:, which * HD : (which + 1) * HD, :], held.at[which], arrive.at[which])
+        for which in range(4)
+    ]
+    stores = [pltpu.make_async_copy(full.at[which], outs[which], leave.at[which]) for which in range(4)]
+    for load in loads:
+        load.start()
     for which in range(4):
-        part = parts[:, which * HD : (which + 1) * HD, :].reshape(C, 256).astype(F32)
-        outs[which][...] = part if which == 0 else part.T
+        loads[which].wait()
+        part = held[which].reshape(C, C).astype(F32)
+        full[which] = part if which == 0 else part.T
+        stores[which].start()
+    for store in stores:
+        store.wait()
 
 
 def unpack_weights(parts):
-    turned = pl.BlockSpec((256, C), lambda i: (i, 0))
     return pl.pallas_call(
         unpack_weights_kernel,
         out_shape=[jax.ShapeDtypeStruct((C, C), F32)] * 4,
-        grid=(C // 256,),
-        in_specs=[pl.BlockSpec((H, 4 * HD, 256), lambda i: (0, 0, i))],
-        out_specs=[pl.BlockSpec((C, 256), lambda i: (0, i)), turned, turned, turned],
+        in_specs=[hbm()],
+        out_specs=[hbm()] * 4,
+        scratch_shapes=[
+            pltpu.VMEM((4, H, HD, C), BF),
+            pltpu.VMEM((4, C, C), F32),
+            pltpu.SemaphoreType.DMA((4,)),
+            pltpu.SemaphoreType.DMA((4,)),
+        ],
         compiler_params=params(),
         cost_estimate=pl.CostEstimate(flops=10**7, bytes_accessed=14 * 10**6, transcendentals=0),
         name="unpack_weights",
     )(parts)
 
 
-def unpack_conv_kernel(info, mine, other, out, full):
+def unpack_conv_kernel(info, mine, other, out, full, turned, leave):
     core = info[1]
-    tap = pl.program_id(0)
-
-    @pl.when(tap == 0)
-    def _():
-        full[pl.ds(pl.multiple_of(core * HALF, HALF), HALF), :] = mine[...].astype(F32)
-        full[pl.ds(pl.multiple_of((1 - core) * HALF, HALF), HALF), :] = other[...].astype(F32)
-
-    rows = full[pl.ds(pl.multiple_of(tap * CG, 8), CG), :]
-    out[0] = rows.T.reshape(G, CG, CG)
+    full[pl.ds(pl.multiple_of(core * HALF, HALF), HALF), :] = mine[...].astype(F32)
+    full[pl.ds(pl.multiple_of((1 - core) * HALF, HALF), HALF), :] = other[...].astype(F32)
+    stores = [pltpu.make_async_copy(turned.at[tap], out.at[tap], leave.at[tap]) for tap in range(KW)]
+    for tap in range(KW):
+        turned[tap] = full[tap * CG : (tap + 1) * CG, :].T.reshape(G, CG, CG)
+        stores[tap].start()
+    for store in stores:
+        store.wait()
 
 
 def unpack_conv(info, mine, other):
-    half = pl.BlockSpec((HALF, C), lambda i: (0, 0))
     return pl.pallas_call(
         unpack_conv_kernel,
         out_shape=jax.ShapeDtypeStruct((KW, G, CG, CG), F32),
-        grid=(KW,),
-        in_specs=[smem(), half, half],
-        out_specs=pl.BlockSpec((1, G, CG, CG), lambda i: (i, 0, 0, 0)),
-        scratch_shapes=[pltpu.VMEM((2 * HALF, C), F32)],
+        in_specs=[smem(), vmem(), vmem()],
+        out_specs=hbm(),
+        scratch_shapes=[
+            pltpu.VMEM((2 * HALF, C), F32),
+            pltpu.VMEM((KW, G, CG, CG), F32),
+            pltpu.SemaphoreType.DMA((KW,)),
+        ],
         compiler_params=params(),
         cost_estimate=pl.CostEstimate(flops=10**7, bytes_accessed=5 * 10**6, transcendentals=0),
         name="unpack_conv",
@@ -460,7 +496,7 @@
     wgrad = (wgrad.astype(F32) + twice.astype(F32)).astype(BF)
     thrice = lax.ppermute(wgrad, "dp", apart("dp", 4))
     out_keep, out_give, conv_keep, conv_give = tail(
-        info, got_same, got_cross, hidden, cot, pre_own, emb_own, w_query, w_key, w_value, w_out
+        info, got_same, got_cross, hidden, cot, w_out, w_query, w_key, w_value, pre_own, emb_own
     )
     thrice, conv_give, out_give = lax.optimization_barrier((thrice, conv_give, out_give))
     wgrad = (wgrad.astype(F32) + thrice.astype(F32)).astype(BF)
@@ -470,11 +506,11 @@
     parts = to_chips(share, ALL_CHIPS).reshape(64, HALF // 64, C)
     share = jnp.sum(parts.astype(F32), axis=0).astype(BF)
     conv_mine = to_chips(jnp.broadcast_to(share[None], (64, HALF // 64, C)), ALL_CHIPS).reshape(HALF, C)
-    grad_conv = unpack_conv(info, conv_mine, lax.ppermute(conv_mine, "core", SWAP))
-
-    grad_out, grad_query, grad_key, grad_value = unpack_weights(wgrads)
     taken = lax.ppermute(out_give, "core", SWAP)
     mixed = (out_keep.astype(F32) + taken.astype(F32)).astype(BF)[None]
+    conv_mine, mixed = lax.optimization_barrier((conv_mine, mixed))
+    grad_conv = unpack_conv(info, conv_mine, lax.ppermute(conv_mine, "core", SWAP))
+    grad_out, grad_query, grad_key, grad_value = unpack_weights(wgrads)
     return (mixed, grad_conv, grad_query, grad_key, grad_value, grad_out)
 
 

time: 206 us -> 201 us (0.976)
  blocking collectives: 43.3 us -> 22.2 us
  waiting for transfers between devices: 17.8 us -> 30.2 us
  starting transfers between devices: 28.8 us -> 37.2 us
  Pallas kernels: 85.1 us -> 79.7 us
    all_to_all x2 -> x1, blocking collectives: 43.3 us -> 22.2 us  [to_chips(): return lax.all_to_all(x, axes, 0, 0, tiled=True)]
    all_to_all x3 -> x4, waiting for transfers between devices: 4.76 us -> 16.3 us  [to_chips(): return lax.all_to_all(x, axes, 0, 0, tiled=True)]
    all_to_all x3 -> x4, starting transfers between devices: 16.4 us -> 23.8 us  [to_chips(): return lax.all_to_all(x, axes, 0, 0, tiled=True)]
    pallas_call x2, Pallas kernels: 51.7 us -> 49.2 us  [heads(): pl.pallas_call(functools.partial(heads_kernel, last), out_shape=(jax.Shap...]
  transfers between devices with their start and end apart: 13 -> 14, of which waited for: 6 -> 8; matrix products, arithmetic and copies ran while one was open for 5% -> 5% of each run, Pallas kernels for 38% -> 37%
where the time goes in v5:
time: 201 us; the launch traced here: 200 us
  Pallas kernels  79.7 us (40%)
  starting transfers between devices  37.2 us (19%)
  waiting for transfers between devices  30.2 us (15%)
  blocking collectives  22.2 us (11%)
  between operations  14.9 us (7%)
  other arithmetic  7.34 us (4%)
  local copies, waits for them, and re-layouts  6.96 us (3%)
    pallas_call x2, Pallas kernels, heads(): pl.pallas_call(functools.partial(heads_kernel, last), out_shape=(jax.Shap...  49.2 us
    all_to_all x4, starting transfers between devices, to_chips(): return lax.all_to_all(x, axes, 0, 0, tiled=True)  23.8 us
    all_to_all x1, blocking collectives, to_chips(): return lax.all_to_all(x, axes, 0, 0, tiled=True)  22.2 us
    all_to_all x4, waiting for transfers between devices, to_chips(): return lax.all_to_all(x, axes, 0, 0, tiled=True)  16.3 us
    pallas_call x1, Pallas kernels, front(): pl.pallas_call(front_kernel, out_shape=(jax.ShapeDtypeStruct((BINS, C), B...  13.8 us
    pallas_call x1, Pallas kernels, tail(): pl.pallas_call(tail_kernel, out_shape=outs, in_specs=[smem()] + [hbm()] *...  7.72 us
    ppermute x1, waiting for transfers between devices, body(): twice = lax.ppermute(wgrad, 'dp', apart('dp', 2))  6.04 us
    pallas_call x1, Pallas kernels, unpack_weights(): pl.pallas_call(unpack_weights_kernel, out_shape=[jax.ShapeDtypeStruct((C,...  5.16 us
  transfers between devices with their start and end apart: 14, of which 8 were waited for; matrix products, arithmetic and copies ran while one was open for 5% of the time, Pallas kernels for 37%

profile of v5, /device:TPU:1, one launch (start us, length us, event | category | flops | bytes accessed | tf_op | source)
XLA Modules:
  0.0 200.3 jit_solution(17864565649136199735)
XLA Ops:
  7.2 1.0 convert_reduce_fusion
  8.2 1.7 convolution_convert_fusion
  9.9 0.1 broadcast_in_dim.6
  10.0 0.0 copy-start.1
  10.1 0.9 pad_maximum_fusion.1
  11.0 7.8 %all-to-all-start = ((bf16[16,176,128]{2,1,0:T(8,128)(2,1)}), bf16[16,176,128]{2,1,0:T(8,128)(2,1)}, u32[]{:S(2)}, u32[]{:S(2)}) async-start(bf16[16,176,128]{2,1,0:T(8,128)(2,1)} %pad_maximum_fusion.1), calls=%async_computation | async-start | bytes 1441792 | tf_op jit(solution)/shard_map/all_to_all | solution.py:456
  18.8 0.0 all-gather.4.cloned.1.call-start
  18.9 0.0 copy-done.1
  18.9 1.0 slice_bitcast_fusion.3
  20.5 1.1 constant_dynamic-slice_fusion.2
  21.6 0.7 pad_add_fusion.info
  22.3 1.2 pad.27
  23.5 0.1 pad.24
  23.6 0.2 pad.25
  23.8 0.1 pad.26
  23.9 1.3 constant_dynamic-slice_fusion
  25.3 0.9 fusion.6.w_qkv
  26.2 1.8 pad_maximum_fusion.conv
  28.0 3.2 %all-to-all-done.pieces = bf16[16,176,128]{2,1,0:T(8,128)(2,1)} async-done(((bf16[16,176,128]{2,1,0:T(8,128)(2,1)}), bf16[16,176,128]{2,1,0:T(8,128)(2,1)}, u32[]{:S(2)}, u32[]{:S(2)}) %all-to-all-start) | async-done | bytes 720928 | tf_op jit(solution)/shard_map/all_to_all | solution.py:456
  31.2 0.0 all-gather.4.cloned.1.call-update
  31.2 13.8 %front.1 = (bf16[2048,768]{1,0:T(8,128)(2,1)}, f32[256,768]{1,0:T(8,128)}, f32[6,320,128]{2,1,0:T(8,128)}) custom-call(s32[3]{0:T(128)} %pad_add_fusion.info, bf16[16,176,128]{2,1,0:T(8,128)(2,1)} %all-to-all-done.pieces, bf16[512,768]{1,0:T(8,128)(2,1)} %w_stem.1, bf16[4,1280,256]{2,1,0:T(8,128)(2,1)} %pad_maximum_fusion.conv), custom_call_target="tpu_custom_call" | custom-call | flops 20000000000 | bytes 10000000 | tf_op jit(solution)/shard_map/front/pallas_call | solution.py:122
  45.0 0.9 collective-permute-start
  45.9 24.0 %heads.2 = (bf16[8,192,256]{2,1,0:T(8,128)(2,1)}, f32[144,768]{1,0:T(8,128)}) custom-call(bf16[2048,768]{1,0:T(8,128)(2,1)} %get-tuple-element.39.hidden.refs_2_, bf16[16,176,128]{2,1,0:T(8,128)(2,1)} %all-to-all-done.pieces, bf16[768,384]{1,0:T(8,128)(2,1)} %fusion.6.w_qkv), custom_call_target="tpu_custom_call" | custom-call | flops 30000001024 | bytes 10000000 | tf_op jit(solution)/shard_map/heads/pallas_call | solution.py:271
  69.9 3.8 %all-to-all-start.1 = ((bf16[8,192,256]{2,1,0:T(8,128)(2,1)}), bf16[8,192,256]{2,1,0:T(8,128)(2,1)S(1)}, u32[]{:S(2)}, u32[]{:S(2)}) async-start(bf16[8,192,256]{2,1,0:T(8,128)(2,1)} %get-tuple-element.42.refs_1_), calls=%async_computation.1 | async-start | bytes 1572864 | tf_op jit(solution)/shard_map/all_to_all | solution.py:456
  73.7 0.0 collective-permute-done.hidden
  73.7 0.0 all-gather.4.cloned.1.call-done.refs_0_.refs_3_
  73.7 25.3 %heads.3 = (bf16[8,192,256]{2,1,0:T(8,128)(2,1)}, bf16[192,768]{1,0:T(8,128)(2,1)}) custom-call(bf16[2048,768]{1,0:T(8,128)(2,1)} %collective-permute-done.hidden, bf16[16,176,128]{2,1,0:T(8,128)(2,1)} %all-to-all-done.pieces, bf16[768,384]{1,0:T(8,128)(2,1)} %fusion.6.w_qkv, bf16[2048,768]{1,0:T(8,128)(2,1)} %all-gather.4.cloned.1.call-done.refs_0_.refs_3_, ...), custom_call_target="tpu_custom_call" | custom-call | flops 30000001024 | bytes 10000000 | tf_op jit(solution)/shard_map/heads/pallas_call | solution.py:271
  99.0 0.0 all-to-all-done.1.refs_0_
  99.0 0.1 collective-permute-start.3
  99.1 2.6 %collective-permute-start.1 = (bf16[192,768]{1,0:T(8,128)(2,1)}, bf16[192,768]{1,0:T(8,128)(2,1)S(1)}, u32[]{:S(2)}, u32[]{:S(2)}) collective-permute-start(bf16[192,768]{1,0:T(8,128)(2,1)} %get-tuple-element.47), channel_id=1, source_target_pairs={{0,16},{16,0},{32,48},{48,32},{64,80},{80,64},{96,112},{112,96},{1... | collective-permute-start | bytes 884744 | tf_op jit(solution)/shard_map/ppermute | solution.py:492
  101.7 0.0 collective-permute-done.3
  101.7 4.8 %all-to-all-start.2 = ((bf16[8,192,256]{2,1,0:T(8,128)(2,1)}), bf16[8,192,256]{2,1,0:T(8,128)(2,1)S(1)}, u32[]{:S(2)}, u32[]{:S(2)}) async-start(bf16[8,192,256]{2,1,0:T(8,128)(2,1)} %collective-permute-done.3), calls=%async_computation.2 | async-start | bytes 1572864 | tf_op jit(solution)/shard_map/all_to_all | solution.py:456
  106.6 0.0 all-gather.6.cloned.1.call-start
  106.6 2.5 %collective-permute-done.1 = bf16[192,768]{1,0:T(8,128)(2,1)S(1)} collective-permute-done((bf16[192,768]{1,0:T(8,128)(2,1)}, bf16[192,768]{1,0:T(8,128)(2,1)S(1)}, u32[]{:S(2)}, u32[]{:S(2)}) %collective-permute-start.1) | collective-permute-done | bytes 294944 | tf_op jit(solution)/shard_map/ppermute | solution.py:492
  109.1 0.0 copy-done.6
  109.1 0.1 add_convert_fusion.3
  109.1 1.3 collective-permute-start.2
  110.4 6.0 %collective-permute-done.2 = bf16[192,768]{1,0:T(8,128)(2,1)S(1)} collective-permute-done((bf16[192,768]{1,0:T(8,128)(2,1)S(1)}, bf16[192,768]{1,0:T(8,128)(2,1)S(1)}, u32[]{:S(2)}, u32[]{:S(2)}) %collective-permute-start.2) | collective-permute-done | bytes 294944 | tf_op jit(solution)/shard_map/ppermute | solution.py:494
  116.5 1.6 all-to-all-done.2.refs_1_
  118.1 0.1 add_convert_fusion.2
  118.2 2.8 %collective-permute-start.4 = (bf16[192,768]{1,0:T(8,128)(2,1)S(1)}, bf16[192,768]{1,0:T(8,128)(2,1)S(1)}, u32[]{:S(2)}, u32[]{:S(2)}) collective-permute-start(bf16[192,768]{1,0:T(8,128)(2,1)S(1)} %add_convert_fusion.2), channel_id=1, source_target_pairs={{0,64},{16,80},{32,96},{48,112},{64,0},{80,16},{96,32},{112,48},{1... | collective-permute-start | bytes 884744 | tf_op jit(solution)/shard_map/ppermute | solution.py:497
  121.0 7.7 %tail.1 = (bf16[128,768]{1,0:T(8,128)(2,1)}, bf16[128,768]{1,0:T(8,128)(2,1)}, bf16[512,768]{1,0:T(8,128)(2,1)}, bf16[512,768]{1,0:T(8,128)(2,1)}) custom-call(s32[3]{0:T(128)} %pad_add_fusion.info, bf16[8,192,256]{2,1,0:T(8,128)(2,1)} %copy-done.2, bf16[8,192,256]{2,1,0:T(8,128)(2,1)} %copy-done.3, bf16[2048,768]{1,0:T(8,128)(2,1)} %get-tuple-element.39.hidden.refs_2_, ...), custom_call_target="tpu_custom_call" | custom-call | flops 5000000000 | bytes 10000000 | tf_op jit(solution)/shard_map/tail/pallas_call | solution.py:368
  128.7 0.0 collective-permute-done.4
  128.7 0.8 add_convert_fusion.1
  129.5 0.0 all-gather.6.cloned.1.call-update
  129.6 2.1 %collective-permute-start.5 = (bf16[512,768]{1,0:T(8,128)(2,1)}, bf16[512,768]{1,0:T(8,128)(2,1)S(1)}, u32[]{:S(2)}, u32[]{:S(2)}) collective-permute-start(bf16[512,768]{1,0:T(8,128)(2,1)} %get-tuple-element.56), channel_id=1, source_target_pairs={{0,1},{1,0},{2,3},{3,2},{4,5},{5,4},{6,7},{7,6},{8,9},{9,8},{10,11... | collective-permute-start | bytes 2359304 | tf_op jit(solution)/shard_map/ppermute | solution.py:504
  131.7 2.1 %collective-permute-done.5 = bf16[512,768]{1,0:T(8,128)(2,1)S(1)} collective-permute-done((bf16[512,768]{1,0:T(8,128)(2,1)}, bf16[512,768]{1,0:T(8,128)(2,1)S(1)}, u32[]{:S(2)}, u32[]{:S(2)}) %collective-permute-start.5) | collective-permute-done | bytes 786464 | tf_op jit(solution)/shard_map/ppermute | solution.py:504
  133.8 0.2 fusion.4
  134.0 22.2 %all_to_all.29 = bf16[64,8,768]{2,1,0:T(8,128)(2,1)S(1)} all-to-all(bf16[64,8,768]{2,1,0:T(8,128)(2,1)S(1)} %fusion.4), channel_id=1, replica_groups=mesh['dp'=8,'chip'=8,'core'=2] {'dp','chip'}, dimensions={0} | all-to-all | bytes 1572864 | tf_op jit(solution)/shard_map/all_to_all | solution.py:456
  156.2 0.1 reduce_sum.12
  156.4 0.9 broadcast_in_dim.7
  157.3 7.4 %all-to-all-start.4 = ((bf16[64,8,768]{2,1,0:T(8,128)(2,1)}), bf16[64,8,768]{2,1,0:T(8,128)(2,1)S(1)}, u32[]{:S(2)}, u32[]{:S(2)}) async-start(bf16[64,8,768]{2,1,0:T(8,128)(2,1)} %broadcast_in_dim.7), calls=%async_computation.4 | async-start | bytes 1572864 | tf_op jit(solution)/shard_map/all_to_all | solution.py:456
  164.7 0.9 collective-permute-start.6
  165.7 1.1 collective-permute-done.6
  166.8 0.0 copy-done.7
  166.8 0.7 fusion.7
  167.5 11.5 %all-to-all-done.4 = bf16[64,8,768]{2,1,0:T(8,128)(2,1)S(1)} async-done(((bf16[64,8,768]{2,1,0:T(8,128)(2,1)}), bf16[64,8,768]{2,1,0:T(8,128)(2,1)S(1)}, u32[]{:S(2)}, u32[]{:S(2)}) %all-to-all-start.4) | async-done | bytes 786464 | tf_op jit(solution)/shard_map/all_to_all | solution.py:456
  179.0 2.5 %collective-permute-start.7 = (bf16[512,768]{1,0:T(8,128)(2,1)S(1)}, bf16[512,768]{1,0:T(8,128)(2,1)S(1)}, u32[]{:S(2)}, u32[]{:S(2)}) collective-permute-start(bf16[512,768]{1,0:T(8,128)(2,1)S(1)} %bitcast.32), channel_id=1, source_target_pairs={{0,1},{1,0},{2,3},{3,2},{4,5},{5,4},{6,7},{7,6},{8,9},{9,8},{10,11... | collective-permute-start | bytes 2359304 | tf_op jit(solution)/shard_map/ppermute | solution.py:512
  181.5 2.0 %collective-permute-done.7.other = bf16[512,768]{1,0:T(8,128)(2,1)S(1)} collective-permute-done((bf16[512,768]{1,0:T(8,128)(2,1)S(1)}, bf16[512,768]{1,0:T(8,128)(2,1)S(1)}, u32[]{:S(2)}, u32[]{:S(2)}) %collective-permute-start.7) | collective-permute-done | bytes 786464 | tf_op jit(solution)/shard_map/ppermute | solution.py:512
  183.6 0.0 copy-done
  183.6 0.9 copy-done.5
  184.5 3.8 %unpack_conv.1 = f32[5,4,192,192]{3,2,1,0:T(8,128)} custom-call(s32[3]{0:T(128)} %pad_add_fusion.info, bf16[512,768]{1,0:T(8,128)(2,1)} %bitcast.33, bf16[512,768]{1,0:T(8,128)(2,1)} %copy-done.5), custom_call_target="tpu_custom_call" | custom-call | flops 10000000 | bytes 5000000 | tf_op jit(solution)/shard_map/unpack_conv/pallas_call | solution.py:430
  188.3 0.0 all-gather.6.cloned.1.call-done
  188.3 5.2 %unpack_weights.1 = (f32[768,768]{1,0:T(8,128)}, f32[768,768]{1,0:T(8,128)}, f32[768,768]{1,0:T(8,128)}, f32[768,768]{1,0:T(8,128)}) custom-call(bf16[16,192,768]{2,1,0:T(8,128)(2,1)} %bitcast.31), custom_call_target="tpu_custom_call" | custom-call | flops 10000000 | bytes 14000000 | tf_op jit(solution)/shard_map/unpack_weights/pallas_call | solution.py:400
  (12 shorter events, 0.0 us)
Async XLA Ops:
  10.0 8.8 %copy-start.1 = (bf16[5,4,192,192]{3,2,1,0:T(8,128)(2,1)S(1)}, bf16[5,4,192,192]{3,2,1,0:T(8,128)(2,1)}, u32[]{:S(2)}) copy-start(bf16[5,4,192,192]{3,2,1,0:T(8,128)(2,1)} %param.12) | copy-start | bytes 4423684
  11.0 20.2 %all-to-all-start = ((bf16[16,176,128]{2,1,0:T(8,128)(2,1)}), bf16[16,176,128]{2,1,0:T(8,128)(2,1)}, u32[]{:S(2)}, u32[]{:S(2)}) async-start(bf16[16,176,128]{2,1,0:T(8,128)(2,1)} %pad_maximum_fusion.1), calls=%async_computation | async-start | bytes 1441792 | tf_op jit(solution)/shard_map/all_to_all | solution.py:456
  18.8 54.9 %all-gather.4.cloned.1.call-start = ((), (), s32[]{:S(2)}) async-start(), calls=%async_computation.5 | async-start | bytes 3342336 | tf_op jit(solution)/shard_map/all_gather | solution.py:484
  45.0 28.6 %collective-permute-start = (bf16[2048,768]{1,0:T(8,128)(2,1)}, bf16[2048,768]{1,0:T(8,128)(2,1)}, u32[]{:S(2)}, u32[]{:S(2)}) collective-permute-start(bf16[2048,768]{1,0:T(8,128)(2,1)} %get-tuple-element.39.hidden.refs_2_), channel_id=1, source_target_pairs={{0,1},{1,0},{2,3},{3,2},{4,5},{5,4},{6,7},{7,6},{8,9},{9,8},{10,11... | collective-permute-start | bytes 9437192 | tf_op jit(solution)/shard_map/ppermute | solution.py:486
  69.9 29.1 %all-to-all-start.1 = ((bf16[8,192,256]{2,1,0:T(8,128)(2,1)}), bf16[8,192,256]{2,1,0:T(8,128)(2,1)S(1)}, u32[]{:S(2)}, u32[]{:S(2)}) async-start(bf16[8,192,256]{2,1,0:T(8,128)(2,1)} %get-tuple-element.42.refs_1_), calls=%async_computation.1 | async-start | bytes 1572864 | tf_op jit(solution)/shard_map/all_to_all | solution.py:456
  99.0 10.1 %copy-start.6 = (bf16[192,768]{1,0:T(8,128)(2,1)S(1)}, bf16[192,768]{1,0:T(8,128)(2,1)}, u32[]{:S(2)}) copy-start(bf16[192,768]{1,0:T(8,128)(2,1)} %get-tuple-element.47) | copy-start | bytes 884740
  99.0 19.1 %copy-start.2 = (bf16[8,192,256]{2,1,0:T(8,128)(2,1)}, bf16[8,192,256]{2,1,0:T(8,128)(2,1)S(1)}, u32[]{:S(2)}) copy-start(bf16[8,192,256]{2,1,0:T(8,128)(2,1)S(1)} %all-to-all-done.1.refs_0_) | copy-start | bytes 2359300
  99.0 2.7 %collective-permute-start.3 = (bf16[8,192,256]{2,1,0:T(8,128)(2,1)}, bf16[8,192,256]{2,1,0:T(8,128)(2,1)}, u32[]{:S(2)}, u32[]{:S(2)}) collective-permute-start(bf16[8,192,256]{2,1,0:T(8,128)(2,1)} %get-tuple-element.48), channel_id=1, source_target_pairs={{0,1},{1,0},{2,3},{3,2},{4,5},{5,4},{6,7},{7,6},{8,9},{9,8},{10,11... | collective-permute-start | bytes 2359304 | tf_op jit(solution)/shard_map/ppermute | solution.py:491
  99.1 10.0 %collective-permute-start.1 = (bf16[192,768]{1,0:T(8,128)(2,1)}, bf16[192,768]{1,0:T(8,128)(2,1)S(1)}, u32[]{:S(2)}, u32[]{:S(2)}) collective-permute-start(bf16[192,768]{1,0:T(8,128)(2,1)} %get-tuple-element.47), channel_id=1, source_target_pairs={{0,16},{16,0},{32,48},{48,32},{64,80},{80,64},{96,112},{112,96},{1... | collective-permute-start | bytes 884744 | tf_op jit(solution)/shard_map/ppermute | solution.py:492
  101.7 16.3 %all-to-all-start.2 = ((bf16[8,192,256]{2,1,0:T(8,128)(2,1)}), bf16[8,192,256]{2,1,0:T(8,128)(2,1)S(1)}, u32[]{:S(2)}, u32[]{:S(2)}) async-start(bf16[8,192,256]{2,1,0:T(8,128)(2,1)} %collective-permute-done.3), calls=%async_computation.2 | async-start | bytes 1572864 | tf_op jit(solution)/shard_map/all_to_all | solution.py:456
  106.6 81.7 %all-gather.6.cloned.1.call-start = ((), (), s32[]{:S(2)}) async-start(), calls=%async_computation.6 | async-start | bytes 5013504 | tf_op jit(solution)/shard_map/all_gather | solution.py:503
  109.1 7.3 %collective-permute-start.2 = (bf16[192,768]{1,0:T(8,128)(2,1)S(1)}, bf16[192,768]{1,0:T(8,128)(2,1)S(1)}, u32[]{:S(2)}, u32[]{:S(2)}) collective-permute-start(bf16[192,768]{1,0:T(8,128)(2,1)S(1)} %add_convert_fusion.3), channel_id=1, source_target_pairs={{0,32},{16,48},{32,0},{48,16},{64,96},{80,112},{96,64},{112,80},{1... | collective-permute-start | bytes 884744 | tf_op jit(solution)/shard_map/ppermute | solution.py:494
  118.1 2.9 %copy-start.3 = (bf16[8,192,256]{2,1,0:T(8,128)(2,1)}, bf16[8,192,256]{2,1,0:T(8,128)(2,1)S(1)}, u32[]{:S(2)}) copy-start(bf16[8,192,256]{2,1,0:T(8,128)(2,1)S(1)} %all-to-all-done.2.refs_1_) | copy-start | bytes 2359300
  118.2 10.6 %collective-permute-start.4 = (bf16[192,768]{1,0:T(8,128)(2,1)S(1)}, bf16[192,768]{1,0:T(8,128)(2,1)S(1)}, u32[]{:S(2)}, u32[]{:S(2)}) collective-permute-start(bf16[192,768]{1,0:T(8,128)(2,1)S(1)} %add_convert_fusion.2), channel_id=1, source_target_pairs={{0,64},{16,80},{32,96},{48,112},{64,0},{80,16},{96,32},{112,48},{1... | collective-permute-start | bytes 884744 | tf_op jit(solution)/shard_map/ppermute | solution.py:497
  128.7 5.1 %copy-start.4 = (bf16[512,768]{1,0:T(8,128)(2,1)S(1)}, bf16[512,768]{1,0:T(8,128)(2,1)}, u32[]{:S(2)}) copy-start(bf16[512,768]{1,0:T(8,128)(2,1)} %get-tuple-element.52) | copy-start | bytes 2359300
  129.6 4.3 %collective-permute-start.5 = (bf16[512,768]{1,0:T(8,128)(2,1)}, bf16[512,768]{1,0:T(8,128)(2,1)S(1)}, u32[]{:S(2)}, u32[]{:S(2)}) collective-permute-start(bf16[512,768]{1,0:T(8,128)(2,1)} %get-tuple-element.56), channel_id=1, source_target_pairs={{0,1},{1,0},{2,3},{3,2},{4,5},{5,4},{6,7},{7,6},{8,9},{9,8},{10,11... | collective-permute-start | bytes 2359304 | tf_op jit(solution)/shard_map/ppermute | solution.py:504
  156.2 8.5 %copy-start.8 = (bf16[128,768]{1,0:T(8,128)(2,1)S(1)}, bf16[128,768]{1,0:T(8,128)(2,1)}, u32[]{:S(2)}) copy-start(bf16[128,768]{1,0:T(8,128)(2,1)} %get-tuple-element.58) | copy-start | bytes 589828
  156.2 10.6 %copy-start.7 = (bf16[128,768]{1,0:T(8,128)(2,1)S(1)}, bf16[128,768]{1,0:T(8,128)(2,1)}, u32[]{:S(2)}) copy-start(bf16[128,768]{1,0:T(8,128)(2,1)} %get-tuple-element.57) | copy-start | bytes 589828
  157.3 21.8 %all-to-all-start.4 = ((bf16[64,8,768]{2,1,0:T(8,128)(2,1)}), bf16[64,8,768]{2,1,0:T(8,128)(2,1)S(1)}, u32[]{:S(2)}, u32[]{:S(2)}) async-start(bf16[64,8,768]{2,1,0:T(8,128)(2,1)} %broadcast_in_dim.7), calls=%async_computation.4 | async-start | bytes 1572864 | tf_op jit(solution)/shard_map/all_to_all | solution.py:456
  164.7 2.1 %collective-permute-start.6 = (bf16[128,768]{1,0:T(8,128)(2,1)S(1)}, bf16[128,768]{1,0:T(8,128)(2,1)S(1)}, u32[]{:S(2)}, u32[]{:S(2)}) collective-permute-start(bf16[128,768]{1,0:T(8,128)(2,1)S(1)} %copy-done.8), channel_id=1, source_target_pairs={{0,1},{1,0},{2,3},{3,2},{4,5},{5,4},{6,7},{7,6},{8,9},{9,8},{10,11... | collective-permute-start | bytes 589832 | tf_op jit(solution)/shard_map/ppermute | solution.py:509
  179.0 4.5 %copy-start = (bf16[64,8,768]{2,1,0:T(8,128)(2,1)}, bf16[64,8,768]{2,1,0:T(8,128)(2,1)S(1)}, u32[]{:S(2)}) copy-start(bf16[64,8,768]{2,1,0:T(8,128)(2,1)S(1)} %all-to-all-done.4) | copy-start | bytes 2359300
  179.0 4.5 %collective-permute-start.7 = (bf16[512,768]{1,0:T(8,128)(2,1)S(1)}, bf16[512,768]{1,0:T(8,128)(2,1)S(1)}, u32[]{:S(2)}, u32[]{:S(2)}) collective-permute-start(bf16[512,768]{1,0:T(8,128)(2,1)S(1)} %bitcast.32), channel_id=1, source_target_pairs={{0,1},{1,0},{2,3},{3,2},{4,5},{5,4},{6,7},{7,6},{8,9},{9,8},{10,11... | collective-permute-start | bytes 2359304 | tf_op jit(solution)/shard_map/ppermute | solution.py:512
  183.6 0.9 copy-start.5
Sparse Core Ops, SparseCore 0:
  31.3 35.6 all-gather.3
  129.7 54.8 all-gather.5

commit v6 on v5

--- a/solution.py
+++ b/solution.py
@@ -378,69 +378,54 @@
     )(info, *operands)
 
 
-def unpack_weights_kernel(parts, *refs):
-    outs, held, full, arrive, leave = refs[:4], refs[4], refs[5], refs[6], refs[7]
+def unpack_kernel(info, mine, other, parts, *refs):
+    conv_out, outs, refs = refs[0], refs[1:5], refs[5:]
+    halves, turned, held, full, arrive, leave = refs
+    core = info[1]
     loads = [
-        pltpu.make_async_copy(parts.at[:, which * HD : (which + 1) * HD, :], held.at[which], arrive.at[which])
-        for which in range(4)
+        pltpu.make_async_copy(mine, halves.at[core], arrive.at[4]),
+        pltpu.make_async_copy(other, halves.at[1 - core], arrive.at[5]),
     ]
-    stores = [pltpu.make_async_copy(full.at[which], outs[which], leave.at[which]) for which in range(4)]
+    for which in range(4):
+        at = slice(which * HD, (which + 1) * HD)
+        loads.append(pltpu.make_async_copy(parts.at[:, at, :], held.at[which], arrive.at[which]))
     for load in loads:
         load.start()
+    stores = [pltpu.make_async_copy(turned.at[tap], conv_out.at[tap], leave.at[4 + tap]) for tap in range(KW)]
+    stores += [pltpu.make_async_copy(full.at[which], outs[which], leave.at[which]) for which in range(4)]
+    loads[0].wait()
+    loads[1].wait()
+    rows = halves[...].reshape(2 * HALF, C)
+    for tap in range(KW):
+        turned[tap] = rows[tap * CG : (tap + 1) * CG, :].astype(F32).T.reshape(G, CG, CG)
+        stores[tap].start()
     for which in range(4):
-        loads[which].wait()
+        loads[2 + which].wait()
         part = held[which].reshape(C, C).astype(F32)
         full[which] = part if which == 0 else part.T
-        stores[which].start()
+        stores[KW + which].start()
     for store in stores:
         store.wait()
 
 
-def unpack_weights(parts):
+def unpack(info, mine, other, parts):
     return pl.pallas_call(
-        unpack_weights_kernel,
-        out_shape=[jax.ShapeDtypeStruct((C, C), F32)] * 4,
-        in_specs=[hbm()],
-        out_specs=[hbm()] * 4,
+        unpack_kernel,
+        out_shape=[jax.ShapeDtypeStruct((KW, G, CG, CG), F32)] + [jax.ShapeDtypeStruct((C, C), F32)] * 4,
+        in_specs=[smem()] + [hbm()] * 3,
+        out_specs=[hbm()] * 5,
         scratch_shapes=[
+            pltpu.VMEM((2, HALF, C), BF),
+            pltpu.VMEM((KW, G, CG, CG), F32),
             pltpu.VMEM((4, H, HD, C), BF),
             pltpu.VMEM((4, C, C), F32),
-            pltpu.SemaphoreType.DMA((4,)),
-            pltpu.SemaphoreType.DMA((4,)),
+            pltpu.SemaphoreType.DMA((6,)),
+            pltpu.SemaphoreType.DMA((4 + KW,)),
         ],
         compiler_params=params(),
-        cost_estimate=pl.CostEstimate(flops=10**7, bytes_accessed=14 * 10**6, transcendentals=0),
-        name="unpack_weights",
-    )(parts)
-
-
-def unpack_conv_kernel(info, mine, other, out, full, turned, leave):
-    core = info[1]
-    full[pl.ds(pl.multiple_of(core * HALF, HALF), HALF), :] = mine[...].astype(F32)
-    full[pl.ds(pl.multiple_of((1 - core) * HALF, HALF), HALF), :] = other[...].astype(F32)
-    stores = [pltpu.make_async_copy(turned.at[tap], out.at[tap], leave.at[tap]) for tap in range(KW)]
-    for tap in range(KW):
-        turned[tap] = full[tap * CG : (tap + 1) * CG, :].T.reshape(G, CG, CG)
-        stores[tap].start()
-    for store in stores:
-        store.wait()
-
-
-def unpack_conv(info, mine, other):
-    return pl.pallas_call(
-        unpack_conv_kernel,
-        out_shape=jax.ShapeDtypeStruct((KW, G, CG, CG), F32),
-        in_specs=[smem(), vmem(), vmem()],
-        out_specs=hbm(),
-        scratch_shapes=[
-            pltpu.VMEM((2 * HALF, C), F32),
-            pltpu.VMEM((KW, G, CG, CG), F32),
-            pltpu.SemaphoreType.DMA((KW,)),
-        ],
-        compiler_params=params(),
-        cost_estimate=pl.CostEstimate(flops=10**7, bytes_accessed=5 * 10**6, transcendentals=0),
-        name="unpack_conv",
-    )(info, mine, other)
+        cost_estimate=pl.CostEstimate(flops=10**7, bytes_accessed=20 * 10**6, transcendentals=0),
+        name="unpack",
+    )(info, mine, other, parts)
 
 
 SWAP = [(0, 1), (1, 0)]
@@ -509,8 +494,9 @@
     taken = lax.ppermute(out_give, "core", SWAP)
     mixed = (out_keep.astype(F32) + taken.astype(F32)).astype(BF)[None]
     conv_mine, mixed = lax.optimization_barrier((conv_mine, mixed))
-    grad_conv = unpack_conv(info, conv_mine, lax.ppermute(conv_mine, "core", SWAP))
-    grad_out, grad_query, grad_key, grad_value = unpack_weights(wgrads)
+    grad_conv, grad_out, grad_query, grad_key, grad_value = unpack(
+        info, conv_mine, lax.ppermute(conv_mine, "core", SWAP), wgrads
+    )
     return (mixed, grad_conv, grad_query, grad_key, grad_value, grad_out)
 
 

time: 201 us -> 199 us (0.990)
    pallas_call x2 -> x1, Pallas kernels: 8.98 us -> 7.24 us  [unpack(): pl.pallas_call(unpack_kernel, out_shape=[jax.ShapeDtypeStruct((KW, G, CG,...]
  transfers between devices with their start and end apart: 14 -> 14, of which waited for: 8 -> 9; matrix products, arithmetic and copies ran while one was open for 5% -> 5% of each run, Pallas kernels for 37% -> 36%
where the time goes in v6:
time: 199 us
  Pallas kernels  78 us (39%)
  starting transfers between devices  37.2 us (19%)
  waiting for transfers between devices  31.2 us (16%)
  blocking collectives  22.2 us (11%)
  between operations  14.9 us (7%)
  other arithmetic  7.34 us (4%)
  local copies, waits for them, and re-layouts  6.06 us (3%)
    pallas_call x2, Pallas kernels, heads(): pl.pallas_call(functools.partial(heads_kernel, last), out_shape=(jax.Shap...  49.3 us
    all_to_all x4, starting transfers between devices, to_chips(): return lax.all_to_all(x, axes, 0, 0, tiled=True)  23.7 us
    all_to_all x1, blocking collectives, to_chips(): return lax.all_to_all(x, axes, 0, 0, tiled=True)  22.2 us
    all_to_all x4, waiting for transfers between devices, to_chips(): return lax.all_to_all(x, axes, 0, 0, tiled=True)  16.3 us
    pallas_call x1, Pallas kernels, front(): pl.pallas_call(front_kernel, out_shape=(jax.ShapeDtypeStruct((BINS, C), B...  13.8 us
    pallas_call x1, Pallas kernels, tail(): pl.pallas_call(tail_kernel, out_shape=outs, in_specs=[smem()] + [hbm()] *...  7.73 us
    pallas_call x1, Pallas kernels, unpack(): pl.pallas_call(unpack_kernel, out_shape=[jax.ShapeDtypeStruct((KW, G, CG,...  7.24 us
    ppermute x1, waiting for transfers between devices, body(): twice = lax.ppermute(wgrad, 'dp', apart('dp', 2))  6.03 us
  transfers between devices with their start and end apart: 14, of which 9 were waited for; matrix products, arithmetic and copies ran while one was open for 5% of the time, Pallas kernels for 36%

profile of v6, /device:TPU:1, one launch (start us, length us, event | category | flops | bytes accessed | tf_op | source)
XLA Modules:
  0.0 198.7 jit_solution(16288907484207626878)
XLA Ops:
  7.2 1.0 convert_reduce_fusion
  8.2 1.7 convolution_convert_fusion
  9.9 0.1 broadcast_in_dim.6
  10.0 0.0 copy-start.1
  10.1 0.9 pad_maximum_fusion.1
  11.0 7.8 %all-to-all-start = ((bf16[16,176,128]{2,1,0:T(8,128)(2,1)}), bf16[16,176,128]{2,1,0:T(8,128)(2,1)}, u32[]{:S(2)}, u32[]{:S(2)}) async-start(bf16[16,176,128]{2,1,0:T(8,128)(2,1)} %pad_maximum_fusion.1), calls=%async_computation | async-start | bytes 1441792 | tf_op jit(solution)/shard_map/all_to_all | solution.py:441
  18.8 0.0 all-gather.4.cloned.1.call-start
  19.5 0.0 copy-done.1
  19.5 1.0 slice_bitcast_fusion.3
  20.5 1.1 constant_dynamic-slice_fusion.2
  21.6 0.7 pad_add_fusion.info
  22.3 1.1 pad.24
  23.4 0.2 pad.27
  23.6 0.1 pad.26
  23.7 0.2 pad.25
  23.9 1.3 constant_dynamic-slice_fusion
  25.2 0.9 fusion.6.w_qkv
  26.2 1.8 pad_maximum_fusion.conv
  28.0 3.2 %all-to-all-done.pieces = bf16[16,176,128]{2,1,0:T(8,128)(2,1)} async-done(((bf16[16,176,128]{2,1,0:T(8,128)(2,1)}), bf16[16,176,128]{2,1,0:T(8,128)(2,1)}, u32[]{:S(2)}, u32[]{:S(2)}) %all-to-all-start) | async-done | bytes 720928 | tf_op jit(solution)/shard_map/all_to_all | solution.py:441
  31.2 0.0 all-gather.4.cloned.1.call-update
  31.2 13.8 %front.1 = (bf16[2048,768]{1,0:T(8,128)(2,1)}, f32[256,768]{1,0:T(8,128)}, f32[6,320,128]{2,1,0:T(8,128)}) custom-call(s32[3]{0:T(128)} %pad_add_fusion.info, bf16[16,176,128]{2,1,0:T(8,128)(2,1)} %all-to-all-done.pieces, bf16[512,768]{1,0:T(8,128)(2,1)} %w_stem.1, bf16[4,1280,256]{2,1,0:T(8,128)(2,1)} %pad_maximum_fusion.conv), custom_call_target="tpu_custom_call" | custom-call | flops 20000000000 | bytes 10000000 | tf_op jit(solution)/shard_map/front/pallas_call | solution.py:122
  45.0 0.9 collective-permute-start
  45.9 24.0 %heads.2 = (bf16[8,192,256]{2,1,0:T(8,128)(2,1)}, f32[144,768]{1,0:T(8,128)}) custom-call(bf16[2048,768]{1,0:T(8,128)(2,1)} %get-tuple-element.40.hidden.refs_2_, bf16[16,176,128]{2,1,0:T(8,128)(2,1)} %all-to-all-done.pieces, bf16[768,384]{1,0:T(8,128)(2,1)} %fusion.6.w_qkv), custom_call_target="tpu_custom_call" | custom-call | flops 30000001024 | bytes 10000000 | tf_op jit(solution)/shard_map/heads/pallas_call | solution.py:271
  69.9 3.8 %all-to-all-start.1 = ((bf16[8,192,256]{2,1,0:T(8,128)(2,1)}), bf16[8,192,256]{2,1,0:T(8,128)(2,1)S(1)}, u32[]{:S(2)}, u32[]{:S(2)}) async-start(bf16[8,192,256]{2,1,0:T(8,128)(2,1)} %get-tuple-element.43.refs_1_), calls=%async_computation.1 | async-start | bytes 1572864 | tf_op jit(solution)/shard_map/all_to_all | solution.py:441
  73.7 0.0 collective-permute-done.hidden
  73.7 0.0 all-gather.4.cloned.1.call-done.refs_0_.refs_3_
  73.7 25.3 %heads.3 = (bf16[8,192,256]{2,1,0:T(8,128)(2,1)}, bf16[192,768]{1,0:T(8,128)(2,1)}) custom-call(bf16[2048,768]{1,0:T(8,128)(2,1)} %collective-permute-done.hidden, bf16[16,176,128]{2,1,0:T(8,128)(2,1)} %all-to-all-done.pieces, bf16[768,384]{1,0:T(8,128)(2,1)} %fusion.6.w_qkv, bf16[2048,768]{1,0:T(8,128)(2,1)} %all-gather.4.cloned.1.call-done.refs_0_.refs_3_, ...), custom_call_target="tpu_custom_call" | custom-call | flops 30000001024 | bytes 10000000 | tf_op jit(solution)/shard_map/heads/pallas_call | solution.py:271
  99.0 0.0 all-to-all-done.1.refs_0_
  99.0 0.1 collective-permute-start.3
  99.1 2.7 %collective-permute-start.1 = (bf16[192,768]{1,0:T(8,128)(2,1)}, bf16[192,768]{1,0:T(8,128)(2,1)S(1)}, u32[]{:S(2)}, u32[]{:S(2)}) collective-permute-start(bf16[192,768]{1,0:T(8,128)(2,1)} %get-tuple-element.48), channel_id=1, source_target_pairs={{0,16},{16,0},{32,48},{48,32},{64,80},{80,64},{96,112},{112,96},{1... | collective-permute-start | bytes 884744 | tf_op jit(solution)/shard_map/ppermute | solution.py:477
  101.8 0.0 collective-permute-done.3
  101.8 4.7 %all-to-all-start.2 = ((bf16[8,192,256]{2,1,0:T(8,128)(2,1)}), bf16[8,192,256]{2,1,0:T(8,128)(2,1)S(1)}, u32[]{:S(2)}, u32[]{:S(2)}) async-start(bf16[8,192,256]{2,1,0:T(8,128)(2,1)} %collective-permute-done.3), calls=%async_computation.2 | async-start | bytes 1572864 | tf_op jit(solution)/shard_map/all_to_all | solution.py:441
  106.5 0.0 all-gather.6.cloned.1.call-start
  106.6 2.5 %collective-permute-done.1 = bf16[192,768]{1,0:T(8,128)(2,1)S(1)} collective-permute-done((bf16[192,768]{1,0:T(8,128)(2,1)}, bf16[192,768]{1,0:T(8,128)(2,1)S(1)}, u32[]{:S(2)}, u32[]{:S(2)}) %collective-permute-start.1) | collective-permute-done | bytes 294944 | tf_op jit(solution)/shard_map/ppermute | solution.py:477
  109.1 0.0 copy-done.6
  109.1 0.1 add_convert_fusion.3
  109.1 1.3 collective-permute-start.2
  110.4 6.0 %collective-permute-done.2 = bf16[192,768]{1,0:T(8,128)(2,1)S(1)} collective-permute-done((bf16[192,768]{1,0:T(8,128)(2,1)S(1)}, bf16[192,768]{1,0:T(8,128)(2,1)S(1)}, u32[]{:S(2)}, u32[]{:S(2)}) %collective-permute-start.2) | collective-permute-done | bytes 294944 | tf_op jit(solution)/shard_map/ppermute | solution.py:479
  116.5 1.6 all-to-all-done.2.refs_1_
  118.1 0.1 add_convert_fusion.2
  118.1 0.0 copy-done.3
  118.2 2.8 %collective-permute-start.4 = (bf16[192,768]{1,0:T(8,128)(2,1)S(1)}, bf16[192,768]{1,0:T(8,128)(2,1)S(1)}, u32[]{:S(2)}, u32[]{:S(2)}) collective-permute-start(bf16[192,768]{1,0:T(8,128)(2,1)S(1)} %add_convert_fusion.2), channel_id=1, source_target_pairs={{0,64},{16,80},{32,96},{48,112},{64,0},{80,16},{96,32},{112,48},{1... | collective-permute-start | bytes 884744 | tf_op jit(solution)/shard_map/ppermute | solution.py:482
  121.0 7.7 %tail.1 = (bf16[128,768]{1,0:T(8,128)(2,1)}, bf16[128,768]{1,0:T(8,128)(2,1)}, bf16[512,768]{1,0:T(8,128)(2,1)}, bf16[512,768]{1,0:T(8,128)(2,1)}) custom-call(s32[3]{0:T(128)} %pad_add_fusion.info, bf16[8,192,256]{2,1,0:T(8,128)(2,1)} %copy-done.3, bf16[8,192,256]{2,1,0:T(8,128)(2,1)} %copy-done.4, bf16[2048,768]{1,0:T(8,128)(2,1)} %get-tuple-element.40.hidden.refs_2_, ...), custom_call_target="tpu_custom_call" | custom-call | flops 5000000000 | bytes 10000000 | tf_op jit(solution)/shard_map/tail/pallas_call | solution.py:368
  128.7 0.0 collective-permute-done.4
  128.7 0.8 add_convert_fusion.1
  129.5 0.0 all-gather.6.cloned.1.call-update
  129.6 2.1 %collective-permute-start.5 = (bf16[512,768]{1,0:T(8,128)(2,1)}, bf16[512,768]{1,0:T(8,128)(2,1)S(1)}, u32[]{:S(2)}, u32[]{:S(2)}) collective-permute-start(bf16[512,768]{1,0:T(8,128)(2,1)} %get-tuple-element.57), channel_id=1, source_target_pairs={{0,1},{1,0},{2,3},{3,2},{4,5},{5,4},{6,7},{7,6},{8,9},{9,8},{10,11... | collective-permute-start | bytes 2359304 | tf_op jit(solution)/shard_map/ppermute | solution.py:489
  131.7 2.1 %collective-permute-done.5 = bf16[512,768]{1,0:T(8,128)(2,1)S(1)} collective-permute-done((bf16[512,768]{1,0:T(8,128)(2,1)}, bf16[512,768]{1,0:T(8,128)(2,1)S(1)}, u32[]{:S(2)}, u32[]{:S(2)}) %collective-permute-start.5) | collective-permute-done | bytes 786464 | tf_op jit(solution)/shard_map/ppermute | solution.py:489
  133.8 0.2 fusion.4
  134.0 22.2 %all_to_all.29 = bf16[64,8,768]{2,1,0:T(8,128)(2,1)S(1)} all-to-all(bf16[64,8,768]{2,1,0:T(8,128)(2,1)S(1)} %fusion.4), channel_id=1, replica_groups=mesh['dp'=8,'chip'=8,'core'=2] {'dp','chip'}, dimensions={0} | all-to-all | bytes 1572864 | tf_op jit(solution)/shard_map/all_to_all | solution.py:441
  156.2 0.1 reduce_sum.12
  156.3 0.9 broadcast_in_dim.7
  157.3 7.4 %all-to-all-start.4 = ((bf16[64,8,768]{2,1,0:T(8,128)(2,1)}), bf16[64,8,768]{2,1,0:T(8,128)(2,1)S(1)}, u32[]{:S(2)}, u32[]{:S(2)}) async-start(bf16[64,8,768]{2,1,0:T(8,128)(2,1)} %broadcast_in_dim.7), calls=%async_computation.4 | async-start | bytes 1572864 | tf_op jit(solution)/shard_map/all_to_all | solution.py:441
  164.7 0.0 copy-done.8
  164.7 0.9 collective-permute-start.6
  165.6 1.1 collective-permute-done.6
  166.8 0.0 copy-done.7
  166.8 0.7 fusion.7
  167.5 11.5 %all-to-all-done.4 = bf16[64,8,768]{2,1,0:T(8,128)(2,1)S(1)} async-done(((bf16[64,8,768]{2,1,0:T(8,128)(2,1)}), bf16[64,8,768]{2,1,0:T(8,128)(2,1)S(1)}, u32[]{:S(2)}, u32[]{:S(2)}) %all-to-all-start.4) | async-done | bytes 786464 | tf_op jit(solution)/shard_map/all_to_all | solution.py:441
  179.0 2.5 %collective-permute-start.7 = (bf16[512,768]{1,0:T(8,128)(2,1)S(1)}, bf16[512,768]{1,0:T(8,128)(2,1)S(1)}, u32[]{:S(2)}, u32[]{:S(2)}) collective-permute-start(bf16[512,768]{1,0:T(8,128)(2,1)S(1)} %bitcast.32), channel_id=1, source_target_pairs={{0,1},{1,0},{2,3},{3,2},{4,5},{5,4},{6,7},{7,6},{8,9},{9,8},{10,11... | collective-permute-start | bytes 2359304 | tf_op jit(solution)/shard_map/ppermute | solution.py:498
  181.5 2.0 %collective-permute-done.7.other = bf16[512,768]{1,0:T(8,128)(2,1)S(1)} collective-permute-done((bf16[512,768]{1,0:T(8,128)(2,1)S(1)}, bf16[512,768]{1,0:T(8,128)(2,1)S(1)}, u32[]{:S(2)}, u32[]{:S(2)}) %collective-permute-start.7) | collective-permute-done | bytes 786464 | tf_op jit(solution)/shard_map/ppermute | solution.py:498
  183.6 1.0 all-gather.6.cloned.1.call-done
  184.6 0.0 copy-done.2
  184.6 7.2 %unpack.1 = (f32[5,4,192,192]{3,2,1,0:T(8,128)}, f32[768,768]{1,0:T(8,128)}, f32[768,768]{1,0:T(8,128)}, f32[768,768]{1,0:T(8,128)}, f32[768,768]{1,0:T(8,128)}) custom-call(s32[3]{0:T(128)} %pad_add_fusion.info, bf16[512,768]{1,0:T(8,128)(2,1)} %bitcast.33, bf16[512,768]{1,0:T(8,128)(2,1)} %copy-done.2, bf16[16,192,768]{2,1,0:T(8,128)(2,1)} %bitcast.31), custom_call_target="tpu_custom_call" | custom-call | flops 10000000 | bytes 20000000 | tf_op jit(solution)/shard_map/unpack/pallas_call | solution.py:412
  (11 shorter events, 0.0 us)
Async XLA Ops:
  10.0 9.5 %copy-start.1 = (bf16[5,4,192,192]{3,2,1,0:T(8,128)(2,1)S(1)}, bf16[5,4,192,192]{3,2,1,0:T(8,128)(2,1)}, u32[]{:S(2)}) copy-start(bf16[5,4,192,192]{3,2,1,0:T(8,128)(2,1)} %param.12) | copy-start | bytes 4423684
  11.0 20.2 %all-to-all-start = ((bf16[16,176,128]{2,1,0:T(8,128)(2,1)}), bf16[16,176,128]{2,1,0:T(8,128)(2,1)}, u32[]{:S(2)}, u32[]{:S(2)}) async-start(bf16[16,176,128]{2,1,0:T(8,128)(2,1)} %pad_maximum_fusion.1), calls=%async_computation | async-start | bytes 1441792 | tf_op jit(solution)/shard_map/all_to_all | solution.py:441
  18.8 54.9 %all-gather.4.cloned.1.call-start = ((), (), s32[]{:S(2)}) async-start(), calls=%async_computation.5 | async-start | bytes 3342336 | tf_op jit(solution)/shard_map/all_gather | solution.py:469
  45.0 28.6 %collective-permute-start = (bf16[2048,768]{1,0:T(8,128)(2,1)}, bf16[2048,768]{1,0:T(8,128)(2,1)}, u32[]{:S(2)}, u32[]{:S(2)}) collective-permute-start(bf16[2048,768]{1,0:T(8,128)(2,1)} %get-tuple-element.40.hidden.refs_2_), channel_id=1, source_target_pairs={{0,1},{1,0},{2,3},{3,2},{4,5},{5,4},{6,7},{7,6},{8,9},{9,8},{10,11... | collective-permute-start | bytes 9437192 | tf_op jit(solution)/shard_map/ppermute | solution.py:471
  69.9 29.1 %all-to-all-start.1 = ((bf16[8,192,256]{2,1,0:T(8,128)(2,1)}), bf16[8,192,256]{2,1,0:T(8,128)(2,1)S(1)}, u32[]{:S(2)}, u32[]{:S(2)}) async-start(bf16[8,192,256]{2,1,0:T(8,128)(2,1)} %get-tuple-element.43.refs_1_), calls=%async_computation.1 | async-start | bytes 1572864 | tf_op jit(solution)/shard_map/all_to_all | solution.py:441
  99.0 10.1 %copy-start.6 = (bf16[192,768]{1,0:T(8,128)(2,1)S(1)}, bf16[192,768]{1,0:T(8,128)(2,1)}, u32[]{:S(2)}) copy-start(bf16[192,768]{1,0:T(8,128)(2,1)} %get-tuple-element.48) | copy-start | bytes 884740
  99.0 19.2 %copy-start.3 = (bf16[8,192,256]{2,1,0:T(8,128)(2,1)}, bf16[8,192,256]{2,1,0:T(8,128)(2,1)S(1)}, u32[]{:S(2)}) copy-start(bf16[8,192,256]{2,1,0:T(8,128)(2,1)S(1)} %all-to-all-done.1.refs_0_) | copy-start | bytes 2359300
  99.0 2.8 %collective-permute-start.3 = (bf16[8,192,256]{2,1,0:T(8,128)(2,1)}, bf16[8,192,256]{2,1,0:T(8,128)(2,1)}, u32[]{:S(2)}, u32[]{:S(2)}) collective-permute-start(bf16[8,192,256]{2,1,0:T(8,128)(2,1)} %get-tuple-element.49), channel_id=1, source_target_pairs={{0,1},{1,0},{2,3},{3,2},{4,5},{5,4},{6,7},{7,6},{8,9},{9,8},{10,11... | collective-permute-start | bytes 2359304 | tf_op jit(solution)/shard_map/ppermute | solution.py:476
  99.1 10.0 %collective-permute-start.1 = (bf16[192,768]{1,0:T(8,128)(2,1)}, bf16[192,768]{1,0:T(8,128)(2,1)S(1)}, u32[]{:S(2)}, u32[]{:S(2)}) collective-permute-start(bf16[192,768]{1,0:T(8,128)(2,1)} %get-tuple-element.48), channel_id=1, source_target_pairs={{0,16},{16,0},{32,48},{48,32},{64,80},{80,64},{96,112},{112,96},{1... | collective-permute-start | bytes 884744 | tf_op jit(solution)/shard_map/ppermute | solution.py:477
  101.8 16.2 %all-to-all-start.2 = ((bf16[8,192,256]{2,1,0:T(8,128)(2,1)}), bf16[8,192,256]{2,1,0:T(8,128)(2,1)S(1)}, u32[]{:S(2)}, u32[]{:S(2)}) async-start(bf16[8,192,256]{2,1,0:T(8,128)(2,1)} %collective-permute-done.3), calls=%async_computation.2 | async-start | bytes 1572864 | tf_op jit(solution)/shard_map/all_to_all | solution.py:441
  106.5 78.0 %all-gather.6.cloned.1.call-start = ((), (), s32[]{:S(2)}) async-start(), calls=%async_computation.6 | async-start | bytes 5013504 | tf_op jit(solution)/shard_map/all_gather | solution.py:488
  109.1 7.3 %collective-permute-start.2 = (bf16[192,768]{1,0:T(8,128)(2,1)S(1)}, bf16[192,768]{1,0:T(8,128)(2,1)S(1)}, u32[]{:S(2)}, u32[]{:S(2)}) collective-permute-start(bf16[192,768]{1,0:T(8,128)(2,1)S(1)} %add_convert_fusion.3), channel_id=1, source_target_pairs={{0,32},{16,48},{32,0},{48,16},{64,96},{80,112},{96,64},{112,80},{1... | collective-permute-start | bytes 884744 | tf_op jit(solution)/shard_map/ppermute | solution.py:479
  118.1 2.9 %copy-start.4 = (bf16[8,192,256]{2,1,0:T(8,128)(2,1)}, bf16[8,192,256]{2,1,0:T(8,128)(2,1)S(1)}, u32[]{:S(2)}) copy-start(bf16[8,192,256]{2,1,0:T(8,128)(2,1)S(1)} %all-to-all-done.2.refs_1_) | copy-start | bytes 2359300
  118.2 10.6 %collective-permute-start.4 = (bf16[192,768]{1,0:T(8,128)(2,1)S(1)}, bf16[192,768]{1,0:T(8,128)(2,1)S(1)}, u32[]{:S(2)}, u32[]{:S(2)}) collective-permute-start(bf16[192,768]{1,0:T(8,128)(2,1)S(1)} %add_convert_fusion.2), channel_id=1, source_target_pairs={{0,64},{16,80},{32,96},{48,112},{64,0},{80,16},{96,32},{112,48},{1... | collective-permute-start | bytes 884744 | tf_op jit(solution)/shard_map/ppermute | solution.py:482
  128.7 5.1 %copy-start.5 = (bf16[512,768]{1,0:T(8,128)(2,1)S(1)}, bf16[512,768]{1,0:T(8,128)(2,1)}, u32[]{:S(2)}) copy-start(bf16[512,768]{1,0:T(8,128)(2,1)} %get-tuple-element.53) | copy-start | bytes 2359300
  129.6 4.2 %collective-permute-start.5 = (bf16[512,768]{1,0:T(8,128)(2,1)}, bf16[512,768]{1,0:T(8,128)(2,1)S(1)}, u32[]{:S(2)}, u32[]{:S(2)}) collective-permute-start(bf16[512,768]{1,0:T(8,128)(2,1)} %get-tuple-element.57), channel_id=1, source_target_pairs={{0,1},{1,0},{2,3},{3,2},{4,5},{5,4},{6,7},{7,6},{8,9},{9,8},{10,11... | collective-permute-start | bytes 2359304 | tf_op jit(solution)/shard_map/ppermute | solution.py:489
  156.2 8.5 %copy-start.8 = (bf16[128,768]{1,0:T(8,128)(2,1)S(1)}, bf16[128,768]{1,0:T(8,128)(2,1)}, u32[]{:S(2)}) copy-start(bf16[128,768]{1,0:T(8,128)(2,1)} %get-tuple-element.59) | copy-start | bytes 589828
  156.2 10.6 %copy-start.7 = (bf16[128,768]{1,0:T(8,128)(2,1)S(1)}, bf16[128,768]{1,0:T(8,128)(2,1)}, u32[]{:S(2)}) copy-start(bf16[128,768]{1,0:T(8,128)(2,1)} %get-tuple-element.58) | copy-start | bytes 589828
  157.3 21.8 %all-to-all-start.4 = ((bf16[64,8,768]{2,1,0:T(8,128)(2,1)}), bf16[64,8,768]{2,1,0:T(8,128)(2,1)S(1)}, u32[]{:S(2)}, u32[]{:S(2)}) async-start(bf16[64,8,768]{2,1,0:T(8,128)(2,1)} %broadcast_in_dim.7), calls=%async_computation.4 | async-start | bytes 1572864 | tf_op jit(solution)/shard_map/all_to_all | solution.py:441
  164.7 2.1 %collective-permute-start.6 = (bf16[128,768]{1,0:T(8,128)(2,1)S(1)}, bf16[128,768]{1,0:T(8,128)(2,1)S(1)}, u32[]{:S(2)}, u32[]{:S(2)}) collective-permute-start(bf16[128,768]{1,0:T(8,128)(2,1)S(1)} %copy-done.8), channel_id=1, source_target_pairs={{0,1},{1,0},{2,3},{3,2},{4,5},{5,4},{6,7},{7,6},{8,9},{9,8},{10,11... | collective-permute-start | bytes 589832 | tf_op jit(solution)/shard_map/ppermute | solution.py:494
  179.0 5.6 %copy-start = (bf16[64,8,768]{2,1,0:T(8,128)(2,1)}, bf16[64,8,768]{2,1,0:T(8,128)(2,1)S(1)}, u32[]{:S(2)}) copy-start(bf16[64,8,768]{2,1,0:T(8,128)(2,1)S(1)} %all-to-all-done.4) | copy-start | bytes 2359300
  179.0 4.5 %collective-permute-start.7 = (bf16[512,768]{1,0:T(8,128)(2,1)S(1)}, bf16[512,768]{1,0:T(8,128)(2,1)S(1)}, u32[]{:S(2)}, u32[]{:S(2)}) collective-permute-start(bf16[512,768]{1,0:T(8,128)(2,1)S(1)} %bitcast.32), channel_id=1, source_target_pairs={{0,1},{1,0},{2,3},{3,2},{4,5},{5,4},{6,7},{7,6},{8,9},{9,8},{10,11... | collective-permute-start | bytes 2359304 | tf_op jit(solution)/shard_map/ppermute | solution.py:498
  183.6 1.0 copy-start.2
Sparse Core Ops, SparseCore 0:
  31.3 35.6 all-gather.3
  129.7 54.8 all-gather.5

commit v7 on v6

--- a/solution.py
+++ b/solution.py
@@ -232,15 +232,15 @@
 
     def attend(pair, carry):
         a, b = 2 * pair, 2 * pair + 1
+        backward(1, jnp.maximum(b - 2, 0))
         inv = softmax(0)
-        backward(1, jnp.maximum(b - 2, 0))
+        products(1, b)
         dot = mix(0, a)
-        products(1, b)
         score_grads(0, inv, dot, a)
+        backward(0, a)
         inv = softmax(1)
-        backward(0, a)
+        products(0, jnp.minimum(b + 1, BLOCKS - 1))
         dot = mix(1, b)
-        products(0, jnp.minimum(b + 1, BLOCKS - 1))
         score_grads(1, inv, dot, b)
         return carry
 

time: 199 us -> 198 us (level)
  transfers between devices with their start and end apart: 14 -> 14, of which waited for: 9 -> 9; matrix products, arithmetic and copies ran while one was open for 5% -> 5% of each run, Pallas kernels for 36% -> 35%
where the time goes in v7:
time: 198 us
  Pallas kernels  76.8 us (39%)
  starting transfers between devices  37.2 us (19%)
  waiting for transfers between devices  31.3 us (16%)
  blocking collectives  22.2 us (11%)
  between operations  14.9 us (8%)
  other arithmetic  7.34 us (4%)
  local copies, waits for them, and re-layouts  6.06 us (3%)
    pallas_call x2, Pallas kernels, heads(): pl.pallas_call(functools.partial(heads_kernel, last), out_shape=(jax.Shap...  48.1 us
    all_to_all x4, starting transfers between devices, to_chips(): return lax.all_to_all(x, axes, 0, 0, tiled=True)  23.7 us
    all_to_all x1, blocking collectives, to_chips(): return lax.all_to_all(x, axes, 0, 0, tiled=True)  22.2 us
    all_to_all x4, waiting for transfers between devices, to_chips(): return lax.all_to_all(x, axes, 0, 0, tiled=True)  16.5 us
    pallas_call x1, Pallas kernels, front(): pl.pallas_call(front_kernel, out_shape=(jax.ShapeDtypeStruct((BINS, C), B...  13.8 us
    pallas_call x1, Pallas kernels, tail(): pl.pallas_call(tail_kernel, out_shape=outs, in_specs=[smem()] + [hbm()] *...  7.71 us
    pallas_call x1, Pallas kernels, unpack(): pl.pallas_call(unpack_kernel, out_shape=[jax.ShapeDtypeStruct((KW, G, CG,...  7.24 us
    ppermute x1, waiting for transfers between devices, body(): twice = lax.ppermute(wgrad, 'dp', apart('dp', 2))  5.96 us
  transfers between devices with their start and end apart: 14, of which 9 were waited for; matrix products, arithmetic and copies ran while one was open for 5% of the time, Pallas kernels for 35%

profile of v7, /device:TPU:1, one launch (start us, length us, event | category | flops | bytes accessed | tf_op | source)
XLA Modules:
  0.0 197.6 jit_solution(332150338958866009)
XLA Ops:
  7.2 1.0 convert_reduce_fusion
  8.2 1.7 convolution_convert_fusion
  9.9 0.1 broadcast_in_dim.6
  10.0 0.0 copy-start.1
  10.1 0.9 pad_maximum_fusion.1
  11.0 7.8 %all-to-all-start = ((bf16[16,176,128]{2,1,0:T(8,128)(2,1)}), bf16[16,176,128]{2,1,0:T(8,128)(2,1)}, u32[]{:S(2)}, u32[]{:S(2)}) async-start(bf16[16,176,128]{2,1,0:T(8,128)(2,1)} %pad_maximum_fusion.1), calls=%async_computation | async-start | bytes 1441792 | tf_op jit(solution)/shard_map/all_to_all | solution.py:441
  18.8 0.0 all-gather.4.cloned.1.call-start
  19.5 0.0 copy-done.1
  19.5 1.0 slice_bitcast_fusion.3
  20.5 1.1 constant_dynamic-slice_fusion.2
  21.6 0.7 pad_add_fusion.info
  22.3 1.1 pad.24
  23.4 0.2 pad.27
  23.6 0.1 pad.26
  23.7 0.2 pad.25
  23.9 1.3 constant_dynamic-slice_fusion
  25.2 0.9 fusion.6.w_qkv
  26.2 1.8 pad_maximum_fusion.conv
  28.0 3.2 %all-to-all-done.pieces = bf16[16,176,128]{2,1,0:T(8,128)(2,1)} async-done(((bf16[16,176,128]{2,1,0:T(8,128)(2,1)}), bf16[16,176,128]{2,1,0:T(8,128)(2,1)}, u32[]{:S(2)}, u32[]{:S(2)}) %all-to-all-start) | async-done | bytes 720928 | tf_op jit(solution)/shard_map/all_to_all | solution.py:441
  31.2 0.0 all-gather.4.cloned.1.call-update
  31.2 13.8 %front.1 = (bf16[2048,768]{1,0:T(8,128)(2,1)}, f32[256,768]{1,0:T(8,128)}, f32[6,320,128]{2,1,0:T(8,128)}) custom-call(s32[3]{0:T(128)} %pad_add_fusion.info, bf16[16,176,128]{2,1,0:T(8,128)(2,1)} %all-to-all-done.pieces, bf16[512,768]{1,0:T(8,128)(2,1)} %w_stem.1, bf16[4,1280,256]{2,1,0:T(8,128)(2,1)} %pad_maximum_fusion.conv), custom_call_target="tpu_custom_call" | custom-call | flops 20000000000 | bytes 10000000 | tf_op jit(solution)/shard_map/front/pallas_call | solution.py:122
  45.0 0.9 collective-permute-start
  45.9 23.4 %heads.2 = (bf16[8,192,256]{2,1,0:T(8,128)(2,1)}, f32[144,768]{1,0:T(8,128)}) custom-call(bf16[2048,768]{1,0:T(8,128)(2,1)} %get-tuple-element.40.hidden.refs_2_, bf16[16,176,128]{2,1,0:T(8,128)(2,1)} %all-to-all-done.pieces, bf16[768,384]{1,0:T(8,128)(2,1)} %fusion.6.w_qkv), custom_call_target="tpu_custom_call" | custom-call | flops 30000001024 | bytes 10000000 | tf_op jit(solution)/shard_map/heads/pallas_call | solution.py:271
  69.3 3.8 %all-to-all-start.1 = ((bf16[8,192,256]{2,1,0:T(8,128)(2,1)}), bf16[8,192,256]{2,1,0:T(8,128)(2,1)S(1)}, u32[]{:S(2)}, u32[]{:S(2)}) async-start(bf16[8,192,256]{2,1,0:T(8,128)(2,1)} %get-tuple-element.43.refs_1_), calls=%async_computation.1 | async-start | bytes 1572864 | tf_op jit(solution)/shard_map/all_to_all | solution.py:441
  73.1 0.0 collective-permute-done.hidden
  73.1 0.0 all-gather.4.cloned.1.call-done.refs_0_.refs_3_
  73.1 24.7 %heads.3 = (bf16[8,192,256]{2,1,0:T(8,128)(2,1)}, bf16[192,768]{1,0:T(8,128)(2,1)}) custom-call(bf16[2048,768]{1,0:T(8,128)(2,1)} %collective-permute-done.hidden, bf16[16,176,128]{2,1,0:T(8,128)(2,1)} %all-to-all-done.pieces, bf16[768,384]{1,0:T(8,128)(2,1)} %fusion.6.w_qkv, bf16[2048,768]{1,0:T(8,128)(2,1)} %all-gather.4.cloned.1.call-done.refs_0_.refs_3_, ...), custom_call_target="tpu_custom_call" | custom-call | flops 30000001024 | bytes 10000000 | tf_op jit(solution)/shard_map/heads/pallas_call | solution.py:271
  97.8 0.0 all-to-all-done.1.refs_0_
  97.8 0.1 collective-permute-start.3
  97.9 2.8 %collective-permute-start.1 = (bf16[192,768]{1,0:T(8,128)(2,1)}, bf16[192,768]{1,0:T(8,128)(2,1)S(1)}, u32[]{:S(2)}, u32[]{:S(2)}) collective-permute-start(bf16[192,768]{1,0:T(8,128)(2,1)} %get-tuple-element.48), channel_id=1, source_target_pairs={{0,16},{16,0},{32,48},{48,32},{64,80},{80,64},{96,112},{112,96},{1... | collective-permute-start | bytes 884744 | tf_op jit(solution)/shard_map/ppermute | solution.py:477
  100.7 0.0 collective-permute-done.3
  100.7 4.6 %all-to-all-start.2 = ((bf16[8,192,256]{2,1,0:T(8,128)(2,1)}), bf16[8,192,256]{2,1,0:T(8,128)(2,1)S(1)}, u32[]{:S(2)}, u32[]{:S(2)}) async-start(bf16[8,192,256]{2,1,0:T(8,128)(2,1)} %collective-permute-done.3), calls=%async_computation.2 | async-start | bytes 1572864 | tf_op jit(solution)/shard_map/all_to_all | solution.py:441
  105.4 0.0 all-gather.6.cloned.1.call-start
  105.4 2.5 %collective-permute-done.1 = bf16[192,768]{1,0:T(8,128)(2,1)S(1)} collective-permute-done((bf16[192,768]{1,0:T(8,128)(2,1)}, bf16[192,768]{1,0:T(8,128)(2,1)S(1)}, u32[]{:S(2)}, u32[]{:S(2)}) %collective-permute-start.1) | collective-permute-done | bytes 294944 | tf_op jit(solution)/shard_map/ppermute | solution.py:477
  107.9 0.0 copy-done.6
  107.9 0.1 add_convert_fusion.3
  108.0 1.4 collective-permute-start.2
  109.3 6.0 %collective-permute-done.2 = bf16[192,768]{1,0:T(8,128)(2,1)S(1)} collective-permute-done((bf16[192,768]{1,0:T(8,128)(2,1)S(1)}, bf16[192,768]{1,0:T(8,128)(2,1)S(1)}, u32[]{:S(2)}, u32[]{:S(2)}) %collective-permute-start.2) | collective-permute-done | bytes 294944 | tf_op jit(solution)/shard_map/ppermute | solution.py:479
  115.3 1.8 all-to-all-done.2.refs_1_
  117.0 0.1 add_convert_fusion.2
  117.1 0.0 copy-done.3
  117.1 2.8 %collective-permute-start.4 = (bf16[192,768]{1,0:T(8,128)(2,1)S(1)}, bf16[192,768]{1,0:T(8,128)(2,1)S(1)}, u32[]{:S(2)}, u32[]{:S(2)}) collective-permute-start(bf16[192,768]{1,0:T(8,128)(2,1)S(1)} %add_convert_fusion.2), channel_id=1, source_target_pairs={{0,64},{16,80},{32,96},{48,112},{64,0},{80,16},{96,32},{112,48},{1... | collective-permute-start | bytes 884744 | tf_op jit(solution)/shard_map/ppermute | solution.py:482
  119.9 0.0 copy-done.4
  119.9 7.7 %tail.1 = (bf16[128,768]{1,0:T(8,128)(2,1)}, bf16[128,768]{1,0:T(8,128)(2,1)}, bf16[512,768]{1,0:T(8,128)(2,1)}, bf16[512,768]{1,0:T(8,128)(2,1)}) custom-call(s32[3]{0:T(128)} %pad_add_fusion.info, bf16[8,192,256]{2,1,0:T(8,128)(2,1)} %copy-done.3, bf16[8,192,256]{2,1,0:T(8,128)(2,1)} %copy-done.4, bf16[2048,768]{1,0:T(8,128)(2,1)} %get-tuple-element.40.hidden.refs_2_, ...), custom_call_target="tpu_custom_call" | custom-call | flops 5000000000 | bytes 10000000 | tf_op jit(solution)/shard_map/tail/pallas_call | solution.py:368
  127.6 0.0 copy-start.5
  127.6 0.0 collective-permute-done.4
  127.7 0.8 add_convert_fusion.1
  128.4 0.0 all-gather.6.cloned.1.call-update
  128.5 2.1 %collective-permute-start.5 = (bf16[512,768]{1,0:T(8,128)(2,1)}, bf16[512,768]{1,0:T(8,128)(2,1)S(1)}, u32[]{:S(2)}, u32[]{:S(2)}) collective-permute-start(bf16[512,768]{1,0:T(8,128)(2,1)} %get-tuple-element.57), channel_id=1, source_target_pairs={{0,1},{1,0},{2,3},{3,2},{4,5},{5,4},{6,7},{7,6},{8,9},{9,8},{10,11... | collective-permute-start | bytes 2359304 | tf_op jit(solution)/shard_map/ppermute | solution.py:489
  130.6 2.1 %collective-permute-done.5 = bf16[512,768]{1,0:T(8,128)(2,1)S(1)} collective-permute-done((bf16[512,768]{1,0:T(8,128)(2,1)}, bf16[512,768]{1,0:T(8,128)(2,1)S(1)}, u32[]{:S(2)}, u32[]{:S(2)}) %collective-permute-start.5) | collective-permute-done | bytes 786464 | tf_op jit(solution)/shard_map/ppermute | solution.py:489
  132.7 0.0 copy-done.5
  132.7 0.2 fusion.4
  132.9 22.2 %all_to_all.29 = bf16[64,8,768]{2,1,0:T(8,128)(2,1)S(1)} all-to-all(bf16[64,8,768]{2,1,0:T(8,128)(2,1)S(1)} %fusion.4), channel_id=1, replica_groups=mesh['dp'=8,'chip'=8,'core'=2] {'dp','chip'}, dimensions={0} | all-to-all | bytes 1572864 | tf_op jit(solution)/shard_map/all_to_all | solution.py:441
  155.1 0.1 reduce_sum.12
  155.3 0.9 broadcast_in_dim.7
  156.2 7.4 %all-to-all-start.4 = ((bf16[64,8,768]{2,1,0:T(8,128)(2,1)}), bf16[64,8,768]{2,1,0:T(8,128)(2,1)S(1)}, u32[]{:S(2)}, u32[]{:S(2)}) async-start(bf16[64,8,768]{2,1,0:T(8,128)(2,1)} %broadcast_in_dim.7), calls=%async_computation.4 | async-start | bytes 1572864 | tf_op jit(solution)/shard_map/all_to_all | solution.py:441
  163.6 0.9 collective-permute-start.6
  164.6 1.1 collective-permute-done.6
  165.7 0.7 fusion.7
  166.4 11.5 %all-to-all-done.4 = bf16[64,8,768]{2,1,0:T(8,128)(2,1)S(1)} async-done(((bf16[64,8,768]{2,1,0:T(8,128)(2,1)}), bf16[64,8,768]{2,1,0:T(8,128)(2,1)S(1)}, u32[]{:S(2)}, u32[]{:S(2)}) %all-to-all-start.4) | async-done | bytes 786464 | tf_op jit(solution)/shard_map/all_to_all | solution.py:441
  177.9 2.5 %collective-permute-start.7 = (bf16[512,768]{1,0:T(8,128)(2,1)S(1)}, bf16[512,768]{1,0:T(8,128)(2,1)S(1)}, u32[]{:S(2)}, u32[]{:S(2)}) collective-permute-start(bf16[512,768]{1,0:T(8,128)(2,1)S(1)} %bitcast.32), channel_id=1, source_target_pairs={{0,1},{1,0},{2,3},{3,2},{4,5},{5,4},{6,7},{7,6},{8,9},{9,8},{10,11... | collective-permute-start | bytes 2359304 | tf_op jit(solution)/shard_map/ppermute | solution.py:498
  180.4 2.0 %collective-permute-done.7.other = bf16[512,768]{1,0:T(8,128)(2,1)S(1)} collective-permute-done((bf16[512,768]{1,0:T(8,128)(2,1)S(1)}, bf16[512,768]{1,0:T(8,128)(2,1)S(1)}, u32[]{:S(2)}, u32[]{:S(2)}) %collective-permute-start.7) | collective-permute-done | bytes 786464 | tf_op jit(solution)/shard_map/ppermute | solution.py:498
  182.5 1.0 all-gather.6.cloned.1.call-done
  183.5 7.2 %unpack.1 = (f32[5,4,192,192]{3,2,1,0:T(8,128)}, f32[768,768]{1,0:T(8,128)}, f32[768,768]{1,0:T(8,128)}, f32[768,768]{1,0:T(8,128)}, f32[768,768]{1,0:T(8,128)}) custom-call(s32[3]{0:T(128)} %pad_add_fusion.info, bf16[512,768]{1,0:T(8,128)(2,1)} %bitcast.33, bf16[512,768]{1,0:T(8,128)(2,1)} %copy-done.2, bf16[16,192,768]{2,1,0:T(8,128)(2,1)} %bitcast.31), custom_call_target="tpu_custom_call" | custom-call | flops 10000000 | bytes 20000000 | tf_op jit(solution)/shard_map/unpack/pallas_call | solution.py:412
  (11 shorter events, 0.0 us)
Async XLA Ops:
  10.0 9.5 %copy-start.1 = (bf16[5,4,192,192]{3,2,1,0:T(8,128)(2,1)S(1)}, bf16[5,4,192,192]{3,2,1,0:T(8,128)(2,1)}, u32[]{:S(2)}) copy-start(bf16[5,4,192,192]{3,2,1,0:T(8,128)(2,1)} %param.12) | copy-start | bytes 4423684
  11.0 20.2 %all-to-all-start = ((bf16[16,176,128]{2,1,0:T(8,128)(2,1)}), bf16[16,176,128]{2,1,0:T(8,128)(2,1)}, u32[]{:S(2)}, u32[]{:S(2)}) async-start(bf16[16,176,128]{2,1,0:T(8,128)(2,1)} %pad_maximum_fusion.1), calls=%async_computation | async-start | bytes 1441792 | tf_op jit(solution)/shard_map/all_to_all | solution.py:441
  18.8 54.3 %all-gather.4.cloned.1.call-start = ((), (), s32[]{:S(2)}) async-start(), calls=%async_computation.5 | async-start | bytes 3342336 | tf_op jit(solution)/shard_map/all_gather | solution.py:469
  45.0 28.1 %collective-permute-start = (bf16[2048,768]{1,0:T(8,128)(2,1)}, bf16[2048,768]{1,0:T(8,128)(2,1)}, u32[]{:S(2)}, u32[]{:S(2)}) collective-permute-start(bf16[2048,768]{1,0:T(8,128)(2,1)} %get-tuple-element.40.hidden.refs_2_), channel_id=1, source_target_pairs={{0,1},{1,0},{2,3},{3,2},{4,5},{5,4},{6,7},{7,6},{8,9},{9,8},{10,11... | collective-permute-start | bytes 9437192 | tf_op jit(solution)/shard_map/ppermute | solution.py:471
  69.3 28.5 %all-to-all-start.1 = ((bf16[8,192,256]{2,1,0:T(8,128)(2,1)}), bf16[8,192,256]{2,1,0:T(8,128)(2,1)S(1)}, u32[]{:S(2)}, u32[]{:S(2)}) async-start(bf16[8,192,256]{2,1,0:T(8,128)(2,1)} %get-tuple-element.43.refs_1_), calls=%async_computation.1 | async-start | bytes 1572864 | tf_op jit(solution)/shard_map/all_to_all | solution.py:441
  97.8 10.1 %copy-start.6 = (bf16[192,768]{1,0:T(8,128)(2,1)S(1)}, bf16[192,768]{1,0:T(8,128)(2,1)}, u32[]{:S(2)}) copy-start(bf16[192,768]{1,0:T(8,128)(2,1)} %get-tuple-element.48) | copy-start | bytes 884740
  97.8 19.3 %copy-start.3 = (bf16[8,192,256]{2,1,0:T(8,128)(2,1)}, bf16[8,192,256]{2,1,0:T(8,128)(2,1)S(1)}, u32[]{:S(2)}) copy-start(bf16[8,192,256]{2,1,0:T(8,128)(2,1)S(1)} %all-to-all-done.1.refs_0_) | copy-start | bytes 2359300
  97.8 2.9 %collective-permute-start.3 = (bf16[8,192,256]{2,1,0:T(8,128)(2,1)}, bf16[8,192,256]{2,1,0:T(8,128)(2,1)}, u32[]{:S(2)}, u32[]{:S(2)}) collective-permute-start(bf16[8,192,256]{2,1,0:T(8,128)(2,1)} %get-tuple-element.49), channel_id=1, source_target_pairs={{0,1},{1,0},{2,3},{3,2},{4,5},{5,4},{6,7},{7,6},{8,9},{9,8},{10,11... | collective-permute-start | bytes 2359304 | tf_op jit(solution)/shard_map/ppermute | solution.py:476
  97.9 10.0 %collective-permute-start.1 = (bf16[192,768]{1,0:T(8,128)(2,1)}, bf16[192,768]{1,0:T(8,128)(2,1)S(1)}, u32[]{:S(2)}, u32[]{:S(2)}) collective-permute-start(bf16[192,768]{1,0:T(8,128)(2,1)} %get-tuple-element.48), channel_id=1, source_target_pairs={{0,16},{16,0},{32,48},{48,32},{64,80},{80,64},{96,112},{112,96},{1... | collective-permute-start | bytes 884744 | tf_op jit(solution)/shard_map/ppermute | solution.py:477
  100.7 16.3 %all-to-all-start.2 = ((bf16[8,192,256]{2,1,0:T(8,128)(2,1)}), bf16[8,192,256]{2,1,0:T(8,128)(2,1)S(1)}, u32[]{:S(2)}, u32[]{:S(2)}) async-start(bf16[8,192,256]{2,1,0:T(8,128)(2,1)} %collective-permute-done.3), calls=%async_computation.2 | async-start | bytes 1572864 | tf_op jit(solution)/shard_map/all_to_all | solution.py:441
  105.4 78.1 %all-gather.6.cloned.1.call-start = ((), (), s32[]{:S(2)}) async-start(), calls=%async_computation.6 | async-start | bytes 5013504 | tf_op jit(solution)/shard_map/all_gather | solution.py:488
  108.0 7.3 %collective-permute-start.2 = (bf16[192,768]{1,0:T(8,128)(2,1)S(1)}, bf16[192,768]{1,0:T(8,128)(2,1)S(1)}, u32[]{:S(2)}, u32[]{:S(2)}) collective-permute-start(bf16[192,768]{1,0:T(8,128)(2,1)S(1)} %add_convert_fusion.3), channel_id=1, source_target_pairs={{0,32},{16,48},{32,0},{48,16},{64,96},{80,112},{96,64},{112,80},{1... | collective-permute-start | bytes 884744 | tf_op jit(solution)/shard_map/ppermute | solution.py:479
  117.0 2.9 %copy-start.4 = (bf16[8,192,256]{2,1,0:T(8,128)(2,1)}, bf16[8,192,256]{2,1,0:T(8,128)(2,1)S(1)}, u32[]{:S(2)}) copy-start(bf16[8,192,256]{2,1,0:T(8,128)(2,1)S(1)} %all-to-all-done.2.refs_1_) | copy-start | bytes 2359300
  117.1 10.5 %collective-permute-start.4 = (bf16[192,768]{1,0:T(8,128)(2,1)S(1)}, bf16[192,768]{1,0:T(8,128)(2,1)S(1)}, u32[]{:S(2)}, u32[]{:S(2)}) collective-permute-start(bf16[192,768]{1,0:T(8,128)(2,1)S(1)} %add_convert_fusion.2), channel_id=1, source_target_pairs={{0,64},{16,80},{32,96},{48,112},{64,0},{80,16},{96,32},{112,48},{1... | collective-permute-start | bytes 884744 | tf_op jit(solution)/shard_map/ppermute | solution.py:482
  127.6 5.0 %copy-start.5 = (bf16[512,768]{1,0:T(8,128)(2,1)S(1)}, bf16[512,768]{1,0:T(8,128)(2,1)}, u32[]{:S(2)}) copy-start(bf16[512,768]{1,0:T(8,128)(2,1)} %get-tuple-element.53) | copy-start | bytes 2359300
  128.5 4.2 %collective-permute-start.5 = (bf16[512,768]{1,0:T(8,128)(2,1)}, bf16[512,768]{1,0:T(8,128)(2,1)S(1)}, u32[]{:S(2)}, u32[]{:S(2)}) collective-permute-start(bf16[512,768]{1,0:T(8,128)(2,1)} %get-tuple-element.57), channel_id=1, source_target_pairs={{0,1},{1,0},{2,3},{3,2},{4,5},{5,4},{6,7},{7,6},{8,9},{9,8},{10,11... | collective-permute-start | bytes 2359304 | tf_op jit(solution)/shard_map/ppermute | solution.py:489
  155.1 8.5 %copy-start.8 = (bf16[128,768]{1,0:T(8,128)(2,1)S(1)}, bf16[128,768]{1,0:T(8,128)(2,1)}, u32[]{:S(2)}) copy-start(bf16[128,768]{1,0:T(8,128)(2,1)} %get-tuple-element.59) | copy-start | bytes 589828
  155.1 10.6 %copy-start.7 = (bf16[128,768]{1,0:T(8,128)(2,1)S(1)}, bf16[128,768]{1,0:T(8,128)(2,1)}, u32[]{:S(2)}) copy-start(bf16[128,768]{1,0:T(8,128)(2,1)} %get-tuple-element.58) | copy-start | bytes 589828
  156.2 21.8 %all-to-all-start.4 = ((bf16[64,8,768]{2,1,0:T(8,128)(2,1)}), bf16[64,8,768]{2,1,0:T(8,128)(2,1)S(1)}, u32[]{:S(2)}, u32[]{:S(2)}) async-start(bf16[64,8,768]{2,1,0:T(8,128)(2,1)} %broadcast_in_dim.7), calls=%async_computation.4 | async-start | bytes 1572864 | tf_op jit(solution)/shard_map/all_to_all | solution.py:441
  163.6 2.1 %collective-permute-start.6 = (bf16[128,768]{1,0:T(8,128)(2,1)S(1)}, bf16[128,768]{1,0:T(8,128)(2,1)S(1)}, u32[]{:S(2)}, u32[]{:S(2)}) collective-permute-start(bf16[128,768]{1,0:T(8,128)(2,1)S(1)} %copy-done.8), channel_id=1, source_target_pairs={{0,1},{1,0},{2,3},{3,2},{4,5},{5,4},{6,7},{7,6},{8,9},{9,8},{10,11... | collective-permute-start | bytes 589832 | tf_op jit(solution)/shard_map/ppermute | solution.py:494
  177.9 5.6 %copy-start = (bf16[64,8,768]{2,1,0:T(8,128)(2,1)}, bf16[64,8,768]{2,1,0:T(8,128)(2,1)S(1)}, u32[]{:S(2)}) copy-start(bf16[64,8,768]{2,1,0:T(8,128)(2,1)S(1)} %all-to-all-done.4) | copy-start | bytes 2359300
  177.9 4.5 %collective-permute-start.7 = (bf16[512,768]{1,0:T(8,128)(2,1)S(1)}, bf16[512,768]{1,0:T(8,128)(2,1)S(1)}, u32[]{:S(2)}, u32[]{:S(2)}) collective-permute-start(bf16[512,768]{1,0:T(8,128)(2,1)S(1)} %bitcast.32), channel_id=1, source_target_pairs={{0,1},{1,0},{2,3},{3,2},{4,5},{5,4},{6,7},{7,6},{8,9},{9,8},{10,11... | collective-permute-start | bytes 2359304 | tf_op jit(solution)/shard_map/ppermute | solution.py:498
  182.5 1.0 copy-start.2
Sparse Core Ops, SparseCore 0:
  31.3 35.6 all-gather.3
  128.6 54.8 all-gather.5
